TPU v7x, 32 devices: a whole 2x2x4 slice. The times are simulated.
32 devices in a mesh: samp: 8 (over z, y), var: 4 (over x, core).
Axes of the slice: x: 2, y: 2, z: 4, core: 2. Of those that a mesh axis runs over, the one named last changes fastest.
Arguments:
- geno: int32 [16384, 8192], P('samp', 'var'), may hold values from 0 to 2, as said below
- allele_pct: int32 [8192], P('var'), may hold values from 5 to 50
- test_geno: int32 [16384, 2048], P('samp', 'var'), may hold values from 0 to 2, as said below
- test_pct: int32 [2048], P('var'), may hold values from 5 to 50
- exposure: float32 [16384], P('samp'), may hold values from -4 to 4
- perm: int32 [8, 16384], P(None, 'samp'), may hold values from 0 to 16383, each once within a row
- var_comp: float32 [3], replicated, may hold values from 0.3 to 1.5
- solution: float32 [8, 16384], P(None, 'samp'), may hold values from -6 to 6
- resid: float32 [8, 16384], P(None, 'samp'), may hold values from -32 to 32
- direction: float32 [8, 16384], P(None, 'samp'), may hold values from -32 to 32
Outputs:
- new_solution: float32 [8, 16384], P(None, 'samp')
- new_resid: float32 [8, 16384], P(None, 'samp')
- new_direction: float32 [8, 16384], P(None, 'samp')
- assoc_scores: float32 [16, 2048], P(None, 'var')
Inputs may be any that keep to these rules, and one draw needn't show every extreme that they name: `geno`: dosages of a variant follow its allele frequency. `test_geno`: dosages of a variant follow its allele frequency.
All inputs are finite; a program needn't handle non-finite values.
Results may differ from a plain program's by a relative error of at most 0.00016.
Values sent between devices are 32-bit elements; how exact they have to be, the bound alone decides.
No kernel may reach another device: no remote copies, remote signals or barrier semaphores. Data moves between devices by JAX's collectives and lax.ppermute only.
A program may use at most 64 MiB of HBM per device.

v0:
```python
import math

import jax
import jax.numpy as jnp
from jax import lax
from jax.sharding import PartitionSpec as P

SLAB = 8192


def standardize(codes, pct):
    freq = pct.astype(jnp.float32) / 100.0
    return (codes.astype(jnp.float32) - 2.0 * freq) * lax.rsqrt(2.0 * freq * (1.0 - freq))


def against_columns(left, right):
    return lax.dot_general(
        left,
        right,
        (((1,), (1,)), ((), ())),
        precision=lax.Precision.HIGHEST,
        preferred_element_type=jnp.float32,
    )


def plain_product(left, right):
    return jnp.dot(left, right, precision=lax.Precision.HIGHEST, preferred_element_type=jnp.float32)


def local(
    geno, allele_pct, test_geno, test_pct, exposure, perm, var_comp, solution, resid, direction
):
    rhs_count = resid.shape[0]
    row_count = resid.shape[1]
    full_exposure = lax.all_gather(exposure, "samp", axis=0, tiled=True)
    shuffled = jnp.take(full_exposure, perm, axis=0)
    loadings = standardize(geno, allele_pct)
    stacked = jnp.concatenate([direction, shuffled * direction], axis=0)
    partial_value = plain_product(stacked, loadings)
    summed = lax.psum(partial_value, "samp")
    applied = against_columns(summed, loadings)
    kernel_rows = lax.psum(applied, "var")
    image = (
        var_comp[0] * direction
        + (var_comp[1] * kernel_rows[:rhs_count] + var_comp[2] * shuffled * kernel_rows[rhs_count:])
        / SLAB
    )
    markers = standardize(test_geno, test_pct)
    norm_now, curvature_sum, cross_sum, square_sum = lax.psum(
        (
            jnp.sum(resid * resid, axis=1),
            jnp.sum(direction * image, axis=1),
            jnp.sum(resid * image, axis=1),
            jnp.sum(image * image, axis=1),
        ),
        "samp",
    )
    alpha = norm_now / curvature_sum
    new_resid = resid - alpha[:, None] * image
    norm_next = norm_now - 2.0 * alpha * cross_sum + alpha * alpha * square_sum
    new_solution = solution + alpha[:, None] * direction
    new_direction = new_resid + (norm_next / norm_now)[:, None] * direction
    root_count = math.sqrt(row_count * lax.axis_size("samp"))
    stacked_resid = jnp.concatenate([new_resid, shuffled * new_resid], axis=0)
    assoc_scores = lax.psum(plain_product(stacked_resid, markers), "samp") / root_count
    return (new_solution, new_resid, new_direction, assoc_scores)


def solution(mesh):
    return jax.shard_map(
        local,
        mesh=mesh,
        in_specs=(
            P("samp", "var"),
            P("var"),
            P("samp", "var"),
            P("var"),
            P("samp"),
            P(None, "samp"),
            P(),
            P(None, "samp"),
            P(None, "samp"),
            P(None, "samp"),
        ),
        out_specs=(P(None, "samp"), P(None, "samp"), P(None, "samp"), P(None, "var")),
        check_vma=False,
    )
```

profile of v0, /device:TPU:0, one launch (start us, length us, event | category | flops | bytes accessed | tf_op | source)
XLA Modules:
  0.0 335.2 jit_solution(12436936703636169146)
XLA Ops:
  7.2 0.0 all-reduce.5.cloned.1.call-start
  7.2 0.9 fusion.21
  8.1 32.5 %all_gather.3 = f32[16384]{0:T(1024)S(1)} all-gather(f32[2048]{0:T(1024)} %param.14), channel_id=1, replica_groups=mesh['samp'=8,'var'=4] {'samp'}, dimensions={0}, use_global_device_ids=true | all-gather | bytes 73728 | tf_op jit(solution)/shard_map/all_gather | solution.py:35
  40.6 90.5 %gather_fusion = f32[16384]{0:T(1024)S(1)} fusion(f32[16384]{0:T(1024)S(1)} %all_gather.3, s32[16384]{0:T(1024)S(1)} %broadcast_clamp_fusion), kind=kCustom, calls=%fused_computation | custom fusion | bytes 196608 | tf_op jit(solution)/shard_map/jit(_take)/gather | solution.py:36
  131.2 0.0 copy-start.7
  131.3 0.0 copy-start.6
  131.3 0.0 copy-start.3
  131.3 0.0 copy-start.4
  131.3 13.6 %fusion.1 = f32[16,2048]{1,0:T(8,128)} fusion(s32[2048,2048]{1,0:T(8,128)} %param.10, f32[2048]{0:T(1024)S(1)} %get-tuple-element.19, f32[2048]{0:T(1024)S(1)} %get-tuple-element.18, f32[8,2048]{1,0:T(8,128)S(1)} %fusion.25, f32[8,2048]{1,0:T(8,128)S(1)} %copy-done), kind=kOutput, calls=%fused_computation.3 | convolution fusion | flops 817922048 | bytes 17055744 | tf_op jit(solution)/shard_map/dot_general | solution.py:27
  144.9 0.0 all-reduce.5.cloned.1.call-update
  144.9 0.2 all-reduce.7.cloned.1.call-start
  145.2 70.4 %all-reduce.5.cloned.1.call-done = f32[16,2048]{1,0:T(8,128)} async-done(((f32[16,2048]{1,0:T(8,128)}), f32[16,2048]{1,0:T(8,128)}) %all-reduce.5.cloned.1.call-update) | async-done | bytes 131088 | tf_op jit(solution)/shard_map/psum | solution.py:40
  215.6 18.1 %fusion = f32[16,2048]{1,0:T(8,128)} fusion(f32[16,2048]{1,0:T(8,128)} %all-reduce.5.cloned.1.call-done, s32[2048,2048]{1,0:T(8,128)} %param.10, f32[2048]{0:T(1024)S(1)} %get-tuple-element.19, f32[2048]{0:T(1024)S(1)} %get-tuple-element.18), kind=kOutput, calls=%fused_computation.2 | convolution fusion | flops 817889280 | bytes 17055744 | tf_op jit(solution)/shard_map/dot_general | solution.py:17
  233.7 0.0 all-reduce.7.cloned.1.call-update
  233.7 0.6 fusion.27
  234.3 30.2 %all-reduce.7.cloned.1.call-done = f32[16,2048]{1,0:T(8,128)} async-done(((f32[16,2048]{1,0:T(8,128)}), f32[16,2048]{1,0:T(8,128)}) %all-reduce.7.cloned.1.call-update) | async-done | bytes 131088 | tf_op jit(solution)/shard_map/psum | solution.py:42
  264.5 3.0 multiply_reduce_fusion.1
  267.5 21.4 %all-reduce.1 = (f32[8]{0:T(128)S(1)}, f32[8]{0:T(128)S(1)}) all-reduce(f32[8]{0:T(128)S(1)} %get-tuple-element.7, f32[8]{0:T(128)S(1)} %get-tuple-element.6), channel_id=1, replica_groups=mesh['samp'=8,'var'=4] {'samp'}, use_global_device_ids=true, to_apply=%region_1.2 | all-reduce | flops 16 | bytes 128 | tf_op jit(solution)/shard_map/psum | solution.py:49
  288.9 0.1 fusion.24
  289.0 0.0 copy-start.2
  289.0 4.7 %fusion.6 = f32[16,512]{1,0:T(8,128)S(1)} fusion(s32[2048,512]{1,0:T(8,128)} %param.12, f32[512]{0:T(512)S(1)} %get-tuple-element.21, f32[512]{0:T(512)S(1)} %get-tuple-element.20, f32[8,2048]{1,0:T(8,128)S(1)} %get-tuple-element.13, f32[8,2048]{1,0:T(8,128)S(1)} %get-tuple-element.14), kind=kOutput, calls=%fused_computation.8 | convolution fusion | flops 204505088 | bytes 4362240 | tf_op jit(solution)/shard_map/dot_general | solution.py:27
  293.7 33.3 %all-reduce = (f32[8]{0:T(128)S(1)}, f32[8]{0:T(128)S(1)}, f32[16,512]{1,0:T(8,128)S(1)}) all-reduce(f32[8]{0:T(128)S(1)} %get-tuple-element.5, f32[8]{0:T(128)S(1)} %get-tuple-element.4, f32[16,512]{1,0:T(8,128)S(1)} %fusion.6), channel_id=1, replica_groups=mesh['samp'=8,'var'=4] {'samp'}, use_global_device_ids=true, to_apply=%region_9.10 | all-reduce | flops 8208 | bytes 65664 | tf_op jit(solution)/shard_map/psum | solution.py:49
  327.0 0.6 broadcast_multiply_fusion
  327.6 0.7 multiply_add_fusion
  (19 shorter events, 0.1 us)
Async XLA Ops:
  7.2 208.4 %all-reduce.5.cloned.1.call-start = ((), (), s32[]{:S(2)}) async-start(), calls=%async_computation | async-start | bytes 262144 | tf_op jit(solution)/shard_map/psum | solution.py:40
  40.6 90.6 %copy-start.5 = (s32[2048]{0:T(1024)S(1)}, s32[2048]{0:T(1024)}, u32[]{:S(2)}) copy-start(s32[2048]{0:T(1024)} %param.11) | copy-start | bytes 24580
  40.6 90.6 %copy-start = (f32[8,2048]{1,0:T(8,128)S(1)}, f32[8,2048]{1,0:T(8,128)}, u32[]{:S(2)}) copy-start(f32[8,2048]{1,0:T(8,128)} %param.19) | copy-start | bytes 196612
  40.6 90.6 %copy-start.1 = (s32[8,2048]{1,0:T(8,128)S(1)}, s32[8,2048]{1,0:T(8,128)}, u32[]{:S(2)}) copy-start(s32[8,2048]{1,0:T(8,128)} %param.15) | copy-start | bytes 196612
  131.2 14.0 %copy-start.7 = (s32[512]{0:T(512)S(1)}, s32[512]{0:T(512)}, u32[]{:S(2)}) copy-start(s32[512]{0:T(512)} %param.13) | copy-start | bytes 6148
  131.3 102.5 %copy-start.6 = (f32[3]{0:T(128)S(1)}, f32[3]{0:T(128)}, u32[]{:S(2)}) copy-start(f32[3]{0:T(128)} %param.16) | copy-start | bytes 40
  131.3 133.3 %copy-start.3 = (f32[8,2048]{1,0:T(8,128)S(1)}, f32[8,2048]{1,0:T(8,128)}, u32[]{:S(2)}) copy-start(f32[8,2048]{1,0:T(8,128)} %param.18) | copy-start | bytes 196612
  131.3 196.4 %copy-start.4 = (f32[8,2048]{1,0:T(8,128)S(1)}, f32[8,2048]{1,0:T(8,128)}, u32[]{:S(2)}) copy-start(f32[8,2048]{1,0:T(8,128)} %param.17) | copy-start | bytes 196612
  144.9 119.6 %all-reduce.7.cloned.1.call-start = ((), (), s32[]{:S(2)}) async-start(), calls=%async_computation.1 | async-start | bytes 262144 | tf_op jit(solution)/shard_map/psum | solution.py:42
  289.0 39.4 %copy-start.2 = (f32[8,2048]{1,0:T(8,128)}, f32[8,2048]{1,0:T(8,128)S(1)}, u32[]{:S(2)}) copy-start(f32[8,2048]{1,0:T(8,128)S(1)} %get-tuple-element.14) | copy-start | bytes 196612
Sparse Core Ops, SparseCore 0:
  145.0 70.4 all-reduce.4
  233.9 30.6 all-reduce.6
where the time goes:
time: 336 us; the launch traced here: 335 us
  waiting for transfers between devices  101 us (30%)
  local copies, waits for them, and re-layouts  91.2 us (27%)
  blocking collectives  87.2 us (26%)
  matrix products  36.4 us (11%)
  between operations  14.2 us (4%)
  other arithmetic  5.35 us (2%)
    gather x2, local copies, waits for them, and re-layouts, local(): shuffled = jnp.take(full_exposure, perm, axis=0)  90.6 us
    psum x1, waiting for transfers between devices, local(): summed = lax.psum(partial_value, 'samp')  70.4 us
    psum x2, blocking collectives, local(): lax.psum((jnp.sum(resid * resid, axis=1), jnp.sum(direction * image, axis...  54.7 us
    all_gather x1, blocking collectives, local(): full_exposure = lax.all_gather(exposure, 'samp', axis=0, tiled=True)  32.5 us
    psum x1, waiting for transfers between devices, local(): kernel_rows = lax.psum(applied, 'var')  30.2 us
    dot_general x2, matrix products, plain_product(): jnp.dot(left, right, precision=lax.Precision.HIGHEST, preferred_element_t...  18.3 us
    dot_general x1, matrix products, against_columns(): lax.dot_general(left, right, (((1,), (1,)), ((), ())), precision=lax.Prec...  18.1 us
  transfers between devices with their start and end apart: 2, of which 2 were waited for; matrix products, arithmetic and copies ran while one was open for 0% of the time, Pallas kernels for 0%

commit v1 on v0

v1 whole, which is shorter than its diff:
```python
import functools
import math

import jax
import jax.numpy as jnp
from jax import lax
from jax.experimental import pallas as pl
from jax.experimental.pallas import tpu as pltpu
from jax.sharding import PartitionSpec as P

LANES = 128
ROWS = 8
VMEM_BYTES = 48 << 20
WHOLE = pl.BlockSpec(memory_space=pltpu.VMEM)
SCALARS = pl.BlockSpec(memory_space=pltpu.SMEM)


def in_vmem(shape, dtype=jnp.float32):
    return pltpu.VMEM(shape, dtype)


def call(body, out_shape, in_specs, **kwargs):
    return pl.pallas_call(
        body,
        out_shape=out_shape,
        in_specs=in_specs,
        compiler_params=pltpu.CompilerParams(vmem_limit_bytes=VMEM_BYTES),
        **kwargs,
    )


def bf16_pieces(x):
    pieces = []
    for _ in range(3):
        piece = x.astype(jnp.bfloat16)
        pieces.append(piece)
        x = x - piece.astype(jnp.float32)
    return jnp.concatenate(pieces, axis=0)


def add_pieces(y):
    rows = y.shape[0] // 3
    return y[:rows] + y[rows : 2 * rows] + y[2 * rows :]


def spread(pct):
    freq = pct.astype(jnp.float32) / 100.0
    return 2.0 * freq, lax.rsqrt(2.0 * freq * (1.0 - freq))


def cast_body(geno, test_geno, direction, codes, test_codes, total):
    step = pl.program_id(0)
    rows = geno.shape[0]
    here = pl.ds(pl.multiple_of(step * rows, rows), rows)
    block = geno[...].astype(jnp.float32).astype(jnp.bfloat16)
    codes[here, :] = block
    test_codes[here, :] = test_geno[...].astype(jnp.float32).astype(jnp.bfloat16)
    part = add_pieces(
        jnp.dot(bf16_pieces(direction[...]), block, preferred_element_type=jnp.float32)
    )

    @pl.when(step == 0)
    def _():
        total[...] = part

    @pl.when(step > 0)
    def _():
        total[...] += part


def cast_codes(geno, test_geno, direction):
    count, slab = geno.shape
    tests = test_geno.shape[1]
    rhs = direction.shape[0]
    rows = math.gcd(count, 512)
    return call(
        cast_body,
        [
            in_vmem((count, slab), jnp.bfloat16),
            in_vmem((count, tests), jnp.bfloat16),
            in_vmem((rhs, slab)),
        ],
        [
            pl.BlockSpec((rows, slab), lambda i: (i, 0)),
            pl.BlockSpec((rows, tests), lambda i: (i, 0)),
            pl.BlockSpec((rhs, rows), lambda i: (0, i)),
        ],
        grid=(count // rows,),
        out_specs=[WHOLE, WHOLE, WHOLE],
    )(geno, test_geno, direction)


def lookup(table, index, out):
    height = table.shape[0]
    rhs, count = index.shape
    left = add_columns(table[...])
    for b in range(rhs):
        places = index[b : b + 1, :]
        row = lax.broadcasted_iota(jnp.int32, (height, count), 0)
        chosen = jnp.where(row == places // LANES, 1.0, 0.0).astype(jnp.bfloat16)
        values = add_pieces(jnp.dot(left, chosen, preferred_element_type=jnp.float32))
        lane = lax.broadcasted_iota(jnp.int32, (LANES, count), 0)
        out[b : b + 1, :] = jnp.sum(
            jnp.where(lane == places % LANES, values, 0.0), axis=0, keepdims=True
        )


def add_columns(table):
    return bf16_pieces(table.T)


def slab_body(table, perm, direction, resid, codes, pct, raw, shuffled, sums):
    rhs, slab = raw.shape
    lookup(table, perm, shuffled)
    mean, scale = spread(pct[...])
    straight = direction[...]
    weighted = shuffled[...] * straight
    product = add_pieces(
        jnp.dot(bf16_pieces(weighted), codes[...], preferred_element_type=jnp.float32)
    )
    sums[:rhs, :slab] = scale * (raw[...] - mean * jnp.sum(straight, axis=1, keepdims=True))
    sums[rhs:, :slab] = scale * (product - mean * jnp.sum(weighted, axis=1, keepdims=True))
    left = resid[...]
    norm = jnp.sum(left * left, axis=1, keepdims=True)
    length = jnp.sum(straight * straight, axis=1, keepdims=True)
    sums[:rhs, slab:] = jnp.broadcast_to(norm, (rhs, LANES))
    sums[rhs:, slab:] = jnp.broadcast_to(length, (rhs, LANES))


def slab_sums(table, perm, direction, resid, codes, pct, raw):
    rhs, slab = raw.shape
    return call(
        slab_body,
        [in_vmem(perm.shape), in_vmem((2 * rhs, slab + LANES))],
        [WHOLE] * 7,
        out_specs=[WHOLE, WHOLE],
    )(table, perm, direction, resid, codes, pct, raw)


def kernel_body(parts, codes, pct, shuffled, var_comp, slab_total, out):
    rhs, count = shuffled.shape
    slab = pct.shape[1]
    sums = parts[:, :slab]
    mean, scale = spread(pct[...])
    weights = scale * sums
    product = add_pieces(
        lax.dot_general(
            bf16_pieces(weights),
            codes[...],
            (((1,), (1,)), ((), ())),
            preferred_element_type=jnp.float32,
        )
    ) - jnp.sum(mean * weights, axis=1, keepdims=True)
    share = 1.0 / slab_total
    out[:, :count] = (
        var_comp[1] * product[:rhs] + var_comp[2] * shuffled[...] * product[rhs:]
    ) * share
    squares = jnp.sum(sums * sums, axis=1, keepdims=True)
    energy = (var_comp[1] * squares[:rhs] + var_comp[2] * squares[rhs:]) * share
    out[:, count:] = jnp.broadcast_to(energy, (rhs, LANES))


def kernel_part(parts, codes, pct, shuffled, var_comp, slab_total):
    rhs, count = shuffled.shape

    def body(parts, codes, pct, shuffled, var_comp, out):
        kernel_body(parts, codes, pct, shuffled, var_comp, slab_total, out)

    return call(
        body,
        in_vmem((rhs, count + LANES)),
        [WHOLE, WHOLE, WHOLE, WHOLE, SCALARS],
        out_specs=WHOLE,
    )(parts, codes, pct, shuffled, var_comp)


def step_body(applied, parts, shuffled, direction, resid, solution, codes, pct, var_comp,
              new_solution, new_resid, scores, root):
    rhs, count = shuffled.shape
    tests = pct.shape[1]
    norms = parts[...]
    straight = direction[...]
    image = var_comp[0] * straight + applied[:, :count]
    curvature = var_comp[0] * norms[rhs:, :1] + applied[:, count : count + 1]
    alpha = norms[:rhs, :1] / curvature
    left = resid[...] - alpha * image
    new_resid[...] = left
    new_solution[...] = solution[...] + alpha * straight
    both = jnp.concatenate([left, shuffled[...] * left], axis=0)
    mean, scale = spread(pct[...])
    product = add_pieces(
        jnp.dot(bf16_pieces(both), codes[...], preferred_element_type=jnp.float32)
    )
    scores[:, :tests] = (scale / root) * (product - mean * jnp.sum(both, axis=1, keepdims=True))
    norm = jnp.sum(left * left, axis=1, keepdims=True)
    scores[:rhs, tests:] = jnp.broadcast_to(norm, (rhs, LANES))
    scores[rhs:, tests:] = jnp.zeros((rhs, LANES), jnp.float32)


def step(applied, norms, shuffled, direction, resid, solution, codes, pct, var_comp, root):
    rhs, count = shuffled.shape
    tests = pct.shape[1]
    return call(
        functools.partial(step_body, root=root),
        [in_vmem((rhs, count)), in_vmem((rhs, count)), in_vmem((2 * rhs, tests + LANES))],
        [WHOLE] * 8 + [SCALARS],
        out_specs=[WHOLE] * 3,
    )(applied, norms, shuffled, direction, resid, solution, codes, pct, var_comp)


def gather_all(x, axis):
    size = lax.axis_size(axis)
    copies = jnp.broadcast_to(x[None], (size, *x.shape))
    return lax.all_to_all(copies, axis, 0, 0)


def swap(x, axis, distance):
    size = lax.axis_size(axis)
    return lax.ppermute(x, axis, [(i, i ^ distance) for i in range(size)])


def sum_all(x, axis, widths):
    size = lax.axis_size(axis)
    if size & (size - 1):
        return lax.psum(x, axis)
    unit = 1
    for width in widths(size):
        if width == 2:
            x = x + swap(x, axis, unit)
        else:
            near, far, last = (swap(x, axis, k * unit) for k in (1, 2, 3))
            x = (x + near) + (far + last)
        unit *= width
    return x


def pairs_then_fours(size):
    bits = size.bit_length() - 1
    return [2] * (bits % 2) + [4] * (bits // 2)


def pairs(size):
    return [2] * (size.bit_length() - 1)


def local(
    geno, allele_pct, test_geno, test_pct, exposure, perm, var_comp, solution, resid, direction
):
    rhs, count = resid.shape
    slab = geno.shape[1]
    tests = test_geno.shape[1]
    table = gather_all(exposure.reshape(-1, LANES), "samp").reshape(-1, LANES)
    codes, test_codes, raw = cast_codes(geno, test_geno, direction)
    pct = allele_pct.reshape(1, slab)
    shuffled, sums = slab_sums(table, perm, direction, resid, codes, pct, raw)
    sums = sum_all(sums, "samp", pairs_then_fours)
    applied = kernel_part(
        sums, codes, pct, shuffled, var_comp, float(slab * lax.axis_size("var"))
    )
    applied = sum_all(applied, "var", pairs)
    norms = sums[:, slab:]
    new_solution, new_resid, scores = step(
        applied, norms, shuffled, direction, resid, solution, test_codes,
        test_pct.reshape(1, tests), var_comp, math.sqrt(count * lax.axis_size("samp")),
    )
    scores = sum_all(scores, "samp", pairs_then_fours)
    ratio = scores[:rhs, tests : tests + 1] / norms[:rhs, :1]
    new_direction = new_resid + ratio * direction
    return (new_solution, new_resid, new_direction, scores[:, :tests])


def solution(mesh):
    return jax.shard_map(
        local,
        mesh=mesh,
        in_specs=(
            P("samp", "var"),
            P("var"),
            P("samp", "var"),
            P("var"),
            P("samp"),
            P(None, "samp"),
            P(),
            P(None, "samp"),
            P(None, "samp"),
            P(None, "samp"),
        ),
        out_specs=(P(None, "samp"), P(None, "samp"), P(None, "samp"), P(None, "var")),
        check_vma=False,
    )
```

time: 336 us -> 75.6 us (0.22)
  blocking collectives: 87.2 us -> 0 us
  local copies, waits for them, and re-layouts: 91.2 us -> 6.48 us
  waiting for transfers between devices: 101 us -> 21 us
  matrix products: 36.4 us -> 0 us
  Pallas kernels: 0 us -> 24.9 us
  starting transfers between devices: 0.26 us -> 21.3 us
  between operations: 14.2 us -> 0.78 us
  other arithmetic: 5.35 us -> 0.91 us
    psum x2 -> x0, waiting for transfers between devices: 101 us -> none  [the longest x1 70.4 us: local(): summed = lax.psum(partial_value, 'samp')]
    gather x2 -> x0, local copies, waits for them, and re-layouts: 90.6 us -> none  [local(): shuffled = jnp.take(full_exposure, perm, axis=0)]
    psum x2 -> x0, blocking collectives: 54.7 us -> none  [local(): lax.psum((jnp.sum(resid * resid, axis=1), jnp.sum(direction * image, axis...]
    dot_general x3 -> x0, matrix products: 36.4 us -> none  [the longest x2 18.3 us: plain_product(): jnp.dot(left, right, precision=lax.Precision.HIGHEST, preferred_element_t...]
    all_gather x1 -> x0, blocking collectives: 32.5 us -> none  [local(): full_exposure = lax.all_gather(exposure, 'samp', axis=0, tiled=True)]
    pallas_call x0 -> x4, Pallas kernels: none -> 24.9 us  [the longest x1 9.09 us: cast_codes(): call(cast_body, [in_vmem((count, slab), jnp.bfloat16), in_vmem((count, te...]
    ppermute x0 -> x10, waiting for transfers between devices: none -> 21 us  [swap(): return lax.ppermute(x, axis, [(i, i ^ distance) for i in range(size)])]
    ppermute x0 -> x10, starting transfers between devices: none -> 14 us  [swap(): return lax.ppermute(x, axis, [(i, i ^ distance) for i in range(size)])]
  transfers between devices with their start and end apart: 2 -> 11, of which waited for: 2 -> 8; matrix products, arithmetic and copies ran while one was open for 0% -> 2% of each run, Pallas kernels for 0% -> 12%
where the time goes in v1:
time: 75.6 us; the launch traced here: 75.4 us
  Pallas kernels  24.9 us (33%)
  starting transfers between devices  21.3 us (28%)
  waiting for transfers between devices  21 us (28%)
  local copies, waits for them, and re-layouts  6.48 us (9%)
  other arithmetic  0.91 us (1%)
  between operations  0.78 us (1%)
    ppermute x10, waiting for transfers between devices, swap(): return lax.ppermute(x, axis, [(i, i ^ distance) for i in range(size)])  21 us
    ppermute x10, starting transfers between devices, swap(): return lax.ppermute(x, axis, [(i, i ^ distance) for i in range(size)])  14 us
    pallas_call x1, Pallas kernels, cast_codes(): call(cast_body, [in_vmem((count, slab), jnp.bfloat16), in_vmem((count, te...  9.09 us
    pallas_call x1, Pallas kernels, slab_sums(): call(slab_body, [in_vmem(perm.shape), in_vmem((2 * rhs, slab + LANES))],...  8.88 us
    all_to_all x1, starting transfers between devices, gather_all(): return lax.all_to_all(copies, axis, 0, 0)  7.28 us
    pallas_call x1, Pallas kernels, kernel_part(): call(body, in_vmem((rhs, count + LANES)), [WHOLE, WHOLE, WHOLE, WHOLE, SC...  5.91 us
    unnamed x18, local copies, waits for them, and re-layouts  4.52 us
  transfers between devices with their start and end apart: 11, of which 8 were waited for; matrix products, arithmetic and copies ran while one was open for 2% of the time, Pallas kernels for 12%

profile of v1, /device:TPU:0, one launch (start us, length us, event | category | flops | bytes accessed | tf_op | source)
XLA Modules:
  0.0 75.4 jit_solution(17017398282256023426)
XLA Ops:
  0.6 1.3 %broadcast_in_dim.8 = f32[8,16,128]{2,1,0:T(8,128)} broadcast(f32[16,128]{1,0:T(8,128)} %bitcast.8), dimensions={1,2} | broadcast | bytes 73728 | tf_op jit(solution)/shard_map/broadcast_in_dim | solution.py:213
  2.0 7.3 %all-to-all-start = ((f32[8,16,128]{2,1,0:T(8,128)}), f32[8,16,128]{2,1,0:T(8,128)S(1)}, u32[]{:S(2)}, u32[]{:S(2)}) async-start(f32[8,16,128]{2,1,0:T(8,128)} %broadcast_in_dim.8), calls=%async_computation | async-start | bytes 131072 | tf_op jit(solution)/shard_map/all_to_all | solution.py:214
  9.3 9.1 %shard_map.129 = (bf16[2048,2048]{1,0:T(8,128)(2,1)S(1)}, bf16[2048,512]{1,0:T(8,128)(2,1)S(1)}, f32[8,2048]{1,0:T(8,128)S(1)}) custom-call(s32[2048,2048]{1,0:T(8,128)} %geno.1, s32[2048,512]{1,0:T(8,128)} %test_geno.1, f32[8,2048]{1,0:T(8,128)} %direction.5), custom_call_target="tpu_custom_call" | custom-call | tf_op jit(solution)/shard_map/pallas_call | solution.py:76
  18.4 3.2 %copy-done = bf16[2048,2048]{1,0:T(8,128)(2,1)} copy-done((bf16[2048,2048]{1,0:T(8,128)(2,1)}, bf16[2048,2048]{1,0:T(8,128)(2,1)S(1)}, u32[]{:S(2)}) %copy-start) | copy-done | bytes 8388632
  21.7 8.9 %shard_map.130 = (f32[8,2048]{1,0:T(8,128)S(1)}, f32[16,2176]{1,0:T(8,128)S(1)}) custom-call(f32[128,128]{1,0:T(8,128)S(1)} %bitcast.4, s32[8,2048]{1,0:T(8,128)S(1)} %copy-done.3, f32[8,2048]{1,0:T(8,128)S(1)} %copy-done.1, f32[8,2048]{1,0:T(8,128)S(1)} %copy-done.2, bf16[2048,2048]{1,0:T(8,128)(2,1)} %copy-done, s32[1,2048]{1,0:T(1,128)S(1)} %bitcast.5, ...), custom_call_target="tpu_custom_call" | custom-call | tf_op jit(solution)/shard_map/pallas_call | solution.py:132
  30.6 2.1 %collective-permute-start = (f32[16,2176]{1,0:T(8,128)S(1)}, f32[16,2176]{1,0:T(8,128)S(1)}, u32[]{:S(2)}, u32[]{:S(2)}) collective-permute-start(f32[16,2176]{1,0:T(8,128)S(1)} %get-tuple-element.14), channel_id=1, source_target_pairs={{0,4},{4,0},{8,12},{12,8},{16,20},{20,16},{24,28},{28,24},{1,5},{5... | collective-permute-start | bytes 417800 | tf_op jit(solution)/shard_map/ppermute | solution.py:219
  32.6 3.1 %collective-permute-done = f32[16,2176]{1,0:T(8,128)S(1)} collective-permute-done((f32[16,2176]{1,0:T(8,128)S(1)}, f32[16,2176]{1,0:T(8,128)S(1)}, u32[]{:S(2)}, u32[]{:S(2)}) %collective-permute-start) | collective-permute-done | bytes 139296 | tf_op jit(solution)/shard_map/ppermute | solution.py:219
  35.8 3.8 %collective-permute-start.3 = (f32[16,2176]{1,0:T(8,128)S(1)}, f32[16,2176]{1,0:T(8,128)S(1)}, u32[]{:S(2)}, u32[]{:S(2)}) collective-permute-start(f32[16,2176]{1,0:T(8,128)S(1)} %add.33), channel_id=1, source_target_pairs={{0,24},{4,28},{8,16},{12,20},{16,8},{20,12},{24,0},{28,4},{1,25},{... | collective-permute-start | bytes 417800 | tf_op jit(solution)/shard_map/ppermute | solution.py:219
  39.6 0.7 collective-permute-start.1
  40.2 4.0 %collective-permute-done.3 = f32[16,2176]{1,0:T(8,128)S(1)} collective-permute-done((f32[16,2176]{1,0:T(8,128)S(1)}, f32[16,2176]{1,0:T(8,128)S(1)}, u32[]{:S(2)}, u32[]{:S(2)}) %collective-permute-start.3) | collective-permute-done | bytes 139296 | tf_op jit(solution)/shard_map/ppermute | solution.py:219
  44.3 5.6 %collective-permute-done.2 = f32[16,2176]{1,0:T(8,128)S(1)} collective-permute-done((f32[16,2176]{1,0:T(8,128)S(1)}, f32[16,2176]{1,0:T(8,128)S(1)}, u32[]{:S(2)}, u32[]{:S(2)}) %collective-permute-start.2) | collective-permute-done | bytes 139296 | tf_op jit(solution)/shard_map/ppermute | solution.py:219
  49.9 5.9 %shard_map.131 = f32[8,2176]{1,0:T(8,128)S(1)} custom-call(f32[16,2176]{1,0:T(8,128)S(1)} %add_add_fusion.parts, bf16[2048,2048]{1,0:T(8,128)(2,1)} %copy-done, s32[1,2048]{1,0:T(1,128)S(1)} %bitcast.6, f32[8,2048]{1,0:T(8,128)S(1)} %get-tuple-element.15.shuffled, f32[3]{0:T(128)S(1)} %copy-done.7), custom_call_target="tpu_custom_call" | custom-call | tf_op jit(solution)/shard_map/pallas_call | solution.py:169
  55.9 1.2 %collective-permute-done.4 = f32[8,2176]{1,0:T(8,128)S(1)} collective-permute-done((f32[8,2176]{1,0:T(8,128)S(1)}, f32[8,2176]{1,0:T(8,128)S(1)}, u32[]{:S(2)}, u32[]{:S(2)}) %collective-permute-start.4) | collective-permute-done | bytes 69664 | tf_op jit(solution)/shard_map/ppermute | solution.py:219
  57.2 1.6 %collective-permute-start.5 = (f32[8,2176]{1,0:T(8,128)S(1)}, f32[8,2176]{1,0:T(8,128)S(1)}, u32[]{:S(2)}, u32[]{:S(2)}) collective-permute-start(f32[8,2176]{1,0:T(8,128)S(1)} %add.37), channel_id=1, source_target_pairs={{0,2},{1,3},{2,0},{3,1},{4,6},{5,7},{6,4},{7,5},{8,10},{9,11},{10,... | collective-permute-start | bytes 208904 | tf_op jit(solution)/shard_map/ppermute | solution.py:219
  58.7 2.8 %collective-permute-done.5 = f32[8,2176]{1,0:T(8,128)S(1)} collective-permute-done((f32[8,2176]{1,0:T(8,128)S(1)}, f32[8,2176]{1,0:T(8,128)S(1)}, u32[]{:S(2)}, u32[]{:S(2)}) %collective-permute-start.5) | collective-permute-done | bytes 69664 | tf_op jit(solution)/shard_map/ppermute | solution.py:219
  61.6 1.0 %shard_map.132 = (f32[8,2048]{1,0:T(8,128)S(1)}, f32[8,2048]{1,0:T(8,128)S(1)}, f32[16,640]{1,0:T(8,128)S(1)}) custom-call(f32[8,2176]{1,0:T(8,128)S(1)} %add.38.applied, f32[16,128]{1,0:T(8,128)S(1)} %slice.17.parts, f32[8,2048]{1,0:T(8,128)S(1)} %get-tuple-element.15.shuffled, f32[8,2048]{1,0:T(8,128)S(1)} %copy-done.1, f32[8,2048]{1,0:T(8,128)S(1)} %copy-done.2, ...), custom_call_target="tpu_custom_call" | custom-call | tf_op jit(solution)/shard_map/pallas_call | solution.py:203
  62.6 1.5 %collective-permute-start.6 = (f32[16,640]{1,0:T(8,128)S(1)}, f32[16,640]{1,0:T(8,128)S(1)}, u32[]{:S(2)}, u32[]{:S(2)}) collective-permute-start(f32[16,640]{1,0:T(8,128)S(1)} %get-tuple-element.19), channel_id=1, source_target_pairs={{0,4},{4,0},{8,12},{12,8},{16,20},{20,16},{24,28},{28,24},{1,5},{5... | collective-permute-start | bytes 122888 | tf_op jit(solution)/shard_map/ppermute | solution.py:219
  64.1 2.5 %collective-permute-done.6 = f32[16,640]{1,0:T(8,128)S(1)} collective-permute-done((f32[16,640]{1,0:T(8,128)S(1)}, f32[16,640]{1,0:T(8,128)S(1)}, u32[]{:S(2)}, u32[]{:S(2)}) %collective-permute-start.6) | collective-permute-done | bytes 40992 | tf_op jit(solution)/shard_map/ppermute | solution.py:219
  66.6 2.4 %collective-permute-start.9 = (f32[16,640]{1,0:T(8,128)S(1)}, f32[16,640]{1,0:T(8,128)S(1)}, u32[]{:S(2)}, u32[]{:S(2)}) collective-permute-start(f32[16,640]{1,0:T(8,128)S(1)} %add.39), channel_id=1, source_target_pairs={{0,24},{4,28},{8,16},{12,20},{16,8},{20,12},{24,0},{28,4},{1,25},{... | collective-permute-start | bytes 122888 | tf_op jit(solution)/shard_map/ppermute | solution.py:219
  69.0 2.0 %collective-permute-start.7 = (f32[16,640]{1,0:T(8,128)S(1)}, f32[16,640]{1,0:T(8,128)S(1)}, u32[]{:S(2)}, u32[]{:S(2)}) collective-permute-start(f32[16,640]{1,0:T(8,128)S(1)} %add.39), channel_id=1, source_target_pairs={{0,8},{4,12},{8,0},{12,4},{16,24},{20,28},{24,16},{28,20},{1,9},{5... | collective-permute-start | bytes 122888 | tf_op jit(solution)/shard_map/ppermute | solution.py:219
  71.0 0.6 copy.14
  71.6 0.6 copy.15
  72.4 1.5 %collective-permute-done.8 = f32[16,640]{1,0:T(8,128)S(1)} collective-permute-done((f32[16,640]{1,0:T(8,128)S(1)}, f32[16,640]{1,0:T(8,128)S(1)}, u32[]{:S(2)}, u32[]{:S(2)}) %collective-permute-start.8) | collective-permute-done | bytes 40992 | tf_op jit(solution)/shard_map/ppermute | solution.py:219
  74.6 0.7 multiply_add_fusion
  (31 shorter events, 1.1 us)
Async XLA Ops:
  2.0 19.7 %all-to-all-start = ((f32[8,16,128]{2,1,0:T(8,128)}), f32[8,16,128]{2,1,0:T(8,128)S(1)}, u32[]{:S(2)}, u32[]{:S(2)}) async-start(f32[8,16,128]{2,1,0:T(8,128)} %broadcast_in_dim.8), calls=%async_computation | async-start | bytes 131072 | tf_op jit(solution)/shard_map/all_to_all | solution.py:214
  9.2 12.4 %copy-start.1 = (f32[8,2048]{1,0:T(8,128)S(1)}, f32[8,2048]{1,0:T(8,128)}, u32[]{:S(2)}) copy-start(f32[8,2048]{1,0:T(8,128)} %direction.5) | copy-start | bytes 196612
  9.2 12.4 %copy-start.2 = (f32[8,2048]{1,0:T(8,128)S(1)}, f32[8,2048]{1,0:T(8,128)}, u32[]{:S(2)}) copy-start(f32[8,2048]{1,0:T(8,128)} %resid.3) | copy-start | bytes 196612
  9.3 12.4 %copy-start.3 = (s32[8,2048]{1,0:T(8,128)S(1)}, s32[8,2048]{1,0:T(8,128)}, u32[]{:S(2)}) copy-start(s32[8,2048]{1,0:T(8,128)} %perm.1) | copy-start | bytes 196612
  9.3 12.4 %copy-start.5 = (s32[2048]{0:T(1024)S(1)}, s32[2048]{0:T(1024)}, u32[]{:S(2)}) copy-start(s32[2048]{0:T(1024)} %param.11) | copy-start | bytes 24580
  18.4 3.2 %copy-start = (bf16[2048,2048]{1,0:T(8,128)(2,1)}, bf16[2048,2048]{1,0:T(8,128)(2,1)S(1)}, u32[]{:S(2)}) copy-start(bf16[2048,2048]{1,0:T(8,128)(2,1)S(1)} %get-tuple-element.12.codes) | copy-start | bytes 25165828
  21.6 28.3 %copy-start.7 = (f32[3]{0:T(128)S(1)}, f32[3]{0:T(128)}, u32[]{:S(2)}) copy-start(f32[3]{0:T(128)} %var_comp.3) | copy-start | bytes 40
  21.7 39.9 %copy-start.4 = (f32[8,2048]{1,0:T(8,128)S(1)}, f32[8,2048]{1,0:T(8,128)}, u32[]{:S(2)}) copy-start(f32[8,2048]{1,0:T(8,128)} %solution.1) | copy-start | bytes 196612
  21.7 39.9 %copy-start.6 = (s32[512]{0:T(512)S(1)}, s32[512]{0:T(512)}, u32[]{:S(2)}) copy-start(s32[512]{0:T(512)} %param.13) | copy-start | bytes 6148
  30.6 5.2 %collective-permute-start = (f32[16,2176]{1,0:T(8,128)S(1)}, f32[16,2176]{1,0:T(8,128)S(1)}, u32[]{:S(2)}, u32[]{:S(2)}) collective-permute-start(f32[16,2176]{1,0:T(8,128)S(1)} %get-tuple-element.14), channel_id=1, source_target_pairs={{0,4},{4,0},{8,12},{12,8},{16,20},{20,16},{24,28},{28,24},{1,5},{5... | collective-permute-start | bytes 417800 | tf_op jit(solution)/shard_map/ppermute | solution.py:219
  35.8 8.5 %collective-permute-start.3 = (f32[16,2176]{1,0:T(8,128)S(1)}, f32[16,2176]{1,0:T(8,128)S(1)}, u32[]{:S(2)}, u32[]{:S(2)}) collective-permute-start(f32[16,2176]{1,0:T(8,128)S(1)} %add.33), channel_id=1, source_target_pairs={{0,24},{4,28},{8,16},{12,20},{16,8},{20,12},{24,0},{28,4},{1,25},{... | collective-permute-start | bytes 417800 | tf_op jit(solution)/shard_map/ppermute | solution.py:219
  39.6 10.3 %collective-permute-start.2 = (f32[16,2176]{1,0:T(8,128)S(1)}, f32[16,2176]{1,0:T(8,128)S(1)}, u32[]{:S(2)}, u32[]{:S(2)}) collective-permute-start(f32[16,2176]{1,0:T(8,128)S(1)} %add.33), channel_id=1, source_target_pairs={{0,16},{4,20},{8,24},{12,28},{16,0},{20,4},{24,8},{28,12},{1,17},{... | collective-permute-start | bytes 417800 | tf_op jit(solution)/shard_map/ppermute | solution.py:219
  39.6 10.3 %collective-permute-start.1 = (f32[16,2176]{1,0:T(8,128)S(1)}, f32[16,2176]{1,0:T(8,128)S(1)}, u32[]{:S(2)}, u32[]{:S(2)}) collective-permute-start(f32[16,2176]{1,0:T(8,128)S(1)} %add.33), channel_id=1, source_target_pairs={{0,8},{4,12},{8,0},{12,4},{16,24},{20,28},{24,16},{28,20},{1,9},{5... | collective-permute-start | bytes 417800 | tf_op jit(solution)/shard_map/ppermute | solution.py:219
  55.8 1.3 %collective-permute-start.4 = (f32[8,2176]{1,0:T(8,128)S(1)}, f32[8,2176]{1,0:T(8,128)S(1)}, u32[]{:S(2)}, u32[]{:S(2)}) collective-permute-start(f32[8,2176]{1,0:T(8,128)S(1)} %shard_map.131), channel_id=1, source_target_pairs={{0,1},{1,0},{2,3},{3,2},{4,5},{5,4},{6,7},{7,6},{8,9},{9,8},{10,11... | collective-permute-start | bytes 208904 | tf_op jit(solution)/shard_map/ppermute | solution.py:219
  57.2 4.4 %collective-permute-start.5 = (f32[8,2176]{1,0:T(8,128)S(1)}, f32[8,2176]{1,0:T(8,128)S(1)}, u32[]{:S(2)}, u32[]{:S(2)}) collective-permute-start(f32[8,2176]{1,0:T(8,128)S(1)} %add.37), channel_id=1, source_target_pairs={{0,2},{1,3},{2,0},{3,1},{4,6},{5,7},{6,4},{7,5},{8,10},{9,11},{10,... | collective-permute-start | bytes 208904 | tf_op jit(solution)/shard_map/ppermute | solution.py:219
  62.6 4.0 %collective-permute-start.6 = (f32[16,640]{1,0:T(8,128)S(1)}, f32[16,640]{1,0:T(8,128)S(1)}, u32[]{:S(2)}, u32[]{:S(2)}) collective-permute-start(f32[16,640]{1,0:T(8,128)S(1)} %get-tuple-element.19), channel_id=1, source_target_pairs={{0,4},{4,0},{8,12},{12,8},{16,20},{20,16},{24,28},{28,24},{1,5},{5... | collective-permute-start | bytes 122888 | tf_op jit(solution)/shard_map/ppermute | solution.py:219
  66.6 5.8 %collective-permute-start.9 = (f32[16,640]{1,0:T(8,128)S(1)}, f32[16,640]{1,0:T(8,128)S(1)}, u32[]{:S(2)}, u32[]{:S(2)}) collective-permute-start(f32[16,640]{1,0:T(8,128)S(1)} %add.39), channel_id=1, source_target_pairs={{0,24},{4,28},{8,16},{12,20},{16,8},{20,12},{24,0},{28,4},{1,25},{... | collective-permute-start | bytes 122888 | tf_op jit(solution)/shard_map/ppermute | solution.py:219
  69.0 4.9 %collective-permute-start.8 = (f32[16,640]{1,0:T(8,128)S(1)}, f32[16,640]{1,0:T(8,128)S(1)}, u32[]{:S(2)}, u32[]{:S(2)}) collective-permute-start(f32[16,640]{1,0:T(8,128)S(1)} %add.39), channel_id=1, source_target_pairs={{0,16},{4,20},{8,24},{12,28},{16,0},{20,4},{24,8},{28,12},{1,17},{... | collective-permute-start | bytes 122888 | tf_op jit(solution)/shard_map/ppermute | solution.py:219
  69.0 4.9 %collective-permute-start.7 = (f32[16,640]{1,0:T(8,128)S(1)}, f32[16,640]{1,0:T(8,128)S(1)}, u32[]{:S(2)}, u32[]{:S(2)}) collective-permute-start(f32[16,640]{1,0:T(8,128)S(1)} %add.39), channel_id=1, source_target_pairs={{0,8},{4,12},{8,0},{12,4},{16,24},{20,28},{24,16},{28,20},{1,9},{5... | collective-permute-start | bytes 122888 | tf_op jit(solution)/shard_map/ppermute | solution.py:219

commit v2 on v1

v2 whole, which is shorter than its diff:
```python
import functools
import math

import jax
import jax.numpy as jnp
from jax import lax
from jax.experimental import pallas as pl
from jax.experimental.pallas import tpu as pltpu
from jax.sharding import PartitionSpec as P

LANES = 128
CAST_ROWS = 64
VMEM_BYTES = 10 << 20
WHOLE = pl.BlockSpec(memory_space=pltpu.VMEM)
SCALARS = pl.BlockSpec(memory_space=pltpu.SMEM)


def in_vmem(shape, dtype=jnp.float32):
    return pltpu.VMEM(shape, dtype)


def call(body, out_shape, in_specs, **kwargs):
    return pl.pallas_call(
        body,
        out_shape=out_shape,
        in_specs=in_specs,
        out_specs=jax.tree.map(lambda _: WHOLE, out_shape),
        compiler_params=pltpu.CompilerParams(vmem_limit_bytes=VMEM_BYTES),
        **kwargs,
    )


def bf16_pieces(x):
    pieces = []
    for _ in range(3):
        piece = x.astype(jnp.bfloat16)
        pieces.append(piece)
        x = x - piece.astype(jnp.float32)
    return jnp.concatenate(pieces, axis=0)


def add_pieces(y):
    rows = y.shape[0] // 3
    return y[:rows] + y[rows : 2 * rows] + y[2 * rows :]


def spread(pct):
    freq = pct.astype(jnp.float32) / 100.0
    return 2.0 * freq, lax.rsqrt(2.0 * freq * (1.0 - freq))


def cast_body(geno, codes):
    rows = math.gcd(geno.shape[0], CAST_ROWS)

    @pl.loop(0, geno.shape[0] // rows)
    def _(step):
        here = pl.ds(pl.multiple_of(step * rows, rows), rows)
        codes[here, :] = geno[here, :].astype(jnp.float32).astype(jnp.bfloat16)


def cast_codes(geno):
    return call(cast_body, in_vmem(geno.shape, jnp.bfloat16), [WHOLE])(geno)


def stack_body(*refs):
    *blocks, out = refs
    out[...] = jnp.concatenate([block[...] for block in blocks], axis=0)


def stack(blocks):
    rows = sum(block.shape[0] for block in blocks)
    return call(
        stack_body,
        in_vmem((rows, LANES)),
        [WHOLE] * len(blocks),
        cost_estimate=pl.CostEstimate(flops=1 << 34, bytes_accessed=1 << 25, transcendentals=0),
    )(*blocks)


def lookup(table, index, out):
    height = table.shape[0]
    rhs, count = index.shape
    exact = jnp.bfloat16 if height <= 256 else jnp.float32
    row = lax.broadcasted_iota(jnp.int32, (height, count), 0).astype(exact)
    lane = lax.broadcasted_iota(jnp.int32, (LANES, count), 0)
    high, middle, low = jnp.split(bf16_pieces(table.T), 3, axis=0)
    left = jnp.concatenate(
        [
            jnp.concatenate([high, middle], axis=1),
            jnp.concatenate([low, jnp.zeros_like(low)], axis=1),
        ],
        axis=0,
    )
    for b in range(rhs):
        places = index[b : b + 1, :]
        wanted = (places // LANES).astype(jnp.float32).astype(exact)
        one, none = jnp.ones((), exact), jnp.zeros((), exact)
        chosen = jnp.where(row == wanted, one, none).astype(jnp.bfloat16)
        values = jnp.dot(
            left,
            jnp.concatenate([chosen, chosen], axis=0),
            preferred_element_type=jnp.float32,
        )
        values = values[:LANES] + values[LANES:]
        out[b : b + 1, :] = jnp.sum(
            jnp.where(lane == places % LANES, values, 0.0), axis=0, keepdims=True
        )


def slab_body(perm, direction, resid, codes, pct, *refs, axis):
    *table, shuffled, sums = refs
    rhs = direction.shape[0]
    slab = codes.shape[1]
    table = jnp.concatenate([block[...] for block in table], axis=0)
    shard = table.size // lax.axis_size(axis)
    lookup(table, perm[...] ^ (lax.axis_index(axis) * shard), shuffled)
    mean, scale = spread(pct[...])
    straight = direction[...]
    both = jnp.concatenate([straight, shuffled[...] * straight], axis=0)
    product = add_pieces(
        jnp.dot(bf16_pieces(both), codes[...], preferred_element_type=jnp.float32)
    )
    sums[:, :slab] = scale * (product - mean * jnp.sum(both, axis=1, keepdims=True))
    left = resid[...]
    norm = jnp.sum(left * left, axis=1, keepdims=True)
    length = jnp.sum(straight * straight, axis=1, keepdims=True)
    sums[:rhs, slab:] = jnp.broadcast_to(norm, (rhs, LANES))
    sums[rhs:, slab:] = jnp.broadcast_to(length, (rhs, LANES))


def slab_sums(table, perm, direction, resid, codes, pct, axis):
    rhs, slab = direction.shape[0], codes.shape[1]
    return call(
        functools.partial(slab_body, axis=axis),
        [in_vmem(perm.shape), in_vmem((2 * rhs, slab + LANES))],
        [WHOLE] * (5 + len(table)),
    )(perm, direction, resid, codes, pct, *table)


def kernel_body(sums, codes, pct, shuffled, var_comp, out, *, slab_total):
    rhs, count = shuffled.shape
    slab = codes.shape[1]
    weights = sums[:, :slab]
    squares = jnp.sum(weights * weights, axis=1, keepdims=True)
    mean, scale = spread(pct[...])
    weights = scale * weights
    product = add_pieces(
        lax.dot_general(
            bf16_pieces(weights),
            codes[...],
            (((1,), (1,)), ((), ())),
            preferred_element_type=jnp.float32,
        )
    ) - jnp.sum(mean * weights, axis=1, keepdims=True)
    share = 1.0 / slab_total
    out[:, :count] = (
        var_comp[1] * product[:rhs] + var_comp[2] * shuffled[...] * product[rhs:]
    ) * share
    energy = (var_comp[1] * squares[:rhs] + var_comp[2] * squares[rhs:]) * share
    out[:, count:] = jnp.broadcast_to(energy, (rhs, LANES))


def kernel_part(sums, codes, pct, shuffled, var_comp, slab_total):
    rhs, count = shuffled.shape
    return call(
        functools.partial(kernel_body, slab_total=slab_total),
        in_vmem((rhs, count + LANES)),
        [WHOLE] * 4 + [SCALARS],
    )(sums, codes, pct, shuffled, var_comp)


def step_body(applied, sums, shuffled, direction, resid, solution, codes, pct, var_comp,
              new_solution, new_resid, scores, *, root):
    rhs, count = shuffled.shape
    tests = codes.shape[1]
    norms = sums[:, -LANES:]
    straight = direction[...]
    image = var_comp[0] * straight + applied[:, :count]
    curvature = var_comp[0] * norms[rhs:, :1] + applied[:, count : count + 1]
    alpha = norms[:rhs, :1] / curvature
    left = resid[...] - alpha * image
    new_resid[...] = left
    new_solution[...] = solution[...] + alpha * straight
    both = jnp.concatenate([left, shuffled[...] * left], axis=0)
    mean, scale = spread(pct[...])
    product = add_pieces(
        jnp.dot(bf16_pieces(both), codes[...], preferred_element_type=jnp.float32)
    )
    scores[:, :tests] = (scale / root) * (product - mean * jnp.sum(both, axis=1, keepdims=True))
    norm = jnp.sum(left * left, axis=1, keepdims=True)
    scores[:rhs, tests:] = jnp.broadcast_to(norm, (rhs, LANES))
    scores[rhs:, tests:] = jnp.zeros((rhs, LANES), jnp.float32)


def step(applied, sums, shuffled, direction, resid, solution, codes, pct, var_comp, root):
    rhs, count = shuffled.shape
    return call(
        functools.partial(step_body, root=root),
        [
            in_vmem((rhs, count)),
            in_vmem((rhs, count)),
            in_vmem((2 * rhs, codes.shape[1] + LANES)),
        ],
        [WHOLE] * 8 + [SCALARS],
    )(applied, sums, shuffled, direction, resid, solution, codes, pct, var_comp)


def finish_body(sums, new_resid, direction, *refs):
    *parts, new_direction, scores = refs
    rhs = direction.shape[0]
    tests = scores.shape[1]
    total = add_parts([part[...] for part in parts])
    scores[...] = total[:, :tests]
    ratio = total[:rhs, tests : tests + 1] / sums[:rhs, -LANES:][:, :1]
    new_direction[...] = new_resid[...] + ratio * direction[...]


def finish(parts, sums, new_resid, direction):
    rows, columns = parts[0].shape
    return call(
        finish_body,
        [
            jax.ShapeDtypeStruct(direction.shape, jnp.float32),
            jax.ShapeDtypeStruct((rows, columns - LANES), jnp.float32),
        ],
        [WHOLE] * (3 + len(parts)),
    )(sums, new_resid, direction, *parts)


def swap(x, axis, distance):
    size = lax.axis_size(axis)
    return lax.ppermute(x, axis, [(i, i ^ distance) for i in range(size)])


def add_parts(parts):
    if len(parts) == 4:
        return (parts[0] + parts[1]) + (parts[2] + parts[3])
    return sum(parts[1:], parts[0])


def sum_parts(x, axis, widths):
    parts = [x]
    unit = 1
    for width in widths(lax.axis_size(axis)):
        held = add_parts(parts)
        parts = [held] + [swap(held, axis, k * unit) for k in range(1, width)]
        unit *= width
    return parts


def sum_all(x, axis, widths):
    return add_parts(sum_parts(x, axis, widths))


def gather_all(x, axis, widths):
    blocks = [x]
    unit = 1
    for width in widths(lax.axis_size(axis)):
        held = blocks[0] if len(blocks) == 1 else stack(blocks)
        blocks = [held] + [swap(held, axis, k * unit) for k in range(1, width)]
        unit *= width
    return blocks


def pairs_then_fours(size):
    bits = size.bit_length() - 1
    return [2] * (bits % 2) + [4] * (bits // 2)


def pairs(size):
    return [2] * (size.bit_length() - 1)


def local(
    geno, allele_pct, test_geno, test_pct, exposure, perm, var_comp, solution, resid, direction
):
    count = resid.shape[1]
    slab = geno.shape[1]
    tests = test_geno.shape[1]
    slab_total = float(slab * lax.axis_size("var"))
    root = math.sqrt(count * lax.axis_size("samp"))
    pct = allele_pct.reshape(1, slab)
    table = gather_all(exposure.reshape(-1, LANES), "samp", pairs_then_fours)
    codes = cast_codes(geno)
    shuffled, sums = slab_sums(table, perm, direction, resid, codes, pct, "samp")
    sums = sum_all(sums, "samp", pairs_then_fours)
    applied = kernel_part(sums, codes, pct, shuffled, var_comp, slab_total)
    applied = sum_all(applied, "var", pairs)
    test_codes = cast_codes(test_geno)
    new_solution, new_resid, scores = step(
        applied, sums, shuffled, direction, resid, solution, test_codes,
        test_pct.reshape(1, tests), var_comp, root,
    )
    parts = sum_parts(scores, "samp", pairs_then_fours)
    new_direction, scores = finish(parts, sums, new_resid, direction)
    return (new_solution, new_resid, new_direction, scores)


def solution(mesh):
    return jax.shard_map(
        local,
        mesh=mesh,
        in_specs=(
            P("samp", "var"),
            P("var"),
            P("samp", "var"),
            P("var"),
            P("samp"),
            P(None, "samp"),
            P(),
            P(None, "samp"),
            P(None, "samp"),
            P(None, "samp"),
        ),
        out_specs=(P(None, "samp"), P(None, "samp"), P(None, "samp"), P(None, "var")),
        check_vma=False,
    )
```

time: 75.6 us -> 59.1 us (0.78)
  Pallas kernels: 24.9 us -> 9.8 us
  local copies, waits for them, and re-layouts: 6.48 us -> 3.01 us
  waiting for transfers between devices: 21 us -> 23.8 us
  other arithmetic: 0.91 us -> 0.08 us
    pallas_call x3 -> x6, Pallas kernels: 23.9 us -> 8.77 us  [the longest x1 3.7 us: slab_sums(): call(functools.partial(slab_body, axis=axis), [in_vmem(perm.shape), in_vm...]
    ppermute x10 -> x14, starting transfers between devices: 14 us -> 21.4 us  [swap(): return lax.ppermute(x, axis, [(i, i ^ distance) for i in range(size)])]
    all_to_all x1 -> x0, starting transfers between devices: 7.28 us -> none  [gather_all(): return lax.all_to_all(copies, axis, 0, 0)]
    ppermute x10 -> x14, waiting for transfers between devices: 21 us -> 23.8 us  [swap(): return lax.ppermute(x, axis, [(i, i ^ distance) for i in range(size)])]
    unnamed x18 -> x22, local copies, waits for them, and re-layouts: 4.52 us -> 3.01 us
    broadcast_in_dim x1 -> x0, local copies, waits for them, and re-layouts: 1.33 us -> none  [gather_all(): copies = jnp.broadcast_to(x[None], (size, *x.shape))]
  transfers between devices with their start and end apart: 11 -> 14, of which waited for: 8 -> 11; matrix products, arithmetic and copies ran while one was open for 2% -> 2% of each run, Pallas kernels for 12% -> 2%
where the time goes in v2:
time: 59.1 us; the launch traced here: 58.9 us
  waiting for transfers between devices  23.8 us (40%)
  starting transfers between devices  21.4 us (36%)
  Pallas kernels  9.8 us (17%)
  local copies, waits for them, and re-layouts  3.01 us (5%)
  between operations  0.78 us (1%)
    ppermute x14, waiting for transfers between devices, swap(): return lax.ppermute(x, axis, [(i, i ^ distance) for i in range(size)])  23.8 us
    ppermute x14, starting transfers between devices, swap(): return lax.ppermute(x, axis, [(i, i ^ distance) for i in range(size)])  21.4 us
    pallas_call x1, Pallas kernels, slab_sums(): call(functools.partial(slab_body, axis=axis), [in_vmem(perm.shape), in_vm...  3.7 us
    pallas_call x1, Pallas kernels, kernel_part(): call(functools.partial(kernel_body, slab_total=slab_total), in_vmem((rhs,...  3.05 us
    unnamed x22, local copies, waits for them, and re-layouts  3.01 us
    pallas_call x2, Pallas kernels, cast_codes(): return call(cast_body, in_vmem(geno.shape, jnp.bfloat16), [WHOLE])(geno)  1.3 us
  transfers between devices with their start and end apart: 14, of which 11 were waited for; matrix products, arithmetic and copies ran while one was open for 2% of the time, Pallas kernels for 2%

profile of v2, /device:TPU:0, one launch (start us, length us, event | category | flops | bytes accessed | tf_op | source)
XLA Modules:
  0.0 58.9 jit_solution(4310821548030115278)
XLA Ops:
  0.6 3.0 %collective-permute-start = (f32[16,128]{1,0:T(8,128)}, f32[16,128]{1,0:T(8,128)S(1)}, u32[]{:S(2)}, u32[]{:S(2)}) collective-permute-start(f32[16,128]{1,0:T(8,128)} %bitcast.6), channel_id=1, source_target_pairs={{0,4},{4,0},{8,12},{12,8},{16,20},{20,16},{24,28},{28,24},{1,5},{5... | collective-permute-start | bytes 24584 | tf_op jit(solution)/shard_map/ppermute | solution.py:232
  3.7 1.8 %collective-permute-done.refs_1_ = f32[16,128]{1,0:T(8,128)S(1)} collective-permute-done((f32[16,128]{1,0:T(8,128)}, f32[16,128]{1,0:T(8,128)S(1)}, u32[]{:S(2)}, u32[]{:S(2)}) %collective-permute-start) | collective-permute-done | bytes 8224 | tf_op jit(solution)/shard_map/ppermute | solution.py:232
  6.2 2.1 %collective-permute-start.1 = (f32[32,128]{1,0:T(8,128)S(1)}, f32[32,128]{1,0:T(8,128)S(1)}, u32[]{:S(2)}, u32[]{:S(2)}) collective-permute-start(f32[32,128]{1,0:T(8,128)S(1)} %shard_map.130.refs_0_), channel_id=1, source_target_pairs={{0,8},{4,12},{8,0},{12,4},{16,24},{20,28},{24,16},{28,20},{1,9},{5... | collective-permute-start | bytes 49160 | tf_op jit(solution)/shard_map/ppermute | solution.py:232
  8.4 2.6 %collective-permute-start.2 = (f32[32,128]{1,0:T(8,128)S(1)}, f32[32,128]{1,0:T(8,128)S(1)}, u32[]{:S(2)}, u32[]{:S(2)}) collective-permute-start(f32[32,128]{1,0:T(8,128)S(1)} %shard_map.130.refs_0_), channel_id=1, source_target_pairs={{0,16},{4,20},{8,24},{12,28},{16,0},{20,4},{24,8},{28,12},{1,17},{... | collective-permute-start | bytes 49160 | tf_op jit(solution)/shard_map/ppermute | solution.py:232
  13.0 3.5 %collective-permute-done.3.refs_3_ = f32[32,128]{1,0:T(8,128)S(1)} collective-permute-done((f32[32,128]{1,0:T(8,128)S(1)}, f32[32,128]{1,0:T(8,128)S(1)}, u32[]{:S(2)}, u32[]{:S(2)}) %collective-permute-start.3) | collective-permute-done | bytes 16416 | tf_op jit(solution)/shard_map/ppermute | solution.py:232
  16.5 3.7 %shard_map.131 = (f32[8,2048]{1,0:T(8,128)S(1)}, f32[16,2176]{1,0:T(8,128)S(1)}) custom-call(s32[8,2048]{1,0:T(8,128)S(1)} %copy-done.4, f32[8,2048]{1,0:T(8,128)S(1)} %copy-done.2, f32[8,2048]{1,0:T(8,128)S(1)} %copy-done.3, bf16[2048,2048]{1,0:T(8,128)(2,1)S(1)} %shard_map.129.codes, s32[1,2048]{1,0:T(1,128)S(1)} %bitcast.3, ...), custom_call_target="tpu_custom_call" | custom-call | tf_op jit(solution)/shard_map/pallas_call | solution.py:133
  20.3 1.6 %collective-permute-start.4 = (f32[16,2176]{1,0:T(8,128)S(1)}, f32[16,2176]{1,0:T(8,128)S(1)}, u32[]{:S(2)}, u32[]{:S(2)}) collective-permute-start(f32[16,2176]{1,0:T(8,128)S(1)} %get-tuple-element.11), channel_id=1, source_target_pairs={{0,4},{4,0},{8,12},{12,8},{16,20},{20,16},{24,28},{28,24},{1,5},{5... | collective-permute-start | bytes 417800 | tf_op jit(solution)/shard_map/ppermute | solution.py:232
  21.8 3.5 %collective-permute-done.4 = f32[16,2176]{1,0:T(8,128)S(1)} collective-permute-done((f32[16,2176]{1,0:T(8,128)S(1)}, f32[16,2176]{1,0:T(8,128)S(1)}, u32[]{:S(2)}, u32[]{:S(2)}) %collective-permute-start.4) | collective-permute-done | bytes 139296 | tf_op jit(solution)/shard_map/ppermute | solution.py:232
  25.5 1.1 %collective-permute-start.6 = (f32[16,2176]{1,0:T(8,128)S(1)}, f32[16,2176]{1,0:T(8,128)S(1)}, u32[]{:S(2)}, u32[]{:S(2)}) collective-permute-start(f32[16,2176]{1,0:T(8,128)S(1)} %add.21), channel_id=1, source_target_pairs={{0,16},{4,20},{8,24},{12,28},{16,0},{20,4},{24,8},{28,12},{1,17},{... | collective-permute-start | bytes 417800 | tf_op jit(solution)/shard_map/ppermute | solution.py:232
  26.6 3.2 %collective-permute-start.7 = (f32[16,2176]{1,0:T(8,128)S(1)}, f32[16,2176]{1,0:T(8,128)S(1)}, u32[]{:S(2)}, u32[]{:S(2)}) collective-permute-start(f32[16,2176]{1,0:T(8,128)S(1)} %add.21), channel_id=1, source_target_pairs={{0,24},{4,28},{8,16},{12,20},{16,8},{20,12},{24,0},{28,4},{1,25},{... | collective-permute-start | bytes 417800 | tf_op jit(solution)/shard_map/ppermute | solution.py:232
  29.9 2.2 %collective-permute-done.5 = f32[16,2176]{1,0:T(8,128)S(1)} collective-permute-done((f32[16,2176]{1,0:T(8,128)S(1)}, f32[16,2176]{1,0:T(8,128)S(1)}, u32[]{:S(2)}, u32[]{:S(2)}) %collective-permute-start.5) | collective-permute-done | bytes 139296 | tf_op jit(solution)/shard_map/ppermute | solution.py:232
  32.1 3.3 %collective-permute-done.6 = f32[16,2176]{1,0:T(8,128)S(1)} collective-permute-done((f32[16,2176]{1,0:T(8,128)S(1)}, f32[16,2176]{1,0:T(8,128)S(1)}, u32[]{:S(2)}, u32[]{:S(2)}) %collective-permute-start.6) | collective-permute-done | bytes 139296 | tf_op jit(solution)/shard_map/ppermute | solution.py:232
  35.4 3.1 %shard_map.132 = f32[8,2176]{1,0:T(8,128)S(1)} custom-call(f32[16,2176]{1,0:T(8,128)S(1)} %add_add_fusion.sums, bf16[2048,2048]{1,0:T(8,128)(2,1)S(1)} %shard_map.129.codes, s32[1,2048]{1,0:T(1,128)S(1)} %bitcast.4, f32[8,2048]{1,0:T(8,128)S(1)} %get-tuple-element.12.shuffled, f32[3]{0:T(128)S(1)} %copy-done.8), custom_call_target="tpu_custom_call" | custom-call | tf_op jit(solution)/shard_map/pallas_call | solution.py:165
  38.5 1.2 %collective-permute-done.8 = f32[8,2176]{1,0:T(8,128)S(1)} collective-permute-done((f32[8,2176]{1,0:T(8,128)S(1)}, f32[8,2176]{1,0:T(8,128)S(1)}, u32[]{:S(2)}, u32[]{:S(2)}) %collective-permute-start.8) | collective-permute-done | bytes 69664 | tf_op jit(solution)/shard_map/ppermute | solution.py:232
  39.8 1.6 %collective-permute-start.9 = (f32[8,2176]{1,0:T(8,128)S(1)}, f32[8,2176]{1,0:T(8,128)S(1)}, u32[]{:S(2)}, u32[]{:S(2)}) collective-permute-start(f32[8,2176]{1,0:T(8,128)S(1)} %add.25), channel_id=1, source_target_pairs={{0,2},{1,3},{2,0},{3,1},{4,6},{5,7},{6,4},{7,5},{8,10},{9,11},{10,... | collective-permute-start | bytes 208904 | tf_op jit(solution)/shard_map/ppermute | solution.py:232
  41.7 2.5 %collective-permute-done.9 = f32[8,2176]{1,0:T(8,128)S(1)} collective-permute-done((f32[8,2176]{1,0:T(8,128)S(1)}, f32[8,2176]{1,0:T(8,128)S(1)}, u32[]{:S(2)}, u32[]{:S(2)}) %collective-permute-start.9) | collective-permute-done | bytes 69664 | tf_op jit(solution)/shard_map/ppermute | solution.py:232
  44.2 1.0 %shard_map.134 = (f32[8,2048]{1,0:T(8,128)S(1)}, f32[8,2048]{1,0:T(8,128)S(1)}, f32[16,640]{1,0:T(8,128)S(1)}) custom-call(f32[8,2176]{1,0:T(8,128)S(1)} %add.26.applied, f32[16,2176]{1,0:T(8,128)S(1)} %add_add_fusion.sums, f32[8,2048]{1,0:T(8,128)S(1)} %get-tuple-element.12.shuffled, f32[8,2048]{1,0:T(8,128)S(1)} %copy-done.2, f32[8,2048]{1,0:T(8,128)S(1)} %copy-done.3, ...), custom_call_target="tpu_custom_call" | custom-call | tf_op jit(solution)/shard_map/pallas_call | solution.py:197
  45.2 1.5 %collective-permute-start.10 = (f32[16,640]{1,0:T(8,128)S(1)}, f32[16,640]{1,0:T(8,128)S(1)}, u32[]{:S(2)}, u32[]{:S(2)}) collective-permute-start(f32[16,640]{1,0:T(8,128)S(1)} %get-tuple-element.15), channel_id=1, source_target_pairs={{0,4},{4,0},{8,12},{12,8},{16,20},{20,16},{24,28},{28,24},{1,5},{5... | collective-permute-start | bytes 122888 | tf_op jit(solution)/shard_map/ppermute | solution.py:232
  46.7 2.5 %collective-permute-done.10 = f32[16,640]{1,0:T(8,128)S(1)} collective-permute-done((f32[16,640]{1,0:T(8,128)S(1)}, f32[16,640]{1,0:T(8,128)S(1)}, u32[]{:S(2)}, u32[]{:S(2)}) %collective-permute-start.10) | collective-permute-done | bytes 40992 | tf_op jit(solution)/shard_map/ppermute | solution.py:232
  49.2 2.0 %collective-permute-start.11 = (f32[16,640]{1,0:T(8,128)S(1)}, f32[16,640]{1,0:T(8,128)S(1)}, u32[]{:S(2)}, u32[]{:S(2)}) collective-permute-start(f32[16,640]{1,0:T(8,128)S(1)} %add.27.refs_0_), channel_id=1, source_target_pairs={{0,8},{4,12},{8,0},{12,4},{16,24},{20,28},{24,16},{28,20},{1,9},{5... | collective-permute-start | bytes 122888 | tf_op jit(solution)/shard_map/ppermute | solution.py:232
  51.3 1.1 %collective-permute-start.12 = (f32[16,640]{1,0:T(8,128)S(1)}, f32[16,640]{1,0:T(8,128)S(1)}, u32[]{:S(2)}, u32[]{:S(2)}) collective-permute-start(f32[16,640]{1,0:T(8,128)S(1)} %add.27.refs_0_), channel_id=1, source_target_pairs={{0,16},{4,20},{8,24},{12,28},{16,0},{20,4},{24,8},{28,12},{1,17},{... | collective-permute-start | bytes 122888 | tf_op jit(solution)/shard_map/ppermute | solution.py:232
  52.3 1.4 %collective-permute-start.13 = (f32[16,640]{1,0:T(8,128)S(1)}, f32[16,640]{1,0:T(8,128)S(1)}, u32[]{:S(2)}, u32[]{:S(2)}) collective-permute-start(f32[16,640]{1,0:T(8,128)S(1)} %add.27.refs_0_), channel_id=1, source_target_pairs={{0,24},{4,28},{8,16},{12,20},{16,8},{20,12},{24,0},{28,4},{1,25},{... | collective-permute-start | bytes 122888 | tf_op jit(solution)/shard_map/ppermute | solution.py:232
  55.0 1.6 %collective-permute-done.12.refs_2_ = f32[16,640]{1,0:T(8,128)S(1)} collective-permute-done((f32[16,640]{1,0:T(8,128)S(1)}, f32[16,640]{1,0:T(8,128)S(1)}, u32[]{:S(2)}, u32[]{:S(2)}) %collective-permute-start.12) | collective-permute-done | bytes 40992 | tf_op jit(solution)/shard_map/ppermute | solution.py:232
  56.6 1.6 %collective-permute-done.13.refs_3_ = f32[16,640]{1,0:T(8,128)S(1)} collective-permute-done((f32[16,640]{1,0:T(8,128)S(1)}, f32[16,640]{1,0:T(8,128)S(1)}, u32[]{:S(2)}, u32[]{:S(2)}) %collective-permute-start.13) | collective-permute-done | bytes 40992 | tf_op jit(solution)/shard_map/ppermute | solution.py:232
  (38 shorter events, 5.3 us)
Async XLA Ops:
  0.6 4.9 %collective-permute-start = (f32[16,128]{1,0:T(8,128)}, f32[16,128]{1,0:T(8,128)S(1)}, u32[]{:S(2)}, u32[]{:S(2)}) collective-permute-start(f32[16,128]{1,0:T(8,128)} %bitcast.6), channel_id=1, source_target_pairs={{0,4},{4,0},{8,12},{12,8},{16,20},{20,16},{24,28},{28,24},{1,5},{5... | collective-permute-start | bytes 24584 | tf_op jit(solution)/shard_map/ppermute | solution.py:232
  5.5 0.7 %copy-start.9 = (f32[2048]{0:T(1024)S(1)}, f32[2048]{0:T(1024)}, u32[]{:S(2)}) copy-start(f32[2048]{0:T(1024)} %param.14) | copy-start | bytes 24580
  6.2 5.8 %copy-start = (s32[2048,2048]{1,0:T(8,128)S(1)}, s32[2048,2048]{1,0:T(8,128)}, u32[]{:S(2)}) copy-start(s32[2048,2048]{1,0:T(8,128)} %geno.2) | copy-start | bytes 50331652
  6.2 10.3 %copy-start.2 = (f32[8,2048]{1,0:T(8,128)S(1)}, f32[8,2048]{1,0:T(8,128)}, u32[]{:S(2)}) copy-start(f32[8,2048]{1,0:T(8,128)} %direction.5) | copy-start | bytes 196612
  6.2 10.3 %copy-start.3 = (f32[8,2048]{1,0:T(8,128)S(1)}, f32[8,2048]{1,0:T(8,128)}, u32[]{:S(2)}) copy-start(f32[8,2048]{1,0:T(8,128)} %resid.3) | copy-start | bytes 196612
  6.2 10.3 %copy-start.4 = (s32[8,2048]{1,0:T(8,128)S(1)}, s32[8,2048]{1,0:T(8,128)}, u32[]{:S(2)}) copy-start(s32[8,2048]{1,0:T(8,128)} %perm.1) | copy-start | bytes 196612
  6.2 10.3 %copy-start.6 = (s32[2048]{0:T(1024)S(1)}, s32[2048]{0:T(1024)}, u32[]{:S(2)}) copy-start(s32[2048]{0:T(1024)} %param.11) | copy-start | bytes 24580
  6.2 6.7 %collective-permute-start.1 = (f32[32,128]{1,0:T(8,128)S(1)}, f32[32,128]{1,0:T(8,128)S(1)}, u32[]{:S(2)}, u32[]{:S(2)}) collective-permute-start(f32[32,128]{1,0:T(8,128)S(1)} %shard_map.130.refs_0_), channel_id=1, source_target_pairs={{0,8},{4,12},{8,0},{12,4},{16,24},{20,28},{24,16},{28,20},{1,9},{5... | collective-permute-start | bytes 49160 | tf_op jit(solution)/shard_map/ppermute | solution.py:232
  8.4 4.6 %collective-permute-start.2 = (f32[32,128]{1,0:T(8,128)S(1)}, f32[32,128]{1,0:T(8,128)S(1)}, u32[]{:S(2)}, u32[]{:S(2)}) collective-permute-start(f32[32,128]{1,0:T(8,128)S(1)} %shard_map.130.refs_0_), channel_id=1, source_target_pairs={{0,16},{4,20},{8,24},{12,28},{16,0},{20,4},{24,8},{28,12},{1,17},{... | collective-permute-start | bytes 49160 | tf_op jit(solution)/shard_map/ppermute | solution.py:232
  11.0 5.5 %collective-permute-start.3 = (f32[32,128]{1,0:T(8,128)S(1)}, f32[32,128]{1,0:T(8,128)S(1)}, u32[]{:S(2)}, u32[]{:S(2)}) collective-permute-start(f32[32,128]{1,0:T(8,128)S(1)} %shard_map.130.refs_0_), channel_id=1, source_target_pairs={{0,24},{4,28},{8,16},{12,20},{16,8},{20,12},{24,0},{28,4},{1,25},{... | collective-permute-start | bytes 49160 | tf_op jit(solution)/shard_map/ppermute | solution.py:232
  12.9 22.5 %copy-start.8 = (f32[3]{0:T(128)S(1)}, f32[3]{0:T(128)}, u32[]{:S(2)}) copy-start(f32[3]{0:T(128)} %var_comp.3) | copy-start | bytes 40
  16.5 24.8 %copy-start.1 = (s32[2048,512]{1,0:T(8,128)S(1)}, s32[2048,512]{1,0:T(8,128)}, u32[]{:S(2)}) copy-start(s32[2048,512]{1,0:T(8,128)} %geno.3) | copy-start | bytes 12582916
  20.2 23.9 %copy-start.5 = (f32[8,2048]{1,0:T(8,128)S(1)}, f32[8,2048]{1,0:T(8,128)}, u32[]{:S(2)}) copy-start(f32[8,2048]{1,0:T(8,128)} %solution.1) | copy-start | bytes 196612
  20.2 23.9 %copy-start.7 = (s32[512]{0:T(512)S(1)}, s32[512]{0:T(512)}, u32[]{:S(2)}) copy-start(s32[512]{0:T(512)} %param.13) | copy-start | bytes 6148
  20.3 5.1 %collective-permute-start.4 = (f32[16,2176]{1,0:T(8,128)S(1)}, f32[16,2176]{1,0:T(8,128)S(1)}, u32[]{:S(2)}, u32[]{:S(2)}) collective-permute-start(f32[16,2176]{1,0:T(8,128)S(1)} %get-tuple-element.11), channel_id=1, source_target_pairs={{0,4},{4,0},{8,12},{12,8},{16,20},{20,16},{24,28},{28,24},{1,5},{5... | collective-permute-start | bytes 417800 | tf_op jit(solution)/shard_map/ppermute | solution.py:232
  25.4 6.7 %collective-permute-start.5 = (f32[16,2176]{1,0:T(8,128)S(1)}, f32[16,2176]{1,0:T(8,128)S(1)}, u32[]{:S(2)}, u32[]{:S(2)}) collective-permute-start(f32[16,2176]{1,0:T(8,128)S(1)} %add.21), channel_id=1, source_target_pairs={{0,8},{4,12},{8,0},{12,4},{16,24},{20,28},{24,16},{28,20},{1,9},{5... | collective-permute-start | bytes 417800 | tf_op jit(solution)/shard_map/ppermute | solution.py:232
  25.5 9.9 %collective-permute-start.6 = (f32[16,2176]{1,0:T(8,128)S(1)}, f32[16,2176]{1,0:T(8,128)S(1)}, u32[]{:S(2)}, u32[]{:S(2)}) collective-permute-start(f32[16,2176]{1,0:T(8,128)S(1)} %add.21), channel_id=1, source_target_pairs={{0,16},{4,20},{8,24},{12,28},{16,0},{20,4},{24,8},{28,12},{1,17},{... | collective-permute-start | bytes 417800 | tf_op jit(solution)/shard_map/ppermute | solution.py:232
  26.6 8.7 %collective-permute-start.7 = (f32[16,2176]{1,0:T(8,128)S(1)}, f32[16,2176]{1,0:T(8,128)S(1)}, u32[]{:S(2)}, u32[]{:S(2)}) collective-permute-start(f32[16,2176]{1,0:T(8,128)S(1)} %add.21), channel_id=1, source_target_pairs={{0,24},{4,28},{8,16},{12,20},{16,8},{20,12},{24,0},{28,4},{1,25},{... | collective-permute-start | bytes 417800 | tf_op jit(solution)/shard_map/ppermute | solution.py:232
  38.5 1.3 %collective-permute-start.8 = (f32[8,2176]{1,0:T(8,128)S(1)}, f32[8,2176]{1,0:T(8,128)S(1)}, u32[]{:S(2)}, u32[]{:S(2)}) collective-permute-start(f32[8,2176]{1,0:T(8,128)S(1)} %shard_map.132), channel_id=1, source_target_pairs={{0,1},{1,0},{2,3},{3,2},{4,5},{5,4},{6,7},{7,6},{8,9},{9,8},{10,11... | collective-permute-start | bytes 208904 | tf_op jit(solution)/shard_map/ppermute | solution.py:232
  39.8 4.4 %collective-permute-start.9 = (f32[8,2176]{1,0:T(8,128)S(1)}, f32[8,2176]{1,0:T(8,128)S(1)}, u32[]{:S(2)}, u32[]{:S(2)}) collective-permute-start(f32[8,2176]{1,0:T(8,128)S(1)} %add.25), channel_id=1, source_target_pairs={{0,2},{1,3},{2,0},{3,1},{4,6},{5,7},{6,4},{7,5},{8,10},{9,11},{10,... | collective-permute-start | bytes 208904 | tf_op jit(solution)/shard_map/ppermute | solution.py:232
  45.2 4.0 %collective-permute-start.10 = (f32[16,640]{1,0:T(8,128)S(1)}, f32[16,640]{1,0:T(8,128)S(1)}, u32[]{:S(2)}, u32[]{:S(2)}) collective-permute-start(f32[16,640]{1,0:T(8,128)S(1)} %get-tuple-element.15), channel_id=1, source_target_pairs={{0,4},{4,0},{8,12},{12,8},{16,20},{20,16},{24,28},{28,24},{1,5},{5... | collective-permute-start | bytes 122888 | tf_op jit(solution)/shard_map/ppermute | solution.py:232
  49.2 5.8 %collective-permute-start.11 = (f32[16,640]{1,0:T(8,128)S(1)}, f32[16,640]{1,0:T(8,128)S(1)}, u32[]{:S(2)}, u32[]{:S(2)}) collective-permute-start(f32[16,640]{1,0:T(8,128)S(1)} %add.27.refs_0_), channel_id=1, source_target_pairs={{0,8},{4,12},{8,0},{12,4},{16,24},{20,28},{24,16},{28,20},{1,9},{5... | collective-permute-start | bytes 122888 | tf_op jit(solution)/shard_map/ppermute | solution.py:232
  51.3 5.3 %collective-permute-start.12 = (f32[16,640]{1,0:T(8,128)S(1)}, f32[16,640]{1,0:T(8,128)S(1)}, u32[]{:S(2)}, u32[]{:S(2)}) collective-permute-start(f32[16,640]{1,0:T(8,128)S(1)} %add.27.refs_0_), channel_id=1, source_target_pairs={{0,16},{4,20},{8,24},{12,28},{16,0},{20,4},{24,8},{28,12},{1,17},{... | collective-permute-start | bytes 122888 | tf_op jit(solution)/shard_map/ppermute | solution.py:232
  52.3 5.8 %collective-permute-start.13 = (f32[16,640]{1,0:T(8,128)S(1)}, f32[16,640]{1,0:T(8,128)S(1)}, u32[]{:S(2)}, u32[]{:S(2)}) collective-permute-start(f32[16,640]{1,0:T(8,128)S(1)} %add.27.refs_0_), channel_id=1, source_target_pairs={{0,24},{4,28},{8,16},{12,20},{16,8},{20,12},{24,0},{28,4},{1,25},{... | collective-permute-start | bytes 122888 | tf_op jit(solution)/shard_map/ppermute | solution.py:232

commit v3 on v2

--- a/solution.py
+++ b/solution.py
@@ -10,6 +10,7 @@
 
 LANES = 128
 CAST_ROWS = 64
+FLIP_ROWS = 512
 VMEM_BYTES = 10 << 20
 WHOLE = pl.BlockSpec(memory_space=pltpu.VMEM)
 SCALARS = pl.BlockSpec(memory_space=pltpu.SMEM)
@@ -30,6 +31,10 @@
     )
 
 
+def cost(products):
+    return pl.CostEstimate(flops=8 * products, bytes_accessed=0, transcendentals=0)
+
+
 def bf16_pieces(x):
     pieces = []
     for _ in range(3):
@@ -60,6 +65,25 @@
 
 def cast_codes(geno):
     return call(cast_body, in_vmem(geno.shape, jnp.bfloat16), [WHOLE])(geno)
+
+
+def flip_body(codes, flipped, *, start):
+    rows = math.gcd(codes.shape[0], FLIP_ROWS)
+    columns = slice(start, start + flipped.shape[0])
+
+    @pl.loop(0, codes.shape[0] // rows)
+    def _(step):
+        here = pl.ds(pl.multiple_of(step * rows, rows), rows)
+        flipped[:, here] = codes[here, columns].T
+
+
+def flip_codes(codes, start, width):
+    return call(
+        functools.partial(flip_body, start=start),
+        in_vmem((width, codes.shape[0]), codes.dtype),
+        [WHOLE],
+        cost_estimate=cost(64 * codes.shape[0] * width),
+    )(codes)
 
 
 def stack_body(*refs):
@@ -137,20 +161,15 @@
     )(perm, direction, resid, codes, pct, *table)
 
 
-def kernel_body(sums, codes, pct, shuffled, var_comp, out, *, slab_total):
+def kernel_body(sums, flipped, pct, shuffled, var_comp, out, *, slab_total):
     rhs, count = shuffled.shape
-    slab = codes.shape[1]
+    slab = flipped.shape[0]
     weights = sums[:, :slab]
     squares = jnp.sum(weights * weights, axis=1, keepdims=True)
     mean, scale = spread(pct[...])
     weights = scale * weights
     product = add_pieces(
-        lax.dot_general(
-            bf16_pieces(weights),
-            codes[...],
-            (((1,), (1,)), ((), ())),
-            preferred_element_type=jnp.float32,
-        )
+        jnp.dot(bf16_pieces(weights), flipped[...], preferred_element_type=jnp.float32)
     ) - jnp.sum(mean * weights, axis=1, keepdims=True)
     share = 1.0 / slab_total
     out[:, :count] = (
@@ -160,13 +179,13 @@
     out[:, count:] = jnp.broadcast_to(energy, (rhs, LANES))
 
 
-def kernel_part(sums, codes, pct, shuffled, var_comp, slab_total):
+def kernel_part(sums, flipped, pct, shuffled, var_comp, slab_total):
     rhs, count = shuffled.shape
     return call(
         functools.partial(kernel_body, slab_total=slab_total),
         in_vmem((rhs, count + LANES)),
         [WHOLE] * 4 + [SCALARS],
-    )(sums, codes, pct, shuffled, var_comp)
+    )(sums, flipped, pct, shuffled, var_comp)
 
 
 def step_body(applied, sums, shuffled, direction, resid, solution, codes, pct, var_comp,
@@ -238,18 +257,17 @@
     return sum(parts[1:], parts[0])
 
 
-def sum_parts(x, axis, widths):
+def sum_parts(x, axis, widths, unit=1):
     parts = [x]
-    unit = 1
-    for width in widths(lax.axis_size(axis)):
+    for width in widths(lax.axis_size(axis) // unit):
         held = add_parts(parts)
         parts = [held] + [swap(held, axis, k * unit) for k in range(1, width)]
         unit *= width
     return parts
 
 
-def sum_all(x, axis, widths):
-    return add_parts(sum_parts(x, axis, widths))
+def sum_all(x, axis, widths, unit=1):
+    return add_parts(sum_parts(x, axis, widths, unit))
 
 
 def gather_all(x, axis, widths):
@@ -283,8 +301,11 @@
     table = gather_all(exposure.reshape(-1, LANES), "samp", pairs_then_fours)
     codes = cast_codes(geno)
     shuffled, sums = slab_sums(table, perm, direction, resid, codes, pct, "samp")
-    sums = sum_all(sums, "samp", pairs_then_fours)
-    applied = kernel_part(sums, codes, pct, shuffled, var_comp, slab_total)
+    sums = sums + swap(sums, "samp", 1)
+    codes, sums = lax.optimization_barrier((codes, sums))
+    flipped = flip_codes(codes, 0, slab)
+    sums = sum_all(sums, "samp", pairs_then_fours, 2)
+    applied = kernel_part(sums, flipped, pct, shuffled, var_comp, slab_total)
     applied = sum_all(applied, "var", pairs)
     test_codes = cast_codes(test_geno)
     new_solution, new_resid, scores = step(

time: 59.1 us -> 57.9 us (0.980)
  waiting for transfers between devices: 23.8 us -> 21.2 us
  Pallas kernels: 9.8 us -> 11.3 us
    ppermute x14, waiting for transfers between devices: 23.8 us -> 21.2 us  [swap(): return lax.ppermute(x, axis, [(i, i ^ distance) for i in range(size)])]
    pallas_call x0 -> x1, Pallas kernels: none -> 2.59 us  [flip_codes(): call(functools.partial(flip_body, start=start), in_vmem((width, codes.sha...]
    pallas_call x1, Pallas kernels: 3.05 us -> 1.95 us  [kernel_part(): call(functools.partial(kernel_body, slab_total=slab_total), in_vmem((rhs,...]
  transfers between devices with their start and end apart: 14 -> 14, of which waited for: 11 -> 10; matrix products, arithmetic and copies ran while one was open for 2% -> 2% of each run, Pallas kernels for 2% -> 7%
where the time goes in v3:
time: 57.9 us; the launch traced here: 57.7 us
  starting transfers between devices  21.3 us (37%)
  waiting for transfers between devices  21.2 us (37%)
  Pallas kernels  11.3 us (20%)
  local copies, waits for them, and re-layouts  3 us (5%)
  between operations  0.8 us (1%)
    ppermute x14, starting transfers between devices, swap(): return lax.ppermute(x, axis, [(i, i ^ distance) for i in range(size)])  21.3 us
    ppermute x14, waiting for transfers between devices, swap(): return lax.ppermute(x, axis, [(i, i ^ distance) for i in range(size)])  21.2 us
    pallas_call x1, Pallas kernels, slab_sums(): call(functools.partial(slab_body, axis=axis), [in_vmem(perm.shape), in_vm...  3.7 us
    unnamed x22, local copies, waits for them, and re-layouts  3 us
    pallas_call x1, Pallas kernels, flip_codes(): call(functools.partial(flip_body, start=start), in_vmem((width, codes.sha...  2.59 us
    pallas_call x1, Pallas kernels, kernel_part(): call(functools.partial(kernel_body, slab_total=slab_total), in_vmem((rhs,...  1.95 us
    pallas_call x2, Pallas kernels, cast_codes(): return call(cast_body, in_vmem(geno.shape, jnp.bfloat16), [WHOLE])(geno)  1.3 us
  transfers between devices with their start and end apart: 14, of which 10 were waited for; matrix products, arithmetic and copies ran while one was open for 2% of the time, Pallas kernels for 7%

profile of v3, /device:TPU:0, one launch (start us, length us, event | category | flops | bytes accessed | tf_op | source)
XLA Modules:
  0.0 57.7 jit_solution(1093362674113785193)
XLA Ops:
  0.6 3.0 %collective-permute-start = (f32[16,128]{1,0:T(8,128)}, f32[16,128]{1,0:T(8,128)S(1)}, u32[]{:S(2)}, u32[]{:S(2)}) collective-permute-start(f32[16,128]{1,0:T(8,128)} %bitcast.6), channel_id=1, source_target_pairs={{0,4},{4,0},{8,12},{12,8},{16,20},{20,16},{24,28},{28,24},{1,5},{5... | collective-permute-start | bytes 24584 | tf_op jit(solution)/shard_map/ppermute | solution.py:251
  3.7 1.8 %collective-permute-done.refs_1_ = f32[16,128]{1,0:T(8,128)S(1)} collective-permute-done((f32[16,128]{1,0:T(8,128)}, f32[16,128]{1,0:T(8,128)S(1)}, u32[]{:S(2)}, u32[]{:S(2)}) %collective-permute-start) | collective-permute-done | bytes 8224 | tf_op jit(solution)/shard_map/ppermute | solution.py:251
  6.2 2.1 %collective-permute-start.1 = (f32[32,128]{1,0:T(8,128)S(1)}, f32[32,128]{1,0:T(8,128)S(1)}, u32[]{:S(2)}, u32[]{:S(2)}) collective-permute-start(f32[32,128]{1,0:T(8,128)S(1)} %shard_map.130.refs_0_), channel_id=1, source_target_pairs={{0,8},{4,12},{8,0},{12,4},{16,24},{20,28},{24,16},{28,20},{1,9},{5... | collective-permute-start | bytes 49160 | tf_op jit(solution)/shard_map/ppermute | solution.py:251
  8.4 2.6 %collective-permute-start.2 = (f32[32,128]{1,0:T(8,128)S(1)}, f32[32,128]{1,0:T(8,128)S(1)}, u32[]{:S(2)}, u32[]{:S(2)}) collective-permute-start(f32[32,128]{1,0:T(8,128)S(1)} %shard_map.130.refs_0_), channel_id=1, source_target_pairs={{0,16},{4,20},{8,24},{12,28},{16,0},{20,4},{24,8},{28,12},{1,17},{... | collective-permute-start | bytes 49160 | tf_op jit(solution)/shard_map/ppermute | solution.py:251
  13.0 3.5 %collective-permute-done.3.refs_3_ = f32[32,128]{1,0:T(8,128)S(1)} collective-permute-done((f32[32,128]{1,0:T(8,128)S(1)}, f32[32,128]{1,0:T(8,128)S(1)}, u32[]{:S(2)}, u32[]{:S(2)}) %collective-permute-start.3) | collective-permute-done | bytes 16416 | tf_op jit(solution)/shard_map/ppermute | solution.py:251
  16.5 3.7 %shard_map.131 = (f32[8,2048]{1,0:T(8,128)S(1)}, f32[16,2176]{1,0:T(8,128)S(1)}) custom-call(s32[8,2048]{1,0:T(8,128)S(1)} %copy-done.4, f32[8,2048]{1,0:T(8,128)S(1)} %copy-done.2, f32[8,2048]{1,0:T(8,128)S(1)} %copy-done.3, bf16[2048,2048]{1,0:T(8,128)(2,1)S(1)} %shard_map.129.codes, s32[1,2048]{1,0:T(1,128)S(1)} %bitcast.3, ...), custom_call_target="tpu_custom_call" | custom-call | tf_op jit(solution)/shard_map/pallas_call | solution.py:157
  20.2 1.5 %collective-permute-start.4 = (f32[16,2176]{1,0:T(8,128)S(1)}, f32[16,2176]{1,0:T(8,128)S(1)}, u32[]{:S(2)}, u32[]{:S(2)}) collective-permute-start(f32[16,2176]{1,0:T(8,128)S(1)} %get-tuple-element.13), channel_id=1, source_target_pairs={{0,4},{4,0},{8,12},{12,8},{16,20},{20,16},{24,28},{28,24},{1,5},{5... | collective-permute-start | bytes 417800 | tf_op jit(solution)/shard_map/ppermute | solution.py:251
  21.8 3.5 %collective-permute-done.4 = f32[16,2176]{1,0:T(8,128)S(1)} collective-permute-done((f32[16,2176]{1,0:T(8,128)S(1)}, f32[16,2176]{1,0:T(8,128)S(1)}, u32[]{:S(2)}, u32[]{:S(2)}) %collective-permute-start.4) | collective-permute-done | bytes 139296 | tf_op jit(solution)/shard_map/ppermute | solution.py:251
  25.4 1.1 %collective-permute-start.6 = (f32[16,2176]{1,0:T(8,128)S(1)}, f32[16,2176]{1,0:T(8,128)S(1)}, u32[]{:S(2)}, u32[]{:S(2)}) collective-permute-start(f32[16,2176]{1,0:T(8,128)S(1)} %add.21), channel_id=1, source_target_pairs={{0,16},{4,20},{8,24},{12,28},{16,0},{20,4},{24,8},{28,12},{1,17},{... | collective-permute-start | bytes 417800 | tf_op jit(solution)/shard_map/ppermute | solution.py:251
  26.5 3.2 %collective-permute-start.7 = (f32[16,2176]{1,0:T(8,128)S(1)}, f32[16,2176]{1,0:T(8,128)S(1)}, u32[]{:S(2)}, u32[]{:S(2)}) collective-permute-start(f32[16,2176]{1,0:T(8,128)S(1)} %add.21), channel_id=1, source_target_pairs={{0,24},{4,28},{8,16},{12,20},{16,8},{20,12},{24,0},{28,4},{1,25},{... | collective-permute-start | bytes 417800 | tf_op jit(solution)/shard_map/ppermute | solution.py:251
  29.8 2.6 %shard_map.132.flipped = bf16[2048,2048]{1,0:T(8,128)(2,1)S(1)} custom-call(bf16[2048,2048]{1,0:T(8,128)(2,1)S(1)} %shard_map.129.codes), custom_call_target="tpu_custom_call" | custom-call | flops 2147483648 | tf_op jit(solution)/shard_map/pallas_call | solution.py:81
  32.4 2.9 %collective-permute-done.6 = f32[16,2176]{1,0:T(8,128)S(1)} collective-permute-done((f32[16,2176]{1,0:T(8,128)S(1)}, f32[16,2176]{1,0:T(8,128)S(1)}, u32[]{:S(2)}, u32[]{:S(2)}) %collective-permute-start.6) | collective-permute-done | bytes 139296 | tf_op jit(solution)/shard_map/ppermute | solution.py:251
  35.3 2.0 %shard_map.133 = f32[8,2176]{1,0:T(8,128)S(1)} custom-call(f32[16,2176]{1,0:T(8,128)S(1)} %add_add_fusion.sums, bf16[2048,2048]{1,0:T(8,128)(2,1)S(1)} %shard_map.132.flipped, s32[1,2048]{1,0:T(1,128)S(1)} %bitcast.4, f32[8,2048]{1,0:T(8,128)S(1)} %get-tuple-element.16.shuffled, f32[3]{0:T(128)S(1)} %copy-done.8), custom_call_target="tpu_custom_call" | custom-call | tf_op jit(solution)/shard_map/pallas_call | solution.py:184
  37.3 1.2 %collective-permute-done.8 = f32[8,2176]{1,0:T(8,128)S(1)} collective-permute-done((f32[8,2176]{1,0:T(8,128)S(1)}, f32[8,2176]{1,0:T(8,128)S(1)}, u32[]{:S(2)}, u32[]{:S(2)}) %collective-permute-start.8) | collective-permute-done | bytes 69664 | tf_op jit(solution)/shard_map/ppermute | solution.py:251
  38.6 1.5 %collective-permute-start.9 = (f32[8,2176]{1,0:T(8,128)S(1)}, f32[8,2176]{1,0:T(8,128)S(1)}, u32[]{:S(2)}, u32[]{:S(2)}) collective-permute-start(f32[8,2176]{1,0:T(8,128)S(1)} %add.25), channel_id=1, source_target_pairs={{0,2},{1,3},{2,0},{3,1},{4,6},{5,7},{6,4},{7,5},{8,10},{9,11},{10,... | collective-permute-start | bytes 208904 | tf_op jit(solution)/shard_map/ppermute | solution.py:251
  40.5 2.5 %collective-permute-done.9 = f32[8,2176]{1,0:T(8,128)S(1)} collective-permute-done((f32[8,2176]{1,0:T(8,128)S(1)}, f32[8,2176]{1,0:T(8,128)S(1)}, u32[]{:S(2)}, u32[]{:S(2)}) %collective-permute-start.9) | collective-permute-done | bytes 69664 | tf_op jit(solution)/shard_map/ppermute | solution.py:251
  43.0 1.0 %shard_map.135 = (f32[8,2048]{1,0:T(8,128)S(1)}, f32[8,2048]{1,0:T(8,128)S(1)}, f32[16,640]{1,0:T(8,128)S(1)}) custom-call(f32[8,2176]{1,0:T(8,128)S(1)} %add.26.applied, f32[16,2176]{1,0:T(8,128)S(1)} %add_add_fusion.sums, f32[8,2048]{1,0:T(8,128)S(1)} %get-tuple-element.16.shuffled, f32[8,2048]{1,0:T(8,128)S(1)} %copy-done.2, f32[8,2048]{1,0:T(8,128)S(1)} %copy-done.3, ...), custom_call_target="tpu_custom_call" | custom-call | tf_op jit(solution)/shard_map/pallas_call | solution.py:216
  44.0 1.5 %collective-permute-start.10 = (f32[16,640]{1,0:T(8,128)S(1)}, f32[16,640]{1,0:T(8,128)S(1)}, u32[]{:S(2)}, u32[]{:S(2)}) collective-permute-start(f32[16,640]{1,0:T(8,128)S(1)} %get-tuple-element.19), channel_id=1, source_target_pairs={{0,4},{4,0},{8,12},{12,8},{16,20},{20,16},{24,28},{28,24},{1,5},{5... | collective-permute-start | bytes 122888 | tf_op jit(solution)/shard_map/ppermute | solution.py:251
  45.6 2.5 %collective-permute-done.10 = f32[16,640]{1,0:T(8,128)S(1)} collective-permute-done((f32[16,640]{1,0:T(8,128)S(1)}, f32[16,640]{1,0:T(8,128)S(1)}, u32[]{:S(2)}, u32[]{:S(2)}) %collective-permute-start.10) | collective-permute-done | bytes 40992 | tf_op jit(solution)/shard_map/ppermute | solution.py:251
  48.0 2.0 %collective-permute-start.11 = (f32[16,640]{1,0:T(8,128)S(1)}, f32[16,640]{1,0:T(8,128)S(1)}, u32[]{:S(2)}, u32[]{:S(2)}) collective-permute-start(f32[16,640]{1,0:T(8,128)S(1)} %add.27.refs_0_), channel_id=1, source_target_pairs={{0,8},{4,12},{8,0},{12,4},{16,24},{20,28},{24,16},{28,20},{1,9},{5... | collective-permute-start | bytes 122888 | tf_op jit(solution)/shard_map/ppermute | solution.py:251
  50.1 1.0 %collective-permute-start.12 = (f32[16,640]{1,0:T(8,128)S(1)}, f32[16,640]{1,0:T(8,128)S(1)}, u32[]{:S(2)}, u32[]{:S(2)}) collective-permute-start(f32[16,640]{1,0:T(8,128)S(1)} %add.27.refs_0_), channel_id=1, source_target_pairs={{0,16},{4,20},{8,24},{12,28},{16,0},{20,4},{24,8},{28,12},{1,17},{... | collective-permute-start | bytes 122888 | tf_op jit(solution)/shard_map/ppermute | solution.py:251
  51.1 1.4 %collective-permute-start.13 = (f32[16,640]{1,0:T(8,128)S(1)}, f32[16,640]{1,0:T(8,128)S(1)}, u32[]{:S(2)}, u32[]{:S(2)}) collective-permute-start(f32[16,640]{1,0:T(8,128)S(1)} %add.27.refs_0_), channel_id=1, source_target_pairs={{0,24},{4,28},{8,16},{12,20},{16,8},{20,12},{24,0},{28,4},{1,25},{... | collective-permute-start | bytes 122888 | tf_op jit(solution)/shard_map/ppermute | solution.py:251
  53.8 1.6 %collective-permute-done.12.refs_2_ = f32[16,640]{1,0:T(8,128)S(1)} collective-permute-done((f32[16,640]{1,0:T(8,128)S(1)}, f32[16,640]{1,0:T(8,128)S(1)}, u32[]{:S(2)}, u32[]{:S(2)}) %collective-permute-start.12) | collective-permute-done | bytes 40992 | tf_op jit(solution)/shard_map/ppermute | solution.py:251
  55.4 1.6 %collective-permute-done.13.refs_3_ = f32[16,640]{1,0:T(8,128)S(1)} collective-permute-done((f32[16,640]{1,0:T(8,128)S(1)}, f32[16,640]{1,0:T(8,128)S(1)}, u32[]{:S(2)}, u32[]{:S(2)}) %collective-permute-start.13) | collective-permute-done | bytes 40992 | tf_op jit(solution)/shard_map/ppermute | solution.py:251
  (39 shorter events, 5.3 us)
Async XLA Ops:
  0.6 4.9 %collective-permute-start = (f32[16,128]{1,0:T(8,128)}, f32[16,128]{1,0:T(8,128)S(1)}, u32[]{:S(2)}, u32[]{:S(2)}) collective-permute-start(f32[16,128]{1,0:T(8,128)} %bitcast.6), channel_id=1, source_target_pairs={{0,4},{4,0},{8,12},{12,8},{16,20},{20,16},{24,28},{28,24},{1,5},{5... | collective-permute-start | bytes 24584 | tf_op jit(solution)/shard_map/ppermute | solution.py:251
  5.5 0.7 %copy-start.9 = (f32[2048]{0:T(1024)S(1)}, f32[2048]{0:T(1024)}, u32[]{:S(2)}) copy-start(f32[2048]{0:T(1024)} %param.14) | copy-start | bytes 24580
  6.2 5.8 %copy-start = (s32[2048,2048]{1,0:T(8,128)S(1)}, s32[2048,2048]{1,0:T(8,128)}, u32[]{:S(2)}) copy-start(s32[2048,2048]{1,0:T(8,128)} %geno.2) | copy-start | bytes 50331652
  6.2 10.3 %copy-start.2 = (f32[8,2048]{1,0:T(8,128)S(1)}, f32[8,2048]{1,0:T(8,128)}, u32[]{:S(2)}) copy-start(f32[8,2048]{1,0:T(8,128)} %direction.5) | copy-start | bytes 196612
  6.2 10.3 %copy-start.3 = (f32[8,2048]{1,0:T(8,128)S(1)}, f32[8,2048]{1,0:T(8,128)}, u32[]{:S(2)}) copy-start(f32[8,2048]{1,0:T(8,128)} %resid.3) | copy-start | bytes 196612
  6.2 10.3 %copy-start.4 = (s32[8,2048]{1,0:T(8,128)S(1)}, s32[8,2048]{1,0:T(8,128)}, u32[]{:S(2)}) copy-start(s32[8,2048]{1,0:T(8,128)} %perm.1) | copy-start | bytes 196612
  6.2 10.3 %copy-start.6 = (s32[2048]{0:T(1024)S(1)}, s32[2048]{0:T(1024)}, u32[]{:S(2)}) copy-start(s32[2048]{0:T(1024)} %param.11) | copy-start | bytes 24580
  6.2 6.7 %collective-permute-start.1 = (f32[32,128]{1,0:T(8,128)S(1)}, f32[32,128]{1,0:T(8,128)S(1)}, u32[]{:S(2)}, u32[]{:S(2)}) collective-permute-start(f32[32,128]{1,0:T(8,128)S(1)} %shard_map.130.refs_0_), channel_id=1, source_target_pairs={{0,8},{4,12},{8,0},{12,4},{16,24},{20,28},{24,16},{28,20},{1,9},{5... | collective-permute-start | bytes 49160 | tf_op jit(solution)/shard_map/ppermute | solution.py:251
  8.4 4.6 %collective-permute-start.2 = (f32[32,128]{1,0:T(8,128)S(1)}, f32[32,128]{1,0:T(8,128)S(1)}, u32[]{:S(2)}, u32[]{:S(2)}) collective-permute-start(f32[32,128]{1,0:T(8,128)S(1)} %shard_map.130.refs_0_), channel_id=1, source_target_pairs={{0,16},{4,20},{8,24},{12,28},{16,0},{20,4},{24,8},{28,12},{1,17},{... | collective-permute-start | bytes 49160 | tf_op jit(solution)/shard_map/ppermute | solution.py:251
  11.0 5.5 %collective-permute-start.3 = (f32[32,128]{1,0:T(8,128)S(1)}, f32[32,128]{1,0:T(8,128)S(1)}, u32[]{:S(2)}, u32[]{:S(2)}) collective-permute-start(f32[32,128]{1,0:T(8,128)S(1)} %shard_map.130.refs_0_), channel_id=1, source_target_pairs={{0,24},{4,28},{8,16},{12,20},{16,8},{20,12},{24,0},{28,4},{1,25},{... | collective-permute-start | bytes 49160 | tf_op jit(solution)/shard_map/ppermute | solution.py:251
  20.2 5.1 %collective-permute-start.4 = (f32[16,2176]{1,0:T(8,128)S(1)}, f32[16,2176]{1,0:T(8,128)S(1)}, u32[]{:S(2)}, u32[]{:S(2)}) collective-permute-start(f32[16,2176]{1,0:T(8,128)S(1)} %get-tuple-element.13), channel_id=1, source_target_pairs={{0,4},{4,0},{8,12},{12,8},{16,20},{20,16},{24,28},{28,24},{1,5},{5... | collective-permute-start | bytes 417800 | tf_op jit(solution)/shard_map/ppermute | solution.py:251
  25.3 10.0 %copy-start.8 = (f32[3]{0:T(128)S(1)}, f32[3]{0:T(128)}, u32[]{:S(2)}) copy-start(f32[3]{0:T(128)} %var_comp.3) | copy-start | bytes 40
  25.3 7.1 %collective-permute-start.5 = (f32[16,2176]{1,0:T(8,128)S(1)}, f32[16,2176]{1,0:T(8,128)S(1)}, u32[]{:S(2)}, u32[]{:S(2)}) collective-permute-start(f32[16,2176]{1,0:T(8,128)S(1)} %add.21), channel_id=1, source_target_pairs={{0,8},{4,12},{8,0},{12,4},{16,24},{20,28},{24,16},{28,20},{1,9},{5... | collective-permute-start | bytes 417800 | tf_op jit(solution)/shard_map/ppermute | solution.py:251
  25.4 9.9 %collective-permute-start.6 = (f32[16,2176]{1,0:T(8,128)S(1)}, f32[16,2176]{1,0:T(8,128)S(1)}, u32[]{:S(2)}, u32[]{:S(2)}) collective-permute-start(f32[16,2176]{1,0:T(8,128)S(1)} %add.21), channel_id=1, source_target_pairs={{0,16},{4,20},{8,24},{12,28},{16,0},{20,4},{24,8},{28,12},{1,17},{... | collective-permute-start | bytes 417800 | tf_op jit(solution)/shard_map/ppermute | solution.py:251
  26.5 8.7 %collective-permute-start.7 = (f32[16,2176]{1,0:T(8,128)S(1)}, f32[16,2176]{1,0:T(8,128)S(1)}, u32[]{:S(2)}, u32[]{:S(2)}) collective-permute-start(f32[16,2176]{1,0:T(8,128)S(1)} %add.21), channel_id=1, source_target_pairs={{0,24},{4,28},{8,16},{12,20},{16,8},{20,12},{24,0},{28,4},{1,25},{... | collective-permute-start | bytes 417800 | tf_op jit(solution)/shard_map/ppermute | solution.py:251
  32.4 7.7 %copy-start.1 = (s32[2048,512]{1,0:T(8,128)S(1)}, s32[2048,512]{1,0:T(8,128)}, u32[]{:S(2)}) copy-start(s32[2048,512]{1,0:T(8,128)} %geno.3) | copy-start | bytes 12582916
  32.4 10.6 %copy-start.5 = (f32[8,2048]{1,0:T(8,128)S(1)}, f32[8,2048]{1,0:T(8,128)}, u32[]{:S(2)}) copy-start(f32[8,2048]{1,0:T(8,128)} %solution.1) | copy-start | bytes 196612
  32.4 10.6 %copy-start.7 = (s32[512]{0:T(512)S(1)}, s32[512]{0:T(512)}, u32[]{:S(2)}) copy-start(s32[512]{0:T(512)} %param.13) | copy-start | bytes 6148
  37.3 1.3 %collective-permute-start.8 = (f32[8,2176]{1,0:T(8,128)S(1)}, f32[8,2176]{1,0:T(8,128)S(1)}, u32[]{:S(2)}, u32[]{:S(2)}) collective-permute-start(f32[8,2176]{1,0:T(8,128)S(1)} %shard_map.133), channel_id=1, source_target_pairs={{0,1},{1,0},{2,3},{3,2},{4,5},{5,4},{6,7},{7,6},{8,9},{9,8},{10,11... | collective-permute-start | bytes 208904 | tf_op jit(solution)/shard_map/ppermute | solution.py:251
  38.6 4.4 %collective-permute-start.9 = (f32[8,2176]{1,0:T(8,128)S(1)}, f32[8,2176]{1,0:T(8,128)S(1)}, u32[]{:S(2)}, u32[]{:S(2)}) collective-permute-start(f32[8,2176]{1,0:T(8,128)S(1)} %add.25), channel_id=1, source_target_pairs={{0,2},{1,3},{2,0},{3,1},{4,6},{5,7},{6,4},{7,5},{8,10},{9,11},{10,... | collective-permute-start | bytes 208904 | tf_op jit(solution)/shard_map/ppermute | solution.py:251
  44.0 4.0 %collective-permute-start.10 = (f32[16,640]{1,0:T(8,128)S(1)}, f32[16,640]{1,0:T(8,128)S(1)}, u32[]{:S(2)}, u32[]{:S(2)}) collective-permute-start(f32[16,640]{1,0:T(8,128)S(1)} %get-tuple-element.19), channel_id=1, source_target_pairs={{0,4},{4,0},{8,12},{12,8},{16,20},{20,16},{24,28},{28,24},{1,5},{5... | collective-permute-start | bytes 122888 | tf_op jit(solution)/shard_map/ppermute | solution.py:251
  48.0 5.7 %collective-permute-start.11 = (f32[16,640]{1,0:T(8,128)S(1)}, f32[16,640]{1,0:T(8,128)S(1)}, u32[]{:S(2)}, u32[]{:S(2)}) collective-permute-start(f32[16,640]{1,0:T(8,128)S(1)} %add.27.refs_0_), channel_id=1, source_target_pairs={{0,8},{4,12},{8,0},{12,4},{16,24},{20,28},{24,16},{28,20},{1,9},{5... | collective-permute-start | bytes 122888 | tf_op jit(solution)/shard_map/ppermute | solution.py:251
  50.1 5.3 %collective-permute-start.12 = (f32[16,640]{1,0:T(8,128)S(1)}, f32[16,640]{1,0:T(8,128)S(1)}, u32[]{:S(2)}, u32[]{:S(2)}) collective-permute-start(f32[16,640]{1,0:T(8,128)S(1)} %add.27.refs_0_), channel_id=1, source_target_pairs={{0,16},{4,20},{8,24},{12,28},{16,0},{20,4},{24,8},{28,12},{1,17},{... | collective-permute-start | bytes 122888 | tf_op jit(solution)/shard_map/ppermute | solution.py:251
  51.1 5.8 %collective-permute-start.13 = (f32[16,640]{1,0:T(8,128)S(1)}, f32[16,640]{1,0:T(8,128)S(1)}, u32[]{:S(2)}, u32[]{:S(2)}) collective-permute-start(f32[16,640]{1,0:T(8,128)S(1)} %add.27.refs_0_), channel_id=1, source_target_pairs={{0,24},{4,28},{8,16},{12,20},{16,8},{20,12},{24,0},{28,4},{1,25},{... | collective-permute-start | bytes 122888 | tf_op jit(solution)/shard_map/ppermute | solution.py:251

commit v4 on v3

--- a/solution.py
+++ b/solution.py
@@ -86,6 +86,15 @@
     )(codes)
 
 
+def blank_body(out):
+    out[...] = jnp.zeros_like(out)
+
+
+def blank(rows):
+    early = pl.CostEstimate(flops=1 << 34, bytes_accessed=1 << 25, transcendentals=0)
+    return call(blank_body, in_vmem((rows, LANES)), [], cost_estimate=early)()
+
+
 def stack_body(*refs):
     *blocks, out = refs
     out[...] = jnp.concatenate([block[...] for block in blocks], axis=0)
@@ -93,41 +102,28 @@
 
 def stack(blocks):
     rows = sum(block.shape[0] for block in blocks)
-    return call(
-        stack_body,
-        in_vmem((rows, LANES)),
-        [WHOLE] * len(blocks),
-        cost_estimate=pl.CostEstimate(flops=1 << 34, bytes_accessed=1 << 25, transcendentals=0),
-    )(*blocks)
+    return call(stack_body, in_vmem((rows, LANES)), [WHOLE] * len(blocks))(*blocks)
 
 
 def lookup(table, index, out):
     height = table.shape[0]
     rhs, count = index.shape
-    exact = jnp.bfloat16 if height <= 256 else jnp.float32
-    row = lax.broadcasted_iota(jnp.int32, (height, count), 0).astype(exact)
-    lane = lax.broadcasted_iota(jnp.int32, (LANES, count), 0)
-    high, middle, low = jnp.split(bf16_pieces(table.T), 3, axis=0)
-    left = jnp.concatenate(
-        [
-            jnp.concatenate([high, middle], axis=1),
-            jnp.concatenate([low, jnp.zeros_like(low)], axis=1),
-        ],
-        axis=0,
-    )
+    half = LANES // 2
+    exact = jnp.bfloat16 if 2 * height <= 256 else jnp.float32
+    row = lax.broadcasted_iota(jnp.int32, (2 * height, count), 0).astype(exact)
+    lane = lax.broadcasted_iota(jnp.int32, (half, count), 0)
+    halves = table.T
+    left = bf16_pieces(jnp.concatenate([halves[:half], halves[half:]], axis=1))
+    one, none = jnp.ones((), exact), jnp.zeros((), exact)
     for b in range(rhs):
         places = index[b : b + 1, :]
-        wanted = (places // LANES).astype(jnp.float32).astype(exact)
-        one, none = jnp.ones((), exact), jnp.zeros((), exact)
-        chosen = jnp.where(row == wanted, one, none).astype(jnp.bfloat16)
-        values = jnp.dot(
-            left,
-            jnp.concatenate([chosen, chosen], axis=0),
-            preferred_element_type=jnp.float32,
+        wanted = places // LANES + height * (places // half % 2)
+        chosen = jnp.where(row == wanted.astype(jnp.float32).astype(exact), one, none)
+        values = add_pieces(
+            jnp.dot(left, chosen.astype(jnp.bfloat16), preferred_element_type=jnp.float32)
         )
-        values = values[:LANES] + values[LANES:]
         out[b : b + 1, :] = jnp.sum(
-            jnp.where(lane == places % LANES, values, 0.0), axis=0, keepdims=True
+            jnp.where(lane == places % half, values, 0.0), axis=0, keepdims=True
         )
 
 
@@ -188,7 +184,7 @@
     )(sums, flipped, pct, shuffled, var_comp)
 
 
-def step_body(applied, sums, shuffled, direction, resid, solution, codes, pct, var_comp,
+def step_body(applied, sums, shuffled, direction, resid, solution, codes, pct, empty, var_comp,
               new_solution, new_resid, scores, *, root):
     rhs, count = shuffled.shape
     tests = codes.shape[1]
@@ -208,10 +204,10 @@
     scores[:, :tests] = (scale / root) * (product - mean * jnp.sum(both, axis=1, keepdims=True))
     norm = jnp.sum(left * left, axis=1, keepdims=True)
     scores[:rhs, tests:] = jnp.broadcast_to(norm, (rhs, LANES))
-    scores[rhs:, tests:] = jnp.zeros((rhs, LANES), jnp.float32)
-
-
-def step(applied, sums, shuffled, direction, resid, solution, codes, pct, var_comp, root):
+    scores[rhs:, tests:] = empty[...]
+
+
+def step(applied, sums, shuffled, direction, resid, solution, codes, pct, empty, var_comp, root):
     rhs, count = shuffled.shape
     return call(
         functools.partial(step_body, root=root),
@@ -220,8 +216,8 @@
             in_vmem((rhs, count)),
             in_vmem((2 * rhs, codes.shape[1] + LANES)),
         ],
-        [WHOLE] * 8 + [SCALARS],
-    )(applied, sums, shuffled, direction, resid, solution, codes, pct, var_comp)
+        [WHOLE] * 9 + [SCALARS],
+    )(applied, sums, shuffled, direction, resid, solution, codes, pct, empty, var_comp)
 
 
 def finish_body(sums, new_resid, direction, *refs):
@@ -292,13 +288,14 @@
 def local(
     geno, allele_pct, test_geno, test_pct, exposure, perm, var_comp, solution, resid, direction
 ):
-    count = resid.shape[1]
+    rhs, count = resid.shape
     slab = geno.shape[1]
     tests = test_geno.shape[1]
     slab_total = float(slab * lax.axis_size("var"))
     root = math.sqrt(count * lax.axis_size("samp"))
     pct = allele_pct.reshape(1, slab)
-    table = gather_all(exposure.reshape(-1, LANES), "samp", pairs_then_fours)
+    empty, shard = lax.optimization_barrier((blank(rhs), exposure.reshape(-1, LANES)))
+    table = gather_all(shard, "samp", pairs_then_fours)
     codes = cast_codes(geno)
     shuffled, sums = slab_sums(table, perm, direction, resid, codes, pct, "samp")
     sums = sums + swap(sums, "samp", 1)
@@ -310,7 +307,7 @@
     test_codes = cast_codes(test_geno)
     new_solution, new_resid, scores = step(
         applied, sums, shuffled, direction, resid, solution, test_codes,
-        test_pct.reshape(1, tests), var_comp, root,
+        test_pct.reshape(1, tests), empty, var_comp, root,
     )
     parts = sum_parts(scores, "samp", pairs_then_fours)
     new_direction, scores = finish(parts, sums, new_resid, direction)

time: 57.9 us -> 56 us (0.967)
  local copies, waits for them, and re-layouts: 3 us -> 1.97 us
    unnamed x22, local copies, waits for them, and re-layouts: 3 us -> 1.97 us
where the time goes in v4:
time: 56 us; the launch traced here: 55.8 us
  starting transfers between devices  21.3 us (38%)
  waiting for transfers between devices  20.9 us (37%)
  Pallas kernels  10.8 us (19%)
  local copies, waits for them, and re-layouts  1.97 us (4%)
  between operations  0.82 us (1%)
    ppermute x14, starting transfers between devices, swap(): return lax.ppermute(x, axis, [(i, i ^ distance) for i in range(size)])  21.3 us
    ppermute x14, waiting for transfers between devices, swap(): return lax.ppermute(x, axis, [(i, i ^ distance) for i in range(size)])  20.9 us
    pallas_call x1, Pallas kernels, slab_sums(): call(functools.partial(slab_body, axis=axis), [in_vmem(perm.shape), in_vm...  3.18 us
    pallas_call x1, Pallas kernels, flip_codes(): call(functools.partial(flip_body, start=start), in_vmem((width, codes.sha...  2.59 us
    unnamed x22, local copies, waits for them, and re-layouts  1.97 us
    pallas_call x1, Pallas kernels, kernel_part(): call(functools.partial(kernel_body, slab_total=slab_total), in_vmem((rhs,...  1.96 us
    pallas_call x2, Pallas kernels, cast_codes(): return call(cast_body, in_vmem(geno.shape, jnp.bfloat16), [WHOLE])(geno)  1.3 us
  transfers between devices with their start and end apart: 14, of which 10 were waited for; matrix products, arithmetic and copies ran while one was open for 2% of the time, Pallas kernels for 7%

profile of v4, /device:TPU:0, one launch (start us, length us, event | category | flops | bytes accessed | tf_op | source)
XLA Modules:
  0.0 55.8 jit_solution(3498310978479103298)
XLA Ops:
  1.3 3.0 %collective-permute-start = (f32[16,128]{1,0:T(8,128)S(1)}, f32[16,128]{1,0:T(8,128)S(1)}, u32[]{:S(2)}, u32[]{:S(2)}) collective-permute-start(f32[16,128]{1,0:T(8,128)S(1)} %bitcast.5), channel_id=1, source_target_pairs={{0,4},{4,0},{8,12},{12,8},{16,20},{20,16},{24,28},{28,24},{1,5},{5... | collective-permute-start | bytes 24584 | tf_op jit(solution)/shard_map/ppermute | solution.py:247
  4.3 1.6 %collective-permute-done.refs_1_ = f32[16,128]{1,0:T(8,128)S(1)} collective-permute-done((f32[16,128]{1,0:T(8,128)S(1)}, f32[16,128]{1,0:T(8,128)S(1)}, u32[]{:S(2)}, u32[]{:S(2)}) %collective-permute-start) | collective-permute-done | bytes 8224 | tf_op jit(solution)/shard_map/ppermute | solution.py:247
  6.0 2.1 %collective-permute-start.1 = (f32[32,128]{1,0:T(8,128)S(1)}, f32[32,128]{1,0:T(8,128)S(1)}, u32[]{:S(2)}, u32[]{:S(2)}) collective-permute-start(f32[32,128]{1,0:T(8,128)S(1)} %shard_map.131.refs_0_), channel_id=1, source_target_pairs={{0,8},{4,12},{8,0},{12,4},{16,24},{20,28},{24,16},{28,20},{1,9},{5... | collective-permute-start | bytes 49160 | tf_op jit(solution)/shard_map/ppermute | solution.py:247
  8.1 2.6 %collective-permute-start.2 = (f32[32,128]{1,0:T(8,128)S(1)}, f32[32,128]{1,0:T(8,128)S(1)}, u32[]{:S(2)}, u32[]{:S(2)}) collective-permute-start(f32[32,128]{1,0:T(8,128)S(1)} %shard_map.131.refs_0_), channel_id=1, source_target_pairs={{0,16},{4,20},{8,24},{12,28},{16,0},{20,4},{24,8},{28,12},{1,17},{... | collective-permute-start | bytes 49160 | tf_op jit(solution)/shard_map/ppermute | solution.py:247
  10.7 1.0 %shard_map.129.codes = bf16[2048,2048]{1,0:T(8,128)(2,1)S(1)} custom-call(s32[2048,2048]{1,0:T(8,128)S(1)} %copy-done), custom_call_target="tpu_custom_call" | custom-call | tf_op jit(solution)/shard_map/pallas_call | solution.py:67
  11.7 1.1 %collective-permute-done.2.refs_2_ = f32[32,128]{1,0:T(8,128)S(1)} collective-permute-done((f32[32,128]{1,0:T(8,128)S(1)}, f32[32,128]{1,0:T(8,128)S(1)}, u32[]{:S(2)}, u32[]{:S(2)}) %collective-permute-start.2) | collective-permute-done | bytes 16416 | tf_op jit(solution)/shard_map/ppermute | solution.py:247
  12.7 3.5 %collective-permute-done.3.refs_3_ = f32[32,128]{1,0:T(8,128)S(1)} collective-permute-done((f32[32,128]{1,0:T(8,128)S(1)}, f32[32,128]{1,0:T(8,128)S(1)}, u32[]{:S(2)}, u32[]{:S(2)}) %collective-permute-start.3) | collective-permute-done | bytes 16416 | tf_op jit(solution)/shard_map/ppermute | solution.py:247
  16.2 3.2 %shard_map.132 = (f32[8,2048]{1,0:T(8,128)S(1)}, f32[16,2176]{1,0:T(8,128)S(1)}) custom-call(s32[8,2048]{1,0:T(8,128)S(1)} %copy-done.4, f32[8,2048]{1,0:T(8,128)S(1)} %copy-done.2, f32[8,2048]{1,0:T(8,128)S(1)} %copy-done.3, bf16[2048,2048]{1,0:T(8,128)(2,1)S(1)} %shard_map.129.codes, s32[1,2048]{1,0:T(1,128)S(1)} %bitcast.3, ...), custom_call_target="tpu_custom_call" | custom-call | tf_op jit(solution)/shard_map/pallas_call | solution.py:153
  19.4 1.5 %collective-permute-start.4 = (f32[16,2176]{1,0:T(8,128)S(1)}, f32[16,2176]{1,0:T(8,128)S(1)}, u32[]{:S(2)}, u32[]{:S(2)}) collective-permute-start(f32[16,2176]{1,0:T(8,128)S(1)} %get-tuple-element.16), channel_id=1, source_target_pairs={{0,4},{4,0},{8,12},{12,8},{16,20},{20,16},{24,28},{28,24},{1,5},{5... | collective-permute-start | bytes 417800 | tf_op jit(solution)/shard_map/ppermute | solution.py:247
  21.0 3.5 %collective-permute-done.4 = f32[16,2176]{1,0:T(8,128)S(1)} collective-permute-done((f32[16,2176]{1,0:T(8,128)S(1)}, f32[16,2176]{1,0:T(8,128)S(1)}, u32[]{:S(2)}, u32[]{:S(2)}) %collective-permute-start.4) | collective-permute-done | bytes 139296 | tf_op jit(solution)/shard_map/ppermute | solution.py:247
  25.3 3.6 %collective-permute-start.7 = (f32[16,2176]{1,0:T(8,128)S(1)}, f32[16,2176]{1,0:T(8,128)S(1)}, u32[]{:S(2)}, u32[]{:S(2)}) collective-permute-start(f32[16,2176]{1,0:T(8,128)S(1)} %add.21), channel_id=1, source_target_pairs={{0,24},{4,28},{8,16},{12,20},{16,8},{20,12},{24,0},{28,4},{1,25},{... | collective-permute-start | bytes 417800 | tf_op jit(solution)/shard_map/ppermute | solution.py:247
  29.0 2.6 %shard_map.133.flipped = bf16[2048,2048]{1,0:T(8,128)(2,1)S(1)} custom-call(bf16[2048,2048]{1,0:T(8,128)(2,1)S(1)} %shard_map.129.codes), custom_call_target="tpu_custom_call" | custom-call | flops 2147483648 | tf_op jit(solution)/shard_map/pallas_call | solution.py:81
  31.6 2.9 %collective-permute-done.6 = f32[16,2176]{1,0:T(8,128)S(1)} collective-permute-done((f32[16,2176]{1,0:T(8,128)S(1)}, f32[16,2176]{1,0:T(8,128)S(1)}, u32[]{:S(2)}, u32[]{:S(2)}) %collective-permute-start.6) | collective-permute-done | bytes 139296 | tf_op jit(solution)/shard_map/ppermute | solution.py:247
  34.5 2.0 %shard_map.134 = f32[8,2176]{1,0:T(8,128)S(1)} custom-call(f32[16,2176]{1,0:T(8,128)S(1)} %add_add_fusion.sums, bf16[2048,2048]{1,0:T(8,128)(2,1)S(1)} %shard_map.133.flipped, s32[1,2048]{1,0:T(1,128)S(1)} %bitcast.4, f32[8,2048]{1,0:T(8,128)S(1)} %get-tuple-element.19.shuffled, f32[3]{0:T(128)S(1)} %copy-done.9), custom_call_target="tpu_custom_call" | custom-call | tf_op jit(solution)/shard_map/pallas_call | solution.py:180
  36.5 1.2 %collective-permute-done.8 = f32[8,2176]{1,0:T(8,128)S(1)} collective-permute-done((f32[8,2176]{1,0:T(8,128)S(1)}, f32[8,2176]{1,0:T(8,128)S(1)}, u32[]{:S(2)}, u32[]{:S(2)}) %collective-permute-start.8) | collective-permute-done | bytes 69664 | tf_op jit(solution)/shard_map/ppermute | solution.py:247
  37.8 1.6 %collective-permute-start.9 = (f32[8,2176]{1,0:T(8,128)S(1)}, f32[8,2176]{1,0:T(8,128)S(1)}, u32[]{:S(2)}, u32[]{:S(2)}) collective-permute-start(f32[8,2176]{1,0:T(8,128)S(1)} %add.25), channel_id=1, source_target_pairs={{0,2},{1,3},{2,0},{3,1},{4,6},{5,7},{6,4},{7,5},{8,10},{9,11},{10,... | collective-permute-start | bytes 208904 | tf_op jit(solution)/shard_map/ppermute | solution.py:247
  39.7 2.5 %collective-permute-done.9 = f32[8,2176]{1,0:T(8,128)S(1)} collective-permute-done((f32[8,2176]{1,0:T(8,128)S(1)}, f32[8,2176]{1,0:T(8,128)S(1)}, u32[]{:S(2)}, u32[]{:S(2)}) %collective-permute-start.9) | collective-permute-done | bytes 69664 | tf_op jit(solution)/shard_map/ppermute | solution.py:247
  42.2 1.0 %shard_map.136 = (f32[8,2048]{1,0:T(8,128)S(1)}, f32[8,2048]{1,0:T(8,128)S(1)}, f32[16,640]{1,0:T(8,128)S(1)}) custom-call(f32[8,2176]{1,0:T(8,128)S(1)} %add.26.applied, f32[16,2176]{1,0:T(8,128)S(1)} %add_add_fusion.sums, f32[8,2048]{1,0:T(8,128)S(1)} %get-tuple-element.19.shuffled, f32[8,2048]{1,0:T(8,128)S(1)} %copy-done.2, f32[8,2048]{1,0:T(8,128)S(1)} %copy-done.3, ...), custom_call_target="tpu_custom_call" | custom-call | tf_op jit(solution)/shard_map/pallas_call | solution.py:212
  43.2 1.5 %collective-permute-start.10 = (f32[16,640]{1,0:T(8,128)S(1)}, f32[16,640]{1,0:T(8,128)S(1)}, u32[]{:S(2)}, u32[]{:S(2)}) collective-permute-start(f32[16,640]{1,0:T(8,128)S(1)} %get-tuple-element.23), channel_id=1, source_target_pairs={{0,4},{4,0},{8,12},{12,8},{16,20},{20,16},{24,28},{28,24},{1,5},{5... | collective-permute-start | bytes 122888 | tf_op jit(solution)/shard_map/ppermute | solution.py:247
  44.8 2.5 %collective-permute-done.10 = f32[16,640]{1,0:T(8,128)S(1)} collective-permute-done((f32[16,640]{1,0:T(8,128)S(1)}, f32[16,640]{1,0:T(8,128)S(1)}, u32[]{:S(2)}, u32[]{:S(2)}) %collective-permute-start.10) | collective-permute-done | bytes 40992 | tf_op jit(solution)/shard_map/ppermute | solution.py:247
  47.3 2.0 %collective-permute-start.11 = (f32[16,640]{1,0:T(8,128)S(1)}, f32[16,640]{1,0:T(8,128)S(1)}, u32[]{:S(2)}, u32[]{:S(2)}) collective-permute-start(f32[16,640]{1,0:T(8,128)S(1)} %add.27.refs_0_), channel_id=1, source_target_pairs={{0,8},{4,12},{8,0},{12,4},{16,24},{20,28},{24,16},{28,20},{1,9},{5... | collective-permute-start | bytes 122888 | tf_op jit(solution)/shard_map/ppermute | solution.py:247
  49.3 2.4 %collective-permute-start.13 = (f32[16,640]{1,0:T(8,128)S(1)}, f32[16,640]{1,0:T(8,128)S(1)}, u32[]{:S(2)}, u32[]{:S(2)}) collective-permute-start(f32[16,640]{1,0:T(8,128)S(1)} %add.27.refs_0_), channel_id=1, source_target_pairs={{0,24},{4,28},{8,16},{12,20},{16,8},{20,12},{24,0},{28,4},{1,25},{... | collective-permute-start | bytes 122888 | tf_op jit(solution)/shard_map/ppermute | solution.py:247
  53.0 1.2 %collective-permute-done.12.refs_2_ = f32[16,640]{1,0:T(8,128)S(1)} collective-permute-done((f32[16,640]{1,0:T(8,128)S(1)}, f32[16,640]{1,0:T(8,128)S(1)}, u32[]{:S(2)}, u32[]{:S(2)}) %collective-permute-start.12) | collective-permute-done | bytes 40992 | tf_op jit(solution)/shard_map/ppermute | solution.py:247
  54.2 0.9 %collective-permute-done.13.refs_3_ = f32[16,640]{1,0:T(8,128)S(1)} collective-permute-done((f32[16,640]{1,0:T(8,128)S(1)}, f32[16,640]{1,0:T(8,128)S(1)}, u32[]{:S(2)}, u32[]{:S(2)}) %collective-permute-start.13) | collective-permute-done | bytes 40992 | tf_op jit(solution)/shard_map/ppermute | solution.py:247
  (40 shorter events, 4.0 us)
Async XLA Ops:
  0.6 0.7 %copy-start.7 = (f32[2048]{0:T(1024)S(1)}, f32[2048]{0:T(1024)}, u32[]{:S(2)}) copy-start(f32[2048]{0:T(1024)} %param.14) | copy-start | bytes 24580
  0.6 10.1 %copy-start = (s32[2048,2048]{1,0:T(8,128)S(1)}, s32[2048,2048]{1,0:T(8,128)}, u32[]{:S(2)}) copy-start(s32[2048,2048]{1,0:T(8,128)} %geno.2) | copy-start | bytes 50331652
  1.3 4.6 %collective-permute-start = (f32[16,128]{1,0:T(8,128)S(1)}, f32[16,128]{1,0:T(8,128)S(1)}, u32[]{:S(2)}, u32[]{:S(2)}) collective-permute-start(f32[16,128]{1,0:T(8,128)S(1)} %bitcast.5), channel_id=1, source_target_pairs={{0,4},{4,0},{8,12},{12,8},{16,20},{20,16},{24,28},{28,24},{1,5},{5... | collective-permute-start | bytes 24584 | tf_op jit(solution)/shard_map/ppermute | solution.py:247
  5.9 10.3 %copy-start.2 = (f32[8,2048]{1,0:T(8,128)S(1)}, f32[8,2048]{1,0:T(8,128)}, u32[]{:S(2)}) copy-start(f32[8,2048]{1,0:T(8,128)} %direction.5) | copy-start | bytes 196612
  5.9 10.3 %copy-start.3 = (f32[8,2048]{1,0:T(8,128)S(1)}, f32[8,2048]{1,0:T(8,128)}, u32[]{:S(2)}) copy-start(f32[8,2048]{1,0:T(8,128)} %resid.3) | copy-start | bytes 196612
  5.9 10.3 %copy-start.4 = (s32[8,2048]{1,0:T(8,128)S(1)}, s32[8,2048]{1,0:T(8,128)}, u32[]{:S(2)}) copy-start(s32[8,2048]{1,0:T(8,128)} %perm.1) | copy-start | bytes 196612
  5.9 10.3 %copy-start.6 = (s32[2048]{0:T(1024)S(1)}, s32[2048]{0:T(1024)}, u32[]{:S(2)}) copy-start(s32[2048]{0:T(1024)} %param.11) | copy-start | bytes 24580
  6.0 5.7 %collective-permute-start.1 = (f32[32,128]{1,0:T(8,128)S(1)}, f32[32,128]{1,0:T(8,128)S(1)}, u32[]{:S(2)}, u32[]{:S(2)}) collective-permute-start(f32[32,128]{1,0:T(8,128)S(1)} %shard_map.131.refs_0_), channel_id=1, source_target_pairs={{0,8},{4,12},{8,0},{12,4},{16,24},{20,28},{24,16},{28,20},{1,9},{5... | collective-permute-start | bytes 49160 | tf_op jit(solution)/shard_map/ppermute | solution.py:247
  8.1 4.6 %collective-permute-start.2 = (f32[32,128]{1,0:T(8,128)S(1)}, f32[32,128]{1,0:T(8,128)S(1)}, u32[]{:S(2)}, u32[]{:S(2)}) collective-permute-start(f32[32,128]{1,0:T(8,128)S(1)} %shard_map.131.refs_0_), channel_id=1, source_target_pairs={{0,16},{4,20},{8,24},{12,28},{16,0},{20,4},{24,8},{28,12},{1,17},{... | collective-permute-start | bytes 49160 | tf_op jit(solution)/shard_map/ppermute | solution.py:247
  10.7 5.5 %collective-permute-start.3 = (f32[32,128]{1,0:T(8,128)S(1)}, f32[32,128]{1,0:T(8,128)S(1)}, u32[]{:S(2)}, u32[]{:S(2)}) collective-permute-start(f32[32,128]{1,0:T(8,128)S(1)} %shard_map.131.refs_0_), channel_id=1, source_target_pairs={{0,24},{4,28},{8,16},{12,20},{16,8},{20,12},{24,0},{28,4},{1,25},{... | collective-permute-start | bytes 49160 | tf_op jit(solution)/shard_map/ppermute | solution.py:247
  19.4 5.1 %collective-permute-start.4 = (f32[16,2176]{1,0:T(8,128)S(1)}, f32[16,2176]{1,0:T(8,128)S(1)}, u32[]{:S(2)}, u32[]{:S(2)}) collective-permute-start(f32[16,2176]{1,0:T(8,128)S(1)} %get-tuple-element.16), channel_id=1, source_target_pairs={{0,4},{4,0},{8,12},{12,8},{16,20},{20,16},{24,28},{28,24},{1,5},{5... | collective-permute-start | bytes 417800 | tf_op jit(solution)/shard_map/ppermute | solution.py:247
  24.5 10.0 %copy-start.9 = (f32[3]{0:T(128)S(1)}, f32[3]{0:T(128)}, u32[]{:S(2)}) copy-start(f32[3]{0:T(128)} %var_comp.3) | copy-start | bytes 40
  24.5 7.1 %collective-permute-start.5 = (f32[16,2176]{1,0:T(8,128)S(1)}, f32[16,2176]{1,0:T(8,128)S(1)}, u32[]{:S(2)}, u32[]{:S(2)}) collective-permute-start(f32[16,2176]{1,0:T(8,128)S(1)} %add.21), channel_id=1, source_target_pairs={{0,8},{4,12},{8,0},{12,4},{16,24},{20,28},{24,16},{28,20},{1,9},{5... | collective-permute-start | bytes 417800 | tf_op jit(solution)/shard_map/ppermute | solution.py:247
  24.6 9.9 %collective-permute-start.6 = (f32[16,2176]{1,0:T(8,128)S(1)}, f32[16,2176]{1,0:T(8,128)S(1)}, u32[]{:S(2)}, u32[]{:S(2)}) collective-permute-start(f32[16,2176]{1,0:T(8,128)S(1)} %add.21), channel_id=1, source_target_pairs={{0,16},{4,20},{8,24},{12,28},{16,0},{20,4},{24,8},{28,12},{1,17},{... | collective-permute-start | bytes 417800 | tf_op jit(solution)/shard_map/ppermute | solution.py:247
  25.3 9.2 %collective-permute-start.7 = (f32[16,2176]{1,0:T(8,128)S(1)}, f32[16,2176]{1,0:T(8,128)S(1)}, u32[]{:S(2)}, u32[]{:S(2)}) collective-permute-start(f32[16,2176]{1,0:T(8,128)S(1)} %add.21), channel_id=1, source_target_pairs={{0,24},{4,28},{8,16},{12,20},{16,8},{20,12},{24,0},{28,4},{1,25},{... | collective-permute-start | bytes 417800 | tf_op jit(solution)/shard_map/ppermute | solution.py:247
  31.6 7.8 %copy-start.1 = (s32[2048,512]{1,0:T(8,128)S(1)}, s32[2048,512]{1,0:T(8,128)}, u32[]{:S(2)}) copy-start(s32[2048,512]{1,0:T(8,128)} %geno.3) | copy-start | bytes 12582916
  31.6 10.6 %copy-start.5 = (f32[8,2048]{1,0:T(8,128)S(1)}, f32[8,2048]{1,0:T(8,128)}, u32[]{:S(2)}) copy-start(f32[8,2048]{1,0:T(8,128)} %solution.1) | copy-start | bytes 196612
  31.6 10.6 %copy-start.8 = (s32[512]{0:T(512)S(1)}, s32[512]{0:T(512)}, u32[]{:S(2)}) copy-start(s32[512]{0:T(512)} %param.13) | copy-start | bytes 6148
  36.5 1.3 %collective-permute-start.8 = (f32[8,2176]{1,0:T(8,128)S(1)}, f32[8,2176]{1,0:T(8,128)S(1)}, u32[]{:S(2)}, u32[]{:S(2)}) collective-permute-start(f32[8,2176]{1,0:T(8,128)S(1)} %shard_map.134), channel_id=1, source_target_pairs={{0,1},{1,0},{2,3},{3,2},{4,5},{5,4},{6,7},{7,6},{8,9},{9,8},{10,11... | collective-permute-start | bytes 208904 | tf_op jit(solution)/shard_map/ppermute | solution.py:247
  37.8 4.4 %collective-permute-start.9 = (f32[8,2176]{1,0:T(8,128)S(1)}, f32[8,2176]{1,0:T(8,128)S(1)}, u32[]{:S(2)}, u32[]{:S(2)}) collective-permute-start(f32[8,2176]{1,0:T(8,128)S(1)} %add.25), channel_id=1, source_target_pairs={{0,2},{1,3},{2,0},{3,1},{4,6},{5,7},{6,4},{7,5},{8,10},{9,11},{10,... | collective-permute-start | bytes 208904 | tf_op jit(solution)/shard_map/ppermute | solution.py:247
  43.2 4.0 %collective-permute-start.10 = (f32[16,640]{1,0:T(8,128)S(1)}, f32[16,640]{1,0:T(8,128)S(1)}, u32[]{:S(2)}, u32[]{:S(2)}) collective-permute-start(f32[16,640]{1,0:T(8,128)S(1)} %get-tuple-element.23), channel_id=1, source_target_pairs={{0,4},{4,0},{8,12},{12,8},{16,20},{20,16},{24,28},{28,24},{1,5},{5... | collective-permute-start | bytes 122888 | tf_op jit(solution)/shard_map/ppermute | solution.py:247
  47.3 5.7 %collective-permute-start.11 = (f32[16,640]{1,0:T(8,128)S(1)}, f32[16,640]{1,0:T(8,128)S(1)}, u32[]{:S(2)}, u32[]{:S(2)}) collective-permute-start(f32[16,640]{1,0:T(8,128)S(1)} %add.27.refs_0_), channel_id=1, source_target_pairs={{0,8},{4,12},{8,0},{12,4},{16,24},{20,28},{24,16},{28,20},{1,9},{5... | collective-permute-start | bytes 122888 | tf_op jit(solution)/shard_map/ppermute | solution.py:247
  49.3 4.9 %collective-permute-start.12 = (f32[16,640]{1,0:T(8,128)S(1)}, f32[16,640]{1,0:T(8,128)S(1)}, u32[]{:S(2)}, u32[]{:S(2)}) collective-permute-start(f32[16,640]{1,0:T(8,128)S(1)} %add.27.refs_0_), channel_id=1, source_target_pairs={{0,16},{4,20},{8,24},{12,28},{16,0},{20,4},{24,8},{28,12},{1,17},{... | collective-permute-start | bytes 122888 | tf_op jit(solution)/shard_map/ppermute | solution.py:247
  49.3 5.8 %collective-permute-start.13 = (f32[16,640]{1,0:T(8,128)S(1)}, f32[16,640]{1,0:T(8,128)S(1)}, u32[]{:S(2)}, u32[]{:S(2)}) collective-permute-start(f32[16,640]{1,0:T(8,128)S(1)} %add.27.refs_0_), channel_id=1, source_target_pairs={{0,24},{4,28},{8,16},{12,20},{16,8},{20,12},{24,0},{28,4},{1,25},{... | collective-permute-start | bytes 122888 | tf_op jit(solution)/shard_map/ppermute | solution.py:247

commit v5 on v4

--- a/solution.py
+++ b/solution.py
@@ -14,6 +14,9 @@
 VMEM_BYTES = 10 << 20
 WHOLE = pl.BlockSpec(memory_space=pltpu.VMEM)
 SCALARS = pl.BlockSpec(memory_space=pltpu.SMEM)
+GATHER_ORDER = (3, 2, 1)
+SLAB_ORDER = (2, 1, 3)
+SCORE_ORDER = (3, 1, 2)
 
 
 def in_vmem(shape, dtype=jnp.float32):
@@ -131,7 +134,7 @@
     *table, shuffled, sums = refs
     rhs = direction.shape[0]
     slab = codes.shape[1]
-    table = jnp.concatenate([block[...] for block in table], axis=0)
+    table = jnp.concatenate([block[...] for block in by_distance(table, GATHER_ORDER)], axis=0)
     shard = table.size // lax.axis_size(axis)
     lookup(table, perm[...] ^ (lax.axis_index(axis) * shard), shuffled)
     mean, scale = spread(pct[...])
@@ -224,7 +227,7 @@
     *parts, new_direction, scores = refs
     rhs = direction.shape[0]
     tests = scores.shape[1]
-    total = add_parts([part[...] for part in parts])
+    total = add_parts([part[...] for part in by_distance(parts, SCORE_ORDER)])
     scores[...] = total[:, :tests]
     ratio = total[:rhs, tests : tests + 1] / sums[:rhs, -LANES:][:, :1]
     new_direction[...] = new_resid[...] + ratio * direction[...]
@@ -242,9 +245,27 @@
     )(sums, new_resid, direction, *parts)
 
 
+def add_body(*refs):
+    *parts, out = refs
+    out[...] = add_parts([part[...] for part in by_distance(parts, SLAB_ORDER)])
+
+
+def add_up(parts):
+    return call(add_body, in_vmem(parts[0].shape), [WHOLE] * len(parts))(*parts)
+
+
 def swap(x, axis, distance):
     size = lax.axis_size(axis)
     return lax.ppermute(x, axis, [(i, i ^ distance) for i in range(size)])
+
+
+def swaps(x, axis, width, unit, order):
+    return [swap(x, axis, k * unit) for k in order if k < width]
+
+
+def by_distance(parts, order):
+    order = [k for k in order if k < len(parts)]
+    return [parts[0]] + [parts[1 + order.index(k)] for k in range(1, len(parts))]
 
 
 def add_parts(parts):
@@ -253,25 +274,25 @@
     return sum(parts[1:], parts[0])
 
 
-def sum_parts(x, axis, widths, unit=1):
+def sum_parts(x, axis, widths, order, unit=1):
     parts = [x]
     for width in widths(lax.axis_size(axis) // unit):
-        held = add_parts(parts)
-        parts = [held] + [swap(held, axis, k * unit) for k in range(1, width)]
+        held = add_parts(by_distance(parts, order))
+        parts = [held] + swaps(held, axis, width, unit, order)
         unit *= width
     return parts
 
 
-def sum_all(x, axis, widths, unit=1):
-    return add_parts(sum_parts(x, axis, widths, unit))
+def sum_all(x, axis, widths):
+    return add_parts(by_distance(sum_parts(x, axis, widths, (1,)), (1,)))
 
 
 def gather_all(x, axis, widths):
     blocks = [x]
     unit = 1
     for width in widths(lax.axis_size(axis)):
-        held = blocks[0] if len(blocks) == 1 else stack(blocks)
-        blocks = [held] + [swap(held, axis, k * unit) for k in range(1, width)]
+        held = blocks[0] if len(blocks) == 1 else stack(by_distance(blocks, GATHER_ORDER))
+        blocks = [held] + swaps(held, axis, width, unit, GATHER_ORDER)
         unit *= width
     return blocks
 
@@ -301,7 +322,8 @@
     sums = sums + swap(sums, "samp", 1)
     codes, sums = lax.optimization_barrier((codes, sums))
     flipped = flip_codes(codes, 0, slab)
-    sums = sum_all(sums, "samp", pairs_then_fours, 2)
+    parts = sum_parts(sums, "samp", pairs_then_fours, SLAB_ORDER, 2)
+    sums = add_up(parts)
     applied = kernel_part(sums, flipped, pct, shuffled, var_comp, slab_total)
     applied = sum_all(applied, "var", pairs)
     test_codes = cast_codes(test_geno)
@@ -309,7 +331,7 @@
         applied, sums, shuffled, direction, resid, solution, test_codes,
         test_pct.reshape(1, tests), empty, var_comp, root,
     )
-    parts = sum_parts(scores, "samp", pairs_then_fours)
+    parts = sum_parts(scores, "samp", pairs_then_fours, SCORE_ORDER)
     new_direction, scores = finish(parts, sums, new_resid, direction)
     return (new_solution, new_resid, new_direction, scores)
 

time: 56 us -> 54.4 us (0.971)
  waiting for transfers between devices: 20.9 us -> 19.2 us
    ppermute x14, waiting for transfers between devices: 20.9 us -> 19.2 us  [swap(): return lax.ppermute(x, axis, [(i, i ^ distance) for i in range(size)])]
  transfers between devices with their start and end apart: 14 -> 14, of which waited for: 10 -> 12; matrix products, arithmetic and copies ran while one was open for 2% -> 2% of each run, Pallas kernels for 7% -> 7%
where the time goes in v5:
time: 54.4 us; the launch traced here: 54.2 us
  starting transfers between devices  21.4 us (39%)
  waiting for transfers between devices  19.2 us (35%)
  Pallas kernels  10.8 us (20%)
  local copies, waits for them, and re-layouts  1.97 us (4%)
  between operations  0.81 us (1%)
    ppermute x14, starting transfers between devices, swap(): return lax.ppermute(x, axis, [(i, i ^ distance) for i in range(size)])  21.4 us
    ppermute x14, waiting for transfers between devices, swap(): return lax.ppermute(x, axis, [(i, i ^ distance) for i in range(size)])  19.2 us
    pallas_call x1, Pallas kernels, slab_sums(): call(functools.partial(slab_body, axis=axis), [in_vmem(perm.shape), in_vm...  3.19 us
    pallas_call x1, Pallas kernels, flip_codes(): call(functools.partial(flip_body, start=start), in_vmem((width, codes.sha...  2.59 us
    unnamed x22, local copies, waits for them, and re-layouts  1.97 us
    pallas_call x1, Pallas kernels, kernel_part(): call(functools.partial(kernel_body, slab_total=slab_total), in_vmem((rhs,...  1.97 us
    pallas_call x2, Pallas kernels, cast_codes(): return call(cast_body, in_vmem(geno.shape, jnp.bfloat16), [WHOLE])(geno)  1.3 us
  transfers between devices with their start and end apart: 14, of which 12 were waited for; matrix products, arithmetic and copies ran while one was open for 2% of the time, Pallas kernels for 7%

profile of v5, /device:TPU:0, one launch (start us, length us, event | category | flops | bytes accessed | tf_op | source)
XLA Modules:
  0.0 54.2 jit_solution(9807422721665001255)
XLA Ops:
  0.7 0.7 %copy-done.7 = f32[2048]{0:T(1024)S(1)} copy-done((f32[2048]{0:T(1024)S(1)}, f32[2048]{0:T(1024)}, u32[]{:S(2)}) %copy-start.7) | copy-done | bytes 8216
  1.3 3.0 %collective-permute-start = (f32[16,128]{1,0:T(8,128)S(1)}, f32[16,128]{1,0:T(8,128)S(1)}, u32[]{:S(2)}, u32[]{:S(2)}) collective-permute-start(f32[16,128]{1,0:T(8,128)S(1)} %bitcast.5), channel_id=1, source_target_pairs={{0,4},{4,0},{8,12},{12,8},{16,20},{20,16},{24,28},{28,24},{1,5},{5... | collective-permute-start | bytes 24584 | tf_op jit(solution)/shard_map/ppermute | solution.py:259
  4.3 1.6 %collective-permute-done.refs_1_ = f32[16,128]{1,0:T(8,128)S(1)} collective-permute-done((f32[16,128]{1,0:T(8,128)S(1)}, f32[16,128]{1,0:T(8,128)S(1)}, u32[]{:S(2)}, u32[]{:S(2)}) %collective-permute-start) | collective-permute-done | bytes 8224 | tf_op jit(solution)/shard_map/ppermute | solution.py:259
  6.0 4.2 %collective-permute-start.1 = (f32[32,128]{1,0:T(8,128)S(1)}, f32[32,128]{1,0:T(8,128)S(1)}, u32[]{:S(2)}, u32[]{:S(2)}) collective-permute-start(f32[32,128]{1,0:T(8,128)S(1)} %shard_map.131.refs_0_), channel_id=1, source_target_pairs={{0,24},{4,28},{8,16},{12,20},{16,8},{20,12},{24,0},{28,4},{1,25},{... | collective-permute-start | bytes 49160 | tf_op jit(solution)/shard_map/ppermute | solution.py:259
  10.8 1.0 %shard_map.129.codes = bf16[2048,2048]{1,0:T(8,128)(2,1)S(1)} custom-call(s32[2048,2048]{1,0:T(8,128)S(1)} %copy-done), custom_call_target="tpu_custom_call" | custom-call | tf_op jit(solution)/shard_map/pallas_call | solution.py:70
  11.8 2.9 %collective-permute-done.2.refs_2_ = f32[32,128]{1,0:T(8,128)S(1)} collective-permute-done((f32[32,128]{1,0:T(8,128)S(1)}, f32[32,128]{1,0:T(8,128)S(1)}, u32[]{:S(2)}, u32[]{:S(2)}) %collective-permute-start.2) | collective-permute-done | bytes 16416 | tf_op jit(solution)/shard_map/ppermute | solution.py:259
  14.8 3.2 %shard_map.132 = (f32[8,2048]{1,0:T(8,128)S(1)}, f32[16,2176]{1,0:T(8,128)S(1)}) custom-call(s32[8,2048]{1,0:T(8,128)S(1)} %copy-done.4, f32[8,2048]{1,0:T(8,128)S(1)} %copy-done.2, f32[8,2048]{1,0:T(8,128)S(1)} %copy-done.3, bf16[2048,2048]{1,0:T(8,128)(2,1)S(1)} %shard_map.129.codes, s32[1,2048]{1,0:T(1,128)S(1)} %bitcast.3, ...), custom_call_target="tpu_custom_call" | custom-call | tf_op jit(solution)/shard_map/pallas_call | solution.py:156
  18.0 1.5 %collective-permute-start.4 = (f32[16,2176]{1,0:T(8,128)S(1)}, f32[16,2176]{1,0:T(8,128)S(1)}, u32[]{:S(2)}, u32[]{:S(2)}) collective-permute-start(f32[16,2176]{1,0:T(8,128)S(1)} %get-tuple-element.16), channel_id=1, source_target_pairs={{0,4},{4,0},{8,12},{12,8},{16,20},{20,16},{24,28},{28,24},{1,5},{5... | collective-permute-start | bytes 417800 | tf_op jit(solution)/shard_map/ppermute | solution.py:259
  19.5 3.5 %collective-permute-done.4 = f32[16,2176]{1,0:T(8,128)S(1)} collective-permute-done((f32[16,2176]{1,0:T(8,128)S(1)}, f32[16,2176]{1,0:T(8,128)S(1)}, u32[]{:S(2)}, u32[]{:S(2)}) %collective-permute-start.4) | collective-permute-done | bytes 139296 | tf_op jit(solution)/shard_map/ppermute | solution.py:259
  23.1 2.1 %collective-permute-start.5 = (f32[16,2176]{1,0:T(8,128)S(1)}, f32[16,2176]{1,0:T(8,128)S(1)}, u32[]{:S(2)}, u32[]{:S(2)}) collective-permute-start(f32[16,2176]{1,0:T(8,128)S(1)} %add.12.refs_0_), channel_id=1, source_target_pairs={{0,16},{4,20},{8,24},{12,28},{16,0},{20,4},{24,8},{28,12},{1,17},{... | collective-permute-start | bytes 417800 | tf_op jit(solution)/shard_map/ppermute | solution.py:259
  25.2 2.4 %collective-permute-start.7 = (f32[16,2176]{1,0:T(8,128)S(1)}, f32[16,2176]{1,0:T(8,128)S(1)}, u32[]{:S(2)}, u32[]{:S(2)}) collective-permute-start(f32[16,2176]{1,0:T(8,128)S(1)} %add.12.refs_0_), channel_id=1, source_target_pairs={{0,24},{4,28},{8,16},{12,20},{16,8},{20,12},{24,0},{28,4},{1,25},{... | collective-permute-start | bytes 417800 | tf_op jit(solution)/shard_map/ppermute | solution.py:259
  27.5 2.6 %shard_map.134.flipped = bf16[2048,2048]{1,0:T(8,128)(2,1)S(1)} custom-call(bf16[2048,2048]{1,0:T(8,128)(2,1)S(1)} %shard_map.129.codes), custom_call_target="tpu_custom_call" | custom-call | flops 2147483648 | tf_op jit(solution)/shard_map/pallas_call | solution.py:84
  30.2 2.5 %collective-permute-done.5.refs_1_ = f32[16,2176]{1,0:T(8,128)S(1)} collective-permute-done((f32[16,2176]{1,0:T(8,128)S(1)}, f32[16,2176]{1,0:T(8,128)S(1)}, u32[]{:S(2)}, u32[]{:S(2)}) %collective-permute-start.5) | collective-permute-done | bytes 139296 | tf_op jit(solution)/shard_map/ppermute | solution.py:259
  33.2 2.0 %shard_map.135 = f32[8,2176]{1,0:T(8,128)S(1)} custom-call(f32[16,2176]{1,0:T(8,128)S(1)} %shard_map.133.sums, bf16[2048,2048]{1,0:T(8,128)(2,1)S(1)} %shard_map.134.flipped, s32[1,2048]{1,0:T(1,128)S(1)} %bitcast.4, f32[8,2048]{1,0:T(8,128)S(1)} %get-tuple-element.19.shuffled, f32[3]{0:T(128)S(1)} %copy-done.9), custom_call_target="tpu_custom_call" | custom-call | tf_op jit(solution)/shard_map/pallas_call | solution.py:183
  35.2 1.2 %collective-permute-done.8 = f32[8,2176]{1,0:T(8,128)S(1)} collective-permute-done((f32[8,2176]{1,0:T(8,128)S(1)}, f32[8,2176]{1,0:T(8,128)S(1)}, u32[]{:S(2)}, u32[]{:S(2)}) %collective-permute-start.8) | collective-permute-done | bytes 69664 | tf_op jit(solution)/shard_map/ppermute | solution.py:259
  36.4 1.6 %collective-permute-start.9 = (f32[8,2176]{1,0:T(8,128)S(1)}, f32[8,2176]{1,0:T(8,128)S(1)}, u32[]{:S(2)}, u32[]{:S(2)}) collective-permute-start(f32[8,2176]{1,0:T(8,128)S(1)} %add.13), channel_id=1, source_target_pairs={{0,2},{1,3},{2,0},{3,1},{4,6},{5,7},{6,4},{7,5},{8,10},{9,11},{10,... | collective-permute-start | bytes 208904 | tf_op jit(solution)/shard_map/ppermute | solution.py:259
  38.4 2.4 %collective-permute-done.9 = f32[8,2176]{1,0:T(8,128)S(1)} collective-permute-done((f32[8,2176]{1,0:T(8,128)S(1)}, f32[8,2176]{1,0:T(8,128)S(1)}, u32[]{:S(2)}, u32[]{:S(2)}) %collective-permute-start.9) | collective-permute-done | bytes 69664 | tf_op jit(solution)/shard_map/ppermute | solution.py:259
  40.9 1.0 %shard_map.137 = (f32[8,2048]{1,0:T(8,128)S(1)}, f32[8,2048]{1,0:T(8,128)S(1)}, f32[16,640]{1,0:T(8,128)S(1)}) custom-call(f32[8,2176]{1,0:T(8,128)S(1)} %add.14.applied, f32[16,2176]{1,0:T(8,128)S(1)} %shard_map.133.sums, f32[8,2048]{1,0:T(8,128)S(1)} %get-tuple-element.19.shuffled, f32[8,2048]{1,0:T(8,128)S(1)} %copy-done.2, f32[8,2048]{1,0:T(8,128)S(1)} %copy-done.3, ...), custom_call_target="tpu_custom_call" | custom-call | tf_op jit(solution)/shard_map/pallas_call | solution.py:215
  41.9 1.6 %collective-permute-start.10 = (f32[16,640]{1,0:T(8,128)S(1)}, f32[16,640]{1,0:T(8,128)S(1)}, u32[]{:S(2)}, u32[]{:S(2)}) collective-permute-start(f32[16,640]{1,0:T(8,128)S(1)} %get-tuple-element.23), channel_id=1, source_target_pairs={{0,4},{4,0},{8,12},{12,8},{16,20},{20,16},{24,28},{28,24},{1,5},{5... | collective-permute-start | bytes 122888 | tf_op jit(solution)/shard_map/ppermute | solution.py:259
  43.5 2.4 %collective-permute-done.10 = f32[16,640]{1,0:T(8,128)S(1)} collective-permute-done((f32[16,640]{1,0:T(8,128)S(1)}, f32[16,640]{1,0:T(8,128)S(1)}, u32[]{:S(2)}, u32[]{:S(2)}) %collective-permute-start.10) | collective-permute-done | bytes 40992 | tf_op jit(solution)/shard_map/ppermute | solution.py:259
  45.9 2.0 %collective-permute-start.11 = (f32[16,640]{1,0:T(8,128)S(1)}, f32[16,640]{1,0:T(8,128)S(1)}, u32[]{:S(2)}, u32[]{:S(2)}) collective-permute-start(f32[16,640]{1,0:T(8,128)S(1)} %add.15.refs_0_), channel_id=1, source_target_pairs={{0,24},{4,28},{8,16},{12,20},{16,8},{20,12},{24,0},{28,4},{1,25},{... | collective-permute-start | bytes 122888 | tf_op jit(solution)/shard_map/ppermute | solution.py:259
  48.6 1.7 %collective-permute-start.13 = (f32[16,640]{1,0:T(8,128)S(1)}, f32[16,640]{1,0:T(8,128)S(1)}, u32[]{:S(2)}, u32[]{:S(2)}) collective-permute-start(f32[16,640]{1,0:T(8,128)S(1)} %add.15.refs_0_), channel_id=1, source_target_pairs={{0,16},{4,20},{8,24},{12,28},{16,0},{20,4},{24,8},{28,12},{1,17},{... | collective-permute-start | bytes 122888 | tf_op jit(solution)/shard_map/ppermute | solution.py:259
  52.1 1.3 %collective-permute-done.13.refs_3_ = f32[16,640]{1,0:T(8,128)S(1)} collective-permute-done((f32[16,640]{1,0:T(8,128)S(1)}, f32[16,640]{1,0:T(8,128)S(1)}, u32[]{:S(2)}, u32[]{:S(2)}) %collective-permute-start.13) | collective-permute-done | bytes 40992 | tf_op jit(solution)/shard_map/ppermute | solution.py:259
  53.5 0.7 %shard_map.138 = (f32[8,2048]{1,0:T(8,128)}, f32[16,512]{1,0:T(8,128)}) custom-call(f32[16,2176]{1,0:T(8,128)S(1)} %shard_map.133.sums, f32[8,2048]{1,0:T(8,128)S(1)} %get-tuple-element.27.new_resid, f32[8,2048]{1,0:T(8,128)S(1)} %copy-done.2, f32[16,640]{1,0:T(8,128)S(1)} %add.15.refs_0_, f32[16,640]{1,0:T(8,128)S(1)} %collective-permute-done.11.refs_1_, ...), custom_call_target="tpu_custom_call" | custom-call | tf_op jit(solution)/shard_map/pallas_call | solution.py:238
  (40 shorter events, 4.2 us)
Async XLA Ops:
  0.6 0.7 %copy-start.7 = (f32[2048]{0:T(1024)S(1)}, f32[2048]{0:T(1024)}, u32[]{:S(2)}) copy-start(f32[2048]{0:T(1024)} %param.14) | copy-start | bytes 24580
  0.6 10.1 %copy-start = (s32[2048,2048]{1,0:T(8,128)S(1)}, s32[2048,2048]{1,0:T(8,128)}, u32[]{:S(2)}) copy-start(s32[2048,2048]{1,0:T(8,128)} %geno.2) | copy-start | bytes 50331652
  1.3 4.6 %collective-permute-start = (f32[16,128]{1,0:T(8,128)S(1)}, f32[16,128]{1,0:T(8,128)S(1)}, u32[]{:S(2)}, u32[]{:S(2)}) collective-permute-start(f32[16,128]{1,0:T(8,128)S(1)} %bitcast.5), channel_id=1, source_target_pairs={{0,4},{4,0},{8,12},{12,8},{16,20},{20,16},{24,28},{28,24},{1,5},{5... | collective-permute-start | bytes 24584 | tf_op jit(solution)/shard_map/ppermute | solution.py:259
  5.9 8.8 %copy-start.2 = (f32[8,2048]{1,0:T(8,128)S(1)}, f32[8,2048]{1,0:T(8,128)}, u32[]{:S(2)}) copy-start(f32[8,2048]{1,0:T(8,128)} %direction.5) | copy-start | bytes 196612
  5.9 8.8 %copy-start.3 = (f32[8,2048]{1,0:T(8,128)S(1)}, f32[8,2048]{1,0:T(8,128)}, u32[]{:S(2)}) copy-start(f32[8,2048]{1,0:T(8,128)} %resid.3) | copy-start | bytes 196612
  5.9 8.8 %copy-start.4 = (s32[8,2048]{1,0:T(8,128)S(1)}, s32[8,2048]{1,0:T(8,128)}, u32[]{:S(2)}) copy-start(s32[8,2048]{1,0:T(8,128)} %perm.1) | copy-start | bytes 196612
  5.9 8.8 %copy-start.6 = (s32[2048]{0:T(1024)S(1)}, s32[2048]{0:T(1024)}, u32[]{:S(2)}) copy-start(s32[2048]{0:T(1024)} %param.11) | copy-start | bytes 24580
  6.0 5.9 %collective-permute-start.1 = (f32[32,128]{1,0:T(8,128)S(1)}, f32[32,128]{1,0:T(8,128)S(1)}, u32[]{:S(2)}, u32[]{:S(2)}) collective-permute-start(f32[32,128]{1,0:T(8,128)S(1)} %shard_map.131.refs_0_), channel_id=1, source_target_pairs={{0,24},{4,28},{8,16},{12,20},{16,8},{20,12},{24,0},{28,4},{1,25},{... | collective-permute-start | bytes 49160 | tf_op jit(solution)/shard_map/ppermute | solution.py:259
  10.1 4.6 %collective-permute-start.2 = (f32[32,128]{1,0:T(8,128)S(1)}, f32[32,128]{1,0:T(8,128)S(1)}, u32[]{:S(2)}, u32[]{:S(2)}) collective-permute-start(f32[32,128]{1,0:T(8,128)S(1)} %shard_map.131.refs_0_), channel_id=1, source_target_pairs={{0,16},{4,20},{8,24},{12,28},{16,0},{20,4},{24,8},{28,12},{1,17},{... | collective-permute-start | bytes 49160 | tf_op jit(solution)/shard_map/ppermute | solution.py:259
  10.1 4.6 %collective-permute-start.3 = (f32[32,128]{1,0:T(8,128)S(1)}, f32[32,128]{1,0:T(8,128)S(1)}, u32[]{:S(2)}, u32[]{:S(2)}) collective-permute-start(f32[32,128]{1,0:T(8,128)S(1)} %shard_map.131.refs_0_), channel_id=1, source_target_pairs={{0,8},{4,12},{8,0},{12,4},{16,24},{20,28},{24,16},{28,20},{1,9},{5... | collective-permute-start | bytes 49160 | tf_op jit(solution)/shard_map/ppermute | solution.py:259
  18.0 5.1 %collective-permute-start.4 = (f32[16,2176]{1,0:T(8,128)S(1)}, f32[16,2176]{1,0:T(8,128)S(1)}, u32[]{:S(2)}, u32[]{:S(2)}) collective-permute-start(f32[16,2176]{1,0:T(8,128)S(1)} %get-tuple-element.16), channel_id=1, source_target_pairs={{0,4},{4,0},{8,12},{12,8},{16,20},{20,16},{24,28},{28,24},{1,5},{5... | collective-permute-start | bytes 417800 | tf_op jit(solution)/shard_map/ppermute | solution.py:259
  23.1 10.1 %copy-start.9 = (f32[3]{0:T(128)S(1)}, f32[3]{0:T(128)}, u32[]{:S(2)}) copy-start(f32[3]{0:T(128)} %var_comp.3) | copy-start | bytes 40
  23.1 9.6 %collective-permute-start.5 = (f32[16,2176]{1,0:T(8,128)S(1)}, f32[16,2176]{1,0:T(8,128)S(1)}, u32[]{:S(2)}, u32[]{:S(2)}) collective-permute-start(f32[16,2176]{1,0:T(8,128)S(1)} %add.12.refs_0_), channel_id=1, source_target_pairs={{0,16},{4,20},{8,24},{12,28},{16,0},{20,4},{24,8},{28,12},{1,17},{... | collective-permute-start | bytes 417800 | tf_op jit(solution)/shard_map/ppermute | solution.py:259
  25.2 8.0 %collective-permute-start.6 = (f32[16,2176]{1,0:T(8,128)S(1)}, f32[16,2176]{1,0:T(8,128)S(1)}, u32[]{:S(2)}, u32[]{:S(2)}) collective-permute-start(f32[16,2176]{1,0:T(8,128)S(1)} %add.12.refs_0_), channel_id=1, source_target_pairs={{0,8},{4,12},{8,0},{12,4},{16,24},{20,28},{24,16},{28,20},{1,9},{5... | collective-permute-start | bytes 417800 | tf_op jit(solution)/shard_map/ppermute | solution.py:259
  25.2 8.0 %collective-permute-start.7 = (f32[16,2176]{1,0:T(8,128)S(1)}, f32[16,2176]{1,0:T(8,128)S(1)}, u32[]{:S(2)}, u32[]{:S(2)}) collective-permute-start(f32[16,2176]{1,0:T(8,128)S(1)} %add.12.refs_0_), channel_id=1, source_target_pairs={{0,24},{4,28},{8,16},{12,20},{16,8},{20,12},{24,0},{28,4},{1,25},{... | collective-permute-start | bytes 417800 | tf_op jit(solution)/shard_map/ppermute | solution.py:259
  30.1 7.9 %copy-start.1 = (s32[2048,512]{1,0:T(8,128)S(1)}, s32[2048,512]{1,0:T(8,128)}, u32[]{:S(2)}) copy-start(s32[2048,512]{1,0:T(8,128)} %geno.3) | copy-start | bytes 12582916
  30.2 10.7 %copy-start.5 = (f32[8,2048]{1,0:T(8,128)S(1)}, f32[8,2048]{1,0:T(8,128)}, u32[]{:S(2)}) copy-start(f32[8,2048]{1,0:T(8,128)} %solution.1) | copy-start | bytes 196612
  30.2 10.7 %copy-start.8 = (s32[512]{0:T(512)S(1)}, s32[512]{0:T(512)}, u32[]{:S(2)}) copy-start(s32[512]{0:T(512)} %param.13) | copy-start | bytes 6148
  35.2 1.3 %collective-permute-start.8 = (f32[8,2176]{1,0:T(8,128)S(1)}, f32[8,2176]{1,0:T(8,128)S(1)}, u32[]{:S(2)}, u32[]{:S(2)}) collective-permute-start(f32[8,2176]{1,0:T(8,128)S(1)} %shard_map.135), channel_id=1, source_target_pairs={{0,1},{1,0},{2,3},{3,2},{4,5},{5,4},{6,7},{7,6},{8,9},{9,8},{10,11... | collective-permute-start | bytes 208904 | tf_op jit(solution)/shard_map/ppermute | solution.py:259
  36.4 4.4 %collective-permute-start.9 = (f32[8,2176]{1,0:T(8,128)S(1)}, f32[8,2176]{1,0:T(8,128)S(1)}, u32[]{:S(2)}, u32[]{:S(2)}) collective-permute-start(f32[8,2176]{1,0:T(8,128)S(1)} %add.13), channel_id=1, source_target_pairs={{0,2},{1,3},{2,0},{3,1},{4,6},{5,7},{6,4},{7,5},{8,10},{9,11},{10,... | collective-permute-start | bytes 208904 | tf_op jit(solution)/shard_map/ppermute | solution.py:259
  41.9 4.0 %collective-permute-start.10 = (f32[16,640]{1,0:T(8,128)S(1)}, f32[16,640]{1,0:T(8,128)S(1)}, u32[]{:S(2)}, u32[]{:S(2)}) collective-permute-start(f32[16,640]{1,0:T(8,128)S(1)} %get-tuple-element.23), channel_id=1, source_target_pairs={{0,4},{4,0},{8,12},{12,8},{16,20},{20,16},{24,28},{28,24},{1,5},{5... | collective-permute-start | bytes 122888 | tf_op jit(solution)/shard_map/ppermute | solution.py:259
  45.9 5.8 %collective-permute-start.11 = (f32[16,640]{1,0:T(8,128)S(1)}, f32[16,640]{1,0:T(8,128)S(1)}, u32[]{:S(2)}, u32[]{:S(2)}) collective-permute-start(f32[16,640]{1,0:T(8,128)S(1)} %add.15.refs_0_), channel_id=1, source_target_pairs={{0,24},{4,28},{8,16},{12,20},{16,8},{20,12},{24,0},{28,4},{1,25},{... | collective-permute-start | bytes 122888 | tf_op jit(solution)/shard_map/ppermute | solution.py:259
  47.9 4.2 %collective-permute-start.12 = (f32[16,640]{1,0:T(8,128)S(1)}, f32[16,640]{1,0:T(8,128)S(1)}, u32[]{:S(2)}, u32[]{:S(2)}) collective-permute-start(f32[16,640]{1,0:T(8,128)S(1)} %add.15.refs_0_), channel_id=1, source_target_pairs={{0,8},{4,12},{8,0},{12,4},{16,24},{20,28},{24,16},{28,20},{1,9},{5... | collective-permute-start | bytes 122888 | tf_op jit(solution)/shard_map/ppermute | solution.py:259
  48.6 4.9 %collective-permute-start.13 = (f32[16,640]{1,0:T(8,128)S(1)}, f32[16,640]{1,0:T(8,128)S(1)}, u32[]{:S(2)}, u32[]{:S(2)}) collective-permute-start(f32[16,640]{1,0:T(8,128)S(1)} %add.15.refs_0_), channel_id=1, source_target_pairs={{0,16},{4,20},{8,24},{12,28},{16,0},{20,4},{24,8},{28,12},{1,17},{... | collective-permute-start | bytes 122888 | tf_op jit(solution)/shard_map/ppermute | solution.py:259

commit v6 on v5

--- a/solution.py
+++ b/solution.py
@@ -287,14 +287,16 @@
     return add_parts(by_distance(sum_parts(x, axis, widths, (1,)), (1,)))
 
 
-def gather_all(x, axis, widths):
+def gather_all(x, axis, widths, beside):
     blocks = [x]
     unit = 1
     for width in widths(lax.axis_size(axis)):
         held = blocks[0] if len(blocks) == 1 else stack(by_distance(blocks, GATHER_ORDER))
         blocks = [held] + swaps(held, axis, width, unit, GATHER_ORDER)
+        if unit == 1:
+            beside, blocks[1] = lax.optimization_barrier((beside, blocks[1]))
         unit *= width
-    return blocks
+    return blocks, beside
 
 
 def pairs_then_fours(size):
@@ -315,8 +317,9 @@
     slab_total = float(slab * lax.axis_size("var"))
     root = math.sqrt(count * lax.axis_size("samp"))
     pct = allele_pct.reshape(1, slab)
-    empty, shard = lax.optimization_barrier((blank(rhs), exposure.reshape(-1, LANES)))
-    table = gather_all(shard, "samp", pairs_then_fours)
+    table, empty = gather_all(
+        exposure.reshape(-1, LANES), "samp", pairs_then_fours, blank(rhs)
+    )
     codes = cast_codes(geno)
     shuffled, sums = slab_sums(table, perm, direction, resid, codes, pct, "samp")
     sums = sums + swap(sums, "samp", 1)

time: 54.4 us -> 54 us (level)
  local copies, waits for them, and re-layouts: 1.97 us -> 1.33 us
    unnamed x22 -> x28, local copies, waits for them, and re-layouts: 1.97 us -> 1.33 us
where the time goes in v6:
time: 54 us; the launch traced here: 53.8 us
  starting transfers between devices  21.6 us (40%)
  waiting for transfers between devices  19.3 us (36%)
  Pallas kernels  10.8 us (20%)
  local copies, waits for them, and re-layouts  1.33 us (2%)
  between operations  0.84 us (2%)
    ppermute x14, starting transfers between devices, swap(): return lax.ppermute(x, axis, [(i, i ^ distance) for i in range(size)])  21.6 us
    ppermute x14, waiting for transfers between devices, swap(): return lax.ppermute(x, axis, [(i, i ^ distance) for i in range(size)])  19.3 us
    pallas_call x1, Pallas kernels, slab_sums(): call(functools.partial(slab_body, axis=axis), [in_vmem(perm.shape), in_vm...  3.18 us
    pallas_call x1, Pallas kernels, flip_codes(): call(functools.partial(flip_body, start=start), in_vmem((width, codes.sha...  2.59 us
    pallas_call x1, Pallas kernels, kernel_part(): call(functools.partial(kernel_body, slab_total=slab_total), in_vmem((rhs,...  1.93 us
    unnamed x28, local copies, waits for them, and re-layouts  1.33 us
    pallas_call x2, Pallas kernels, cast_codes(): return call(cast_body, in_vmem(geno.shape, jnp.bfloat16), [WHOLE])(geno)  1.31 us
  transfers between devices with their start and end apart: 14, of which 12 were waited for; matrix products, arithmetic and copies ran while one was open for 2% of the time, Pallas kernels for 7%

profile of v6, /device:TPU:0, one launch (start us, length us, event | category | flops | bytes accessed | tf_op | source)
XLA Modules:
  0.0 53.8 jit_solution(12825979268863764324)
XLA Ops:
  0.7 3.0 %collective-permute-start = (f32[16,128]{1,0:T(8,128)}, f32[16,128]{1,0:T(8,128)S(1)}, u32[]{:S(2)}, u32[]{:S(2)}) collective-permute-start(f32[16,128]{1,0:T(8,128)} %bitcast.7), channel_id=1, source_target_pairs={{0,4},{4,0},{8,12},{12,8},{16,20},{20,16},{24,28},{28,24},{1,5},{5... | collective-permute-start | bytes 24584 | tf_op jit(solution)/shard_map/ppermute | solution.py:259
  3.7 1.8 %collective-permute-done.refs_1_ = f32[16,128]{1,0:T(8,128)S(1)} collective-permute-done((f32[16,128]{1,0:T(8,128)}, f32[16,128]{1,0:T(8,128)S(1)}, u32[]{:S(2)}, u32[]{:S(2)}) %collective-permute-start) | collective-permute-done | bytes 8224 | tf_op jit(solution)/shard_map/ppermute | solution.py:259
  5.6 4.2 %collective-permute-start.1 = (f32[32,128]{1,0:T(8,128)S(1)}, f32[32,128]{1,0:T(8,128)S(1)}, u32[]{:S(2)}, u32[]{:S(2)}) collective-permute-start(f32[32,128]{1,0:T(8,128)S(1)} %shard_map.131.refs_0_), channel_id=1, source_target_pairs={{0,24},{4,28},{8,16},{12,20},{16,8},{20,12},{24,0},{28,4},{1,25},{... | collective-permute-start | bytes 49160 | tf_op jit(solution)/shard_map/ppermute | solution.py:259
  10.4 1.0 %shard_map.129.codes = bf16[2048,2048]{1,0:T(8,128)(2,1)S(1)} custom-call(s32[2048,2048]{1,0:T(8,128)S(1)} %bitcast.4), custom_call_target="tpu_custom_call" | custom-call | tf_op jit(solution)/shard_map/pallas_call | solution.py:70
  11.5 2.9 %collective-permute-done.2.refs_2_ = f32[32,128]{1,0:T(8,128)S(1)} collective-permute-done((f32[32,128]{1,0:T(8,128)S(1)}, f32[32,128]{1,0:T(8,128)S(1)}, u32[]{:S(2)}, u32[]{:S(2)}) %collective-permute-start.2) | collective-permute-done | bytes 16416 | tf_op jit(solution)/shard_map/ppermute | solution.py:259
  14.4 3.2 %shard_map.132 = (f32[8,2048]{1,0:T(8,128)S(1)}, f32[16,2176]{1,0:T(8,128)S(1)}) custom-call(s32[8,2048]{1,0:T(8,128)S(1)} %copy-done.3, f32[8,2048]{1,0:T(8,128)S(1)} %copy-done.1, f32[8,2048]{1,0:T(8,128)S(1)} %copy-done.2, bf16[2048,2048]{1,0:T(8,128)(2,1)S(1)} %shard_map.129.codes, s32[1,2048]{1,0:T(1,128)S(1)} %bitcast.5, ...), custom_call_target="tpu_custom_call" | custom-call | tf_op jit(solution)/shard_map/pallas_call | solution.py:156
  17.6 1.5 %collective-permute-start.4 = (f32[16,2176]{1,0:T(8,128)S(1)}, f32[16,2176]{1,0:T(8,128)S(1)}, u32[]{:S(2)}, u32[]{:S(2)}) collective-permute-start(f32[16,2176]{1,0:T(8,128)S(1)} %get-tuple-element.16), channel_id=1, source_target_pairs={{0,4},{4,0},{8,12},{12,8},{16,20},{20,16},{24,28},{28,24},{1,5},{5... | collective-permute-start | bytes 417800 | tf_op jit(solution)/shard_map/ppermute | solution.py:259
  19.2 3.5 %collective-permute-done.4 = f32[16,2176]{1,0:T(8,128)S(1)} collective-permute-done((f32[16,2176]{1,0:T(8,128)S(1)}, f32[16,2176]{1,0:T(8,128)S(1)}, u32[]{:S(2)}, u32[]{:S(2)}) %collective-permute-start.4) | collective-permute-done | bytes 139296 | tf_op jit(solution)/shard_map/ppermute | solution.py:259
  22.7 2.1 %collective-permute-start.5 = (f32[16,2176]{1,0:T(8,128)S(1)}, f32[16,2176]{1,0:T(8,128)S(1)}, u32[]{:S(2)}, u32[]{:S(2)}) collective-permute-start(f32[16,2176]{1,0:T(8,128)S(1)} %add.12.refs_0_), channel_id=1, source_target_pairs={{0,16},{4,20},{8,24},{12,28},{16,0},{20,4},{24,8},{28,12},{1,17},{... | collective-permute-start | bytes 417800 | tf_op jit(solution)/shard_map/ppermute | solution.py:259
  24.8 2.4 %collective-permute-start.7 = (f32[16,2176]{1,0:T(8,128)S(1)}, f32[16,2176]{1,0:T(8,128)S(1)}, u32[]{:S(2)}, u32[]{:S(2)}) collective-permute-start(f32[16,2176]{1,0:T(8,128)S(1)} %add.12.refs_0_), channel_id=1, source_target_pairs={{0,24},{4,28},{8,16},{12,20},{16,8},{20,12},{24,0},{28,4},{1,25},{... | collective-permute-start | bytes 417800 | tf_op jit(solution)/shard_map/ppermute | solution.py:259
  27.2 2.6 %shard_map.134.flipped = bf16[2048,2048]{1,0:T(8,128)(2,1)S(1)} custom-call(bf16[2048,2048]{1,0:T(8,128)(2,1)S(1)} %shard_map.129.codes), custom_call_target="tpu_custom_call" | custom-call | flops 2147483648 | tf_op jit(solution)/shard_map/pallas_call | solution.py:84
  29.8 2.6 %collective-permute-done.5.refs_1_ = f32[16,2176]{1,0:T(8,128)S(1)} collective-permute-done((f32[16,2176]{1,0:T(8,128)S(1)}, f32[16,2176]{1,0:T(8,128)S(1)}, u32[]{:S(2)}, u32[]{:S(2)}) %collective-permute-start.5) | collective-permute-done | bytes 139296 | tf_op jit(solution)/shard_map/ppermute | solution.py:259
  32.8 1.9 %shard_map.135 = f32[8,2176]{1,0:T(8,128)S(1)} custom-call(f32[16,2176]{1,0:T(8,128)S(1)} %shard_map.133.sums, bf16[2048,2048]{1,0:T(8,128)(2,1)S(1)} %shard_map.134.flipped, s32[1,2048]{1,0:T(1,128)S(1)} %bitcast.6, f32[8,2048]{1,0:T(8,128)S(1)} %get-tuple-element.19.shuffled, f32[3]{0:T(128)S(1)} %copy-done.8), custom_call_target="tpu_custom_call" | custom-call | tf_op jit(solution)/shard_map/pallas_call | solution.py:183
  34.8 1.2 %collective-permute-done.8 = f32[8,2176]{1,0:T(8,128)S(1)} collective-permute-done((f32[8,2176]{1,0:T(8,128)S(1)}, f32[8,2176]{1,0:T(8,128)S(1)}, u32[]{:S(2)}, u32[]{:S(2)}) %collective-permute-start.8) | collective-permute-done | bytes 69664 | tf_op jit(solution)/shard_map/ppermute | solution.py:259
  36.0 1.7 %collective-permute-start.9 = (f32[8,2176]{1,0:T(8,128)S(1)}, f32[8,2176]{1,0:T(8,128)S(1)}, u32[]{:S(2)}, u32[]{:S(2)}) collective-permute-start(f32[8,2176]{1,0:T(8,128)S(1)} %add.13), channel_id=1, source_target_pairs={{0,2},{1,3},{2,0},{3,1},{4,6},{5,7},{6,4},{7,5},{8,10},{9,11},{10,... | collective-permute-start | bytes 208904 | tf_op jit(solution)/shard_map/ppermute | solution.py:259
  38.1 2.4 %collective-permute-done.9 = f32[8,2176]{1,0:T(8,128)S(1)} collective-permute-done((f32[8,2176]{1,0:T(8,128)S(1)}, f32[8,2176]{1,0:T(8,128)S(1)}, u32[]{:S(2)}, u32[]{:S(2)}) %collective-permute-start.9) | collective-permute-done | bytes 69664 | tf_op jit(solution)/shard_map/ppermute | solution.py:259
  40.5 1.0 %shard_map.137 = (f32[8,2048]{1,0:T(8,128)S(1)}, f32[8,2048]{1,0:T(8,128)S(1)}, f32[16,640]{1,0:T(8,128)S(1)}) custom-call(f32[8,2176]{1,0:T(8,128)S(1)} %add.14.applied, f32[16,2176]{1,0:T(8,128)S(1)} %shard_map.133.sums, f32[8,2048]{1,0:T(8,128)S(1)} %get-tuple-element.19.shuffled, f32[8,2048]{1,0:T(8,128)S(1)} %copy-done.1, f32[8,2048]{1,0:T(8,128)S(1)} %copy-done.2, ...), custom_call_target="tpu_custom_call" | custom-call | tf_op jit(solution)/shard_map/pallas_call | solution.py:215
  41.5 1.7 %collective-permute-start.10 = (f32[16,640]{1,0:T(8,128)S(1)}, f32[16,640]{1,0:T(8,128)S(1)}, u32[]{:S(2)}, u32[]{:S(2)}) collective-permute-start(f32[16,640]{1,0:T(8,128)S(1)} %get-tuple-element.23), channel_id=1, source_target_pairs={{0,4},{4,0},{8,12},{12,8},{16,20},{20,16},{24,28},{28,24},{1,5},{5... | collective-permute-start | bytes 122888 | tf_op jit(solution)/shard_map/ppermute | solution.py:259
  43.1 2.4 %collective-permute-done.10 = f32[16,640]{1,0:T(8,128)S(1)} collective-permute-done((f32[16,640]{1,0:T(8,128)S(1)}, f32[16,640]{1,0:T(8,128)S(1)}, u32[]{:S(2)}, u32[]{:S(2)}) %collective-permute-start.10) | collective-permute-done | bytes 40992 | tf_op jit(solution)/shard_map/ppermute | solution.py:259
  45.5 2.0 %collective-permute-start.11 = (f32[16,640]{1,0:T(8,128)S(1)}, f32[16,640]{1,0:T(8,128)S(1)}, u32[]{:S(2)}, u32[]{:S(2)}) collective-permute-start(f32[16,640]{1,0:T(8,128)S(1)} %add.15.refs_0_), channel_id=1, source_target_pairs={{0,24},{4,28},{8,16},{12,20},{16,8},{20,12},{24,0},{28,4},{1,25},{... | collective-permute-start | bytes 122888 | tf_op jit(solution)/shard_map/ppermute | solution.py:259
  47.5 0.7 %collective-permute-start.12 = (f32[16,640]{1,0:T(8,128)S(1)}, f32[16,640]{1,0:T(8,128)S(1)}, u32[]{:S(2)}, u32[]{:S(2)}) collective-permute-start(f32[16,640]{1,0:T(8,128)S(1)} %add.15.refs_0_), channel_id=1, source_target_pairs={{0,8},{4,12},{8,0},{12,4},{16,24},{20,28},{24,16},{28,20},{1,9},{5... | collective-permute-start | bytes 122888 | tf_op jit(solution)/shard_map/ppermute | solution.py:259
  48.2 1.7 %collective-permute-start.13 = (f32[16,640]{1,0:T(8,128)S(1)}, f32[16,640]{1,0:T(8,128)S(1)}, u32[]{:S(2)}, u32[]{:S(2)}) collective-permute-start(f32[16,640]{1,0:T(8,128)S(1)} %add.15.refs_0_), channel_id=1, source_target_pairs={{0,16},{4,20},{8,24},{12,28},{16,0},{20,4},{24,8},{28,12},{1,17},{... | collective-permute-start | bytes 122888 | tf_op jit(solution)/shard_map/ppermute | solution.py:259
  51.7 1.4 %collective-permute-done.13.refs_3_ = f32[16,640]{1,0:T(8,128)S(1)} collective-permute-done((f32[16,640]{1,0:T(8,128)S(1)}, f32[16,640]{1,0:T(8,128)S(1)}, u32[]{:S(2)}, u32[]{:S(2)}) %collective-permute-start.13) | collective-permute-done | bytes 40992 | tf_op jit(solution)/shard_map/ppermute | solution.py:259
  53.1 0.7 %shard_map.138 = (f32[8,2048]{1,0:T(8,128)}, f32[16,512]{1,0:T(8,128)}) custom-call(f32[16,2176]{1,0:T(8,128)S(1)} %shard_map.133.sums, f32[8,2048]{1,0:T(8,128)S(1)} %get-tuple-element.27.new_resid, f32[8,2048]{1,0:T(8,128)S(1)} %copy-done.1, f32[16,640]{1,0:T(8,128)S(1)} %add.15.refs_0_, f32[16,640]{1,0:T(8,128)S(1)} %collective-permute-done.11.refs_1_, ...), custom_call_target="tpu_custom_call" | custom-call | tf_op jit(solution)/shard_map/pallas_call | solution.py:238
  (47 shorter events, 3.5 us)
Async XLA Ops:
  0.6 9.8 %slice-start = ((s8[16777216]{0:T(1024)(128)(4,1)}), s8[4194304]{0:T(1024)(128)(4,1)S(1)}, s32[]{:S(2)}) async-start(s8[16777216]{0:T(1024)(128)(4,1)} %bitcast.3), calls=%async_computation | async-start | bytes 8388608
  0.7 9.8 %slice-start.1 = ((s8[16777216]{0:T(1024)(128)(4,1)}), s8[4194304]{0:T(1024)(128)(4,1)S(1)}, s32[]{:S(2)}) async-start(s8[16777216]{0:T(1024)(128)(4,1)} %bitcast.3), calls=%async_computation.1 | async-start | bytes 8388608
  0.7 9.8 %slice-start.2 = ((s8[16777216]{0:T(1024)(128)(4,1)}), s8[4194304]{0:T(1024)(128)(4,1)S(1)}, s32[]{:S(2)}) async-start(s8[16777216]{0:T(1024)(128)(4,1)} %bitcast.3), calls=%async_computation.2 | async-start | bytes 8388608
  0.7 9.7 %slice-start.3 = ((s8[16777216]{0:T(1024)(128)(4,1)}), s8[4194304]{0:T(1024)(128)(4,1)S(1)}, s32[]{:S(2)}) async-start(s8[16777216]{0:T(1024)(128)(4,1)} %bitcast.3), calls=%async_computation.3 | async-start | bytes 8388608
  0.7 4.9 %collective-permute-start = (f32[16,128]{1,0:T(8,128)}, f32[16,128]{1,0:T(8,128)S(1)}, u32[]{:S(2)}, u32[]{:S(2)}) collective-permute-start(f32[16,128]{1,0:T(8,128)} %bitcast.7), channel_id=1, source_target_pairs={{0,4},{4,0},{8,12},{12,8},{16,20},{20,16},{24,28},{28,24},{1,5},{5... | collective-permute-start | bytes 24584 | tf_op jit(solution)/shard_map/ppermute | solution.py:259
  5.6 8.8 %copy-start.1 = (f32[8,2048]{1,0:T(8,128)S(1)}, f32[8,2048]{1,0:T(8,128)}, u32[]{:S(2)}) copy-start(f32[8,2048]{1,0:T(8,128)} %direction.5) | copy-start | bytes 196612
  5.6 8.8 %copy-start.2 = (f32[8,2048]{1,0:T(8,128)S(1)}, f32[8,2048]{1,0:T(8,128)}, u32[]{:S(2)}) copy-start(f32[8,2048]{1,0:T(8,128)} %resid.3) | copy-start | bytes 196612
  5.6 8.8 %copy-start.3 = (s32[8,2048]{1,0:T(8,128)S(1)}, s32[8,2048]{1,0:T(8,128)}, u32[]{:S(2)}) copy-start(s32[8,2048]{1,0:T(8,128)} %perm.1) | copy-start | bytes 196612
  5.6 5.9 %collective-permute-start.1 = (f32[32,128]{1,0:T(8,128)S(1)}, f32[32,128]{1,0:T(8,128)S(1)}, u32[]{:S(2)}, u32[]{:S(2)}) collective-permute-start(f32[32,128]{1,0:T(8,128)S(1)} %shard_map.131.refs_0_), channel_id=1, source_target_pairs={{0,24},{4,28},{8,16},{12,20},{16,8},{20,12},{24,0},{28,4},{1,25},{... | collective-permute-start | bytes 49160 | tf_op jit(solution)/shard_map/ppermute | solution.py:259
  9.8 4.6 %collective-permute-start.2 = (f32[32,128]{1,0:T(8,128)S(1)}, f32[32,128]{1,0:T(8,128)S(1)}, u32[]{:S(2)}, u32[]{:S(2)}) collective-permute-start(f32[32,128]{1,0:T(8,128)S(1)} %shard_map.131.refs_0_), channel_id=1, source_target_pairs={{0,16},{4,20},{8,24},{12,28},{16,0},{20,4},{24,8},{28,12},{1,17},{... | collective-permute-start | bytes 49160 | tf_op jit(solution)/shard_map/ppermute | solution.py:259
  9.8 4.6 %collective-permute-start.3 = (f32[32,128]{1,0:T(8,128)S(1)}, f32[32,128]{1,0:T(8,128)S(1)}, u32[]{:S(2)}, u32[]{:S(2)}) collective-permute-start(f32[32,128]{1,0:T(8,128)S(1)} %shard_map.131.refs_0_), channel_id=1, source_target_pairs={{0,8},{4,12},{8,0},{12,4},{16,24},{20,28},{24,16},{28,20},{1,9},{5... | collective-permute-start | bytes 49160 | tf_op jit(solution)/shard_map/ppermute | solution.py:259
  17.6 5.1 %collective-permute-start.4 = (f32[16,2176]{1,0:T(8,128)S(1)}, f32[16,2176]{1,0:T(8,128)S(1)}, u32[]{:S(2)}, u32[]{:S(2)}) collective-permute-start(f32[16,2176]{1,0:T(8,128)S(1)} %get-tuple-element.16), channel_id=1, source_target_pairs={{0,4},{4,0},{8,12},{12,8},{16,20},{20,16},{24,28},{28,24},{1,5},{5... | collective-permute-start | bytes 417800 | tf_op jit(solution)/shard_map/ppermute | solution.py:259
  22.7 10.1 %copy-start.8 = (f32[3]{0:T(128)S(1)}, f32[3]{0:T(128)}, u32[]{:S(2)}) copy-start(f32[3]{0:T(128)} %var_comp.3) | copy-start | bytes 40
  22.7 9.6 %collective-permute-start.5 = (f32[16,2176]{1,0:T(8,128)S(1)}, f32[16,2176]{1,0:T(8,128)S(1)}, u32[]{:S(2)}, u32[]{:S(2)}) collective-permute-start(f32[16,2176]{1,0:T(8,128)S(1)} %add.12.refs_0_), channel_id=1, source_target_pairs={{0,16},{4,20},{8,24},{12,28},{16,0},{20,4},{24,8},{28,12},{1,17},{... | collective-permute-start | bytes 417800 | tf_op jit(solution)/shard_map/ppermute | solution.py:259
  24.8 8.0 %collective-permute-start.6 = (f32[16,2176]{1,0:T(8,128)S(1)}, f32[16,2176]{1,0:T(8,128)S(1)}, u32[]{:S(2)}, u32[]{:S(2)}) collective-permute-start(f32[16,2176]{1,0:T(8,128)S(1)} %add.12.refs_0_), channel_id=1, source_target_pairs={{0,8},{4,12},{8,0},{12,4},{16,24},{20,28},{24,16},{28,20},{1,9},{5... | collective-permute-start | bytes 417800 | tf_op jit(solution)/shard_map/ppermute | solution.py:259
  24.8 8.0 %collective-permute-start.7 = (f32[16,2176]{1,0:T(8,128)S(1)}, f32[16,2176]{1,0:T(8,128)S(1)}, u32[]{:S(2)}, u32[]{:S(2)}) collective-permute-start(f32[16,2176]{1,0:T(8,128)S(1)} %add.12.refs_0_), channel_id=1, source_target_pairs={{0,24},{4,28},{8,16},{12,20},{16,8},{20,12},{24,0},{28,4},{1,25},{... | collective-permute-start | bytes 417800 | tf_op jit(solution)/shard_map/ppermute | solution.py:259
  29.8 10.6 %copy-start.4 = (f32[8,2048]{1,0:T(8,128)S(1)}, f32[8,2048]{1,0:T(8,128)}, u32[]{:S(2)}) copy-start(f32[8,2048]{1,0:T(8,128)} %solution.1) | copy-start | bytes 196612
  29.8 10.6 %copy-start.7 = (s32[512]{0:T(512)S(1)}, s32[512]{0:T(512)}, u32[]{:S(2)}) copy-start(s32[512]{0:T(512)} %param.13) | copy-start | bytes 6148
  34.8 1.3 %collective-permute-start.8 = (f32[8,2176]{1,0:T(8,128)S(1)}, f32[8,2176]{1,0:T(8,128)S(1)}, u32[]{:S(2)}, u32[]{:S(2)}) collective-permute-start(f32[8,2176]{1,0:T(8,128)S(1)} %shard_map.135), channel_id=1, source_target_pairs={{0,1},{1,0},{2,3},{3,2},{4,5},{5,4},{6,7},{7,6},{8,9},{9,8},{10,11... | collective-permute-start | bytes 208904 | tf_op jit(solution)/shard_map/ppermute | solution.py:259
  36.0 4.4 %collective-permute-start.9 = (f32[8,2176]{1,0:T(8,128)S(1)}, f32[8,2176]{1,0:T(8,128)S(1)}, u32[]{:S(2)}, u32[]{:S(2)}) collective-permute-start(f32[8,2176]{1,0:T(8,128)S(1)} %add.13), channel_id=1, source_target_pairs={{0,2},{1,3},{2,0},{3,1},{4,6},{5,7},{6,4},{7,5},{8,10},{9,11},{10,... | collective-permute-start | bytes 208904 | tf_op jit(solution)/shard_map/ppermute | solution.py:259
  41.5 4.0 %collective-permute-start.10 = (f32[16,640]{1,0:T(8,128)S(1)}, f32[16,640]{1,0:T(8,128)S(1)}, u32[]{:S(2)}, u32[]{:S(2)}) collective-permute-start(f32[16,640]{1,0:T(8,128)S(1)} %get-tuple-element.23), channel_id=1, source_target_pairs={{0,4},{4,0},{8,12},{12,8},{16,20},{20,16},{24,28},{28,24},{1,5},{5... | collective-permute-start | bytes 122888 | tf_op jit(solution)/shard_map/ppermute | solution.py:259
  45.5 5.8 %collective-permute-start.11 = (f32[16,640]{1,0:T(8,128)S(1)}, f32[16,640]{1,0:T(8,128)S(1)}, u32[]{:S(2)}, u32[]{:S(2)}) collective-permute-start(f32[16,640]{1,0:T(8,128)S(1)} %add.15.refs_0_), channel_id=1, source_target_pairs={{0,24},{4,28},{8,16},{12,20},{16,8},{20,12},{24,0},{28,4},{1,25},{... | collective-permute-start | bytes 122888 | tf_op jit(solution)/shard_map/ppermute | solution.py:259
  47.5 4.2 %collective-permute-start.12 = (f32[16,640]{1,0:T(8,128)S(1)}, f32[16,640]{1,0:T(8,128)S(1)}, u32[]{:S(2)}, u32[]{:S(2)}) collective-permute-start(f32[16,640]{1,0:T(8,128)S(1)} %add.15.refs_0_), channel_id=1, source_target_pairs={{0,8},{4,12},{8,0},{12,4},{16,24},{20,28},{24,16},{28,20},{1,9},{5... | collective-permute-start | bytes 122888 | tf_op jit(solution)/shard_map/ppermute | solution.py:259
  48.2 4.9 %collective-permute-start.13 = (f32[16,640]{1,0:T(8,128)S(1)}, f32[16,640]{1,0:T(8,128)S(1)}, u32[]{:S(2)}, u32[]{:S(2)}) collective-permute-start(f32[16,640]{1,0:T(8,128)S(1)} %add.15.refs_0_), channel_id=1, source_target_pairs={{0,16},{4,20},{8,24},{12,28},{16,0},{20,4},{24,8},{28,12},{1,17},{... | collective-permute-start | bytes 122888 | tf_op jit(solution)/shard_map/ppermute | solution.py:259
  (3 other events, 21.7 us)

commit v7 on v6

--- a/solution.py
+++ b/solution.py
@@ -16,7 +16,7 @@
 SCALARS = pl.BlockSpec(memory_space=pltpu.SMEM)
 GATHER_ORDER = (3, 2, 1)
 SLAB_ORDER = (2, 1, 3)
-SCORE_ORDER = (3, 1, 2)
+SCORE_ORDER = (3, 2, 1)
 
 
 def in_vmem(shape, dtype=jnp.float32):
@@ -50,6 +50,18 @@
 def add_pieces(y):
     rows = y.shape[0] // 3
     return y[:rows] + y[rows : 2 * rows] + y[2 * rows :]
+
+
+def fold(x):
+    return jnp.concatenate(
+        [x[:, start : start + LANES] for start in range(0, x.shape[1], LANES)], axis=0
+    )
+
+
+def unfold(x, rows):
+    return jnp.concatenate(
+        [x[start : start + rows] for start in range(0, x.shape[0], rows)], axis=1
+    )
 
 
 def spread(pct):
@@ -133,7 +145,6 @@
 def slab_body(perm, direction, resid, codes, pct, *refs, axis):
     *table, shuffled, sums = refs
     rhs = direction.shape[0]
-    slab = codes.shape[1]
     table = jnp.concatenate([block[...] for block in by_distance(table, GATHER_ORDER)], axis=0)
     shard = table.size // lax.axis_size(axis)
     lookup(table, perm[...] ^ (lax.axis_index(axis) * shard), shuffled)
@@ -143,27 +154,26 @@
     product = add_pieces(
         jnp.dot(bf16_pieces(both), codes[...], preferred_element_type=jnp.float32)
     )
-    sums[:, :slab] = scale * (product - mean * jnp.sum(both, axis=1, keepdims=True))
+    sums[:-rhs, :] = fold(scale * (product - mean * jnp.sum(both, axis=1, keepdims=True)))
     left = resid[...]
     norm = jnp.sum(left * left, axis=1, keepdims=True)
     length = jnp.sum(straight * straight, axis=1, keepdims=True)
-    sums[:rhs, slab:] = jnp.broadcast_to(norm, (rhs, LANES))
-    sums[rhs:, slab:] = jnp.broadcast_to(length, (rhs, LANES))
+    lane = lax.broadcasted_iota(jnp.int32, (rhs, LANES), 1)
+    sums[-rhs:, :] = jnp.where(lane < LANES // 2, norm, length)
 
 
 def slab_sums(table, perm, direction, resid, codes, pct, axis):
     rhs, slab = direction.shape[0], codes.shape[1]
     return call(
         functools.partial(slab_body, axis=axis),
-        [in_vmem(perm.shape), in_vmem((2 * rhs, slab + LANES))],
+        [in_vmem(perm.shape), in_vmem((2 * rhs * slab // LANES + rhs, LANES))],
         [WHOLE] * (5 + len(table)),
     )(perm, direction, resid, codes, pct, *table)
 
 
 def kernel_body(sums, flipped, pct, shuffled, var_comp, out, *, slab_total):
     rhs, count = shuffled.shape
-    slab = flipped.shape[0]
-    weights = sums[:, :slab]
+    weights = unfold(sums[:-rhs, :], 2 * rhs)
     squares = jnp.sum(weights * weights, axis=1, keepdims=True)
     mean, scale = spread(pct[...])
     weights = scale * weights
@@ -190,12 +200,11 @@
 def step_body(applied, sums, shuffled, direction, resid, solution, codes, pct, empty, var_comp,
               new_solution, new_resid, scores, *, root):
     rhs, count = shuffled.shape
-    tests = codes.shape[1]
-    norms = sums[:, -LANES:]
+    norms = sums[-rhs:, :]
     straight = direction[...]
     image = var_comp[0] * straight + applied[:, :count]
-    curvature = var_comp[0] * norms[rhs:, :1] + applied[:, count : count + 1]
-    alpha = norms[:rhs, :1] / curvature
+    curvature = var_comp[0] * norms[:, LANES // 2 : LANES // 2 + 1] + applied[:, count : count + 1]
+    alpha = norms[:, :1] / curvature
     left = resid[...] - alpha * image
     new_resid[...] = left
     new_solution[...] = solution[...] + alpha * straight
@@ -204,10 +213,9 @@
     product = add_pieces(
         jnp.dot(bf16_pieces(both), codes[...], preferred_element_type=jnp.float32)
     )
-    scores[:, :tests] = (scale / root) * (product - mean * jnp.sum(both, axis=1, keepdims=True))
-    norm = jnp.sum(left * left, axis=1, keepdims=True)
-    scores[:rhs, tests:] = jnp.broadcast_to(norm, (rhs, LANES))
-    scores[rhs:, tests:] = empty[...]
+    product -= mean * jnp.sum(both, axis=1, keepdims=True)
+    scores[:-rhs, :] = fold((scale / root) * product)
+    scores[-rhs:, :] = empty[...] + jnp.sum(left * left, axis=1, keepdims=True)
 
 
 def step(applied, sums, shuffled, direction, resid, solution, codes, pct, empty, var_comp, root):
@@ -217,7 +225,7 @@
         [
             in_vmem((rhs, count)),
             in_vmem((rhs, count)),
-            in_vmem((2 * rhs, codes.shape[1] + LANES)),
+            in_vmem((2 * rhs * codes.shape[1] // LANES + rhs, LANES)),
         ],
         [WHOLE] * 9 + [SCALARS],
     )(applied, sums, shuffled, direction, resid, solution, codes, pct, empty, var_comp)
@@ -226,20 +234,20 @@
 def finish_body(sums, new_resid, direction, *refs):
     *parts, new_direction, scores = refs
     rhs = direction.shape[0]
-    tests = scores.shape[1]
     total = add_parts([part[...] for part in by_distance(parts, SCORE_ORDER)])
-    scores[...] = total[:, :tests]
-    ratio = total[:rhs, tests : tests + 1] / sums[:rhs, -LANES:][:, :1]
+    scores[...] = unfold(total[:-rhs], 2 * rhs)
+    ratio = total[-rhs:, :1] / sums[-rhs:, :1]
     new_direction[...] = new_resid[...] + ratio * direction[...]
 
 
 def finish(parts, sums, new_resid, direction):
-    rows, columns = parts[0].shape
+    rhs = direction.shape[0]
+    tests = (parts[0].shape[0] - rhs) // (2 * rhs) * LANES
     return call(
         finish_body,
         [
             jax.ShapeDtypeStruct(direction.shape, jnp.float32),
-            jax.ShapeDtypeStruct((rows, columns - LANES), jnp.float32),
+            jax.ShapeDtypeStruct((2 * rhs, tests), jnp.float32),
         ],
         [WHOLE] * (3 + len(parts)),
     )(sums, new_resid, direction, *parts)

time: 54 us -> 53.5 us (level)
  transfers between devices with their start and end apart: 14 -> 14, of which waited for: 12 -> 11; matrix products, arithmetic and copies ran while one was open for 2% -> 2% of each run, Pallas kernels for 7% -> 7%
where the time goes in v7:
time: 53.5 us; the launch traced here: 53.4 us
  starting transfers between devices  21.5 us (40%)
  waiting for transfers between devices  18.8 us (35%)
  Pallas kernels  11 us (21%)
  local copies, waits for them, and re-layouts  1.33 us (2%)
  between operations  0.84 us (2%)
    ppermute x14, starting transfers between devices, swap(): return lax.ppermute(x, axis, [(i, i ^ distance) for i in range(size)])  21.5 us
    ppermute x14, waiting for transfers between devices, swap(): return lax.ppermute(x, axis, [(i, i ^ distance) for i in range(size)])  18.8 us
    pallas_call x1, Pallas kernels, slab_sums(): call(functools.partial(slab_body, axis=axis), [in_vmem(perm.shape), in_vm...  3.18 us
    pallas_call x1, Pallas kernels, flip_codes(): call(functools.partial(flip_body, start=start), in_vmem((width, codes.sha...  2.59 us
    pallas_call x1, Pallas kernels, kernel_part(): call(functools.partial(kernel_body, slab_total=slab_total), in_vmem((rhs,...  1.96 us
    unnamed x28, local copies, waits for them, and re-layouts  1.33 us
    pallas_call x2, Pallas kernels, cast_codes(): return call(cast_body, in_vmem(geno.shape, jnp.bfloat16), [WHOLE])(geno)  1.31 us
    pallas_call x1, Pallas kernels, step(): call(functools.partial(step_body, root=root), [in_vmem((rhs, count)), in_...  1.16 us
  transfers between devices with their start and end apart: 14, of which 11 were waited for; matrix products, arithmetic and copies ran while one was open for 2% of the time, Pallas kernels for 7%

profile of v7, /device:TPU:0, one launch (start us, length us, event | category | flops | bytes accessed | tf_op | source)
XLA Modules:
  0.0 53.4 jit_solution(528600340892113764)
XLA Ops:
  0.7 3.0 %collective-permute-start = (f32[16,128]{1,0:T(8,128)}, f32[16,128]{1,0:T(8,128)S(1)}, u32[]{:S(2)}, u32[]{:S(2)}) collective-permute-start(f32[16,128]{1,0:T(8,128)} %bitcast.7), channel_id=1, source_target_pairs={{0,4},{4,0},{8,12},{12,8},{16,20},{20,16},{24,28},{28,24},{1,5},{5... | collective-permute-start | bytes 24584 | tf_op jit(solution)/shard_map/ppermute | solution.py:267
  3.7 1.8 %collective-permute-done.refs_1_ = f32[16,128]{1,0:T(8,128)S(1)} collective-permute-done((f32[16,128]{1,0:T(8,128)}, f32[16,128]{1,0:T(8,128)S(1)}, u32[]{:S(2)}, u32[]{:S(2)}) %collective-permute-start) | collective-permute-done | bytes 8224 | tf_op jit(solution)/shard_map/ppermute | solution.py:267
  5.6 4.2 %collective-permute-start.1 = (f32[32,128]{1,0:T(8,128)S(1)}, f32[32,128]{1,0:T(8,128)S(1)}, u32[]{:S(2)}, u32[]{:S(2)}) collective-permute-start(f32[32,128]{1,0:T(8,128)S(1)} %shard_map.131.refs_0_), channel_id=1, source_target_pairs={{0,24},{4,28},{8,16},{12,20},{16,8},{20,12},{24,0},{28,4},{1,25},{... | collective-permute-start | bytes 49160 | tf_op jit(solution)/shard_map/ppermute | solution.py:267
  10.4 1.0 %shard_map.129.codes = bf16[2048,2048]{1,0:T(8,128)(2,1)S(1)} custom-call(s32[2048,2048]{1,0:T(8,128)S(1)} %bitcast.4), custom_call_target="tpu_custom_call" | custom-call | tf_op jit(solution)/shard_map/pallas_call | solution.py:82
  11.5 2.9 %collective-permute-done.2.refs_2_ = f32[32,128]{1,0:T(8,128)S(1)} collective-permute-done((f32[32,128]{1,0:T(8,128)S(1)}, f32[32,128]{1,0:T(8,128)S(1)}, u32[]{:S(2)}, u32[]{:S(2)}) %collective-permute-start.2) | collective-permute-done | bytes 16416 | tf_op jit(solution)/shard_map/ppermute | solution.py:267
  14.4 3.2 %shard_map.132 = (f32[8,2048]{1,0:T(8,128)S(1)}, f32[264,128]{1,0:T(8,128)S(1)}) custom-call(s32[8,2048]{1,0:T(8,128)S(1)} %copy-done.3, f32[8,2048]{1,0:T(8,128)S(1)} %copy-done.1, f32[8,2048]{1,0:T(8,128)S(1)} %copy-done.2, bf16[2048,2048]{1,0:T(8,128)(2,1)S(1)} %shard_map.129.codes, s32[1,2048]{1,0:T(1,128)S(1)} %bitcast.5, ...), custom_call_target="tpu_custom_call" | custom-call | tf_op jit(solution)/shard_map/pallas_call | solution.py:167
  17.6 1.5 %collective-permute-start.4 = (f32[264,128]{1,0:T(8,128)S(1)}, f32[264,128]{1,0:T(8,128)S(1)}, u32[]{:S(2)}, u32[]{:S(2)}) collective-permute-start(f32[264,128]{1,0:T(8,128)S(1)} %get-tuple-element.16), channel_id=1, source_target_pairs={{0,4},{4,0},{8,12},{12,8},{16,20},{20,16},{24,28},{28,24},{1,5},{5... | collective-permute-start | bytes 405512 | tf_op jit(solution)/shard_map/ppermute | solution.py:267
  19.2 3.5 %collective-permute-done.4 = f32[264,128]{1,0:T(8,128)S(1)} collective-permute-done((f32[264,128]{1,0:T(8,128)S(1)}, f32[264,128]{1,0:T(8,128)S(1)}, u32[]{:S(2)}, u32[]{:S(2)}) %collective-permute-start.4) | collective-permute-done | bytes 135200 | tf_op jit(solution)/shard_map/ppermute | solution.py:267
  22.7 2.1 %collective-permute-start.5 = (f32[264,128]{1,0:T(8,128)S(1)}, f32[264,128]{1,0:T(8,128)S(1)}, u32[]{:S(2)}, u32[]{:S(2)}) collective-permute-start(f32[264,128]{1,0:T(8,128)S(1)} %add.12.refs_0_), channel_id=1, source_target_pairs={{0,16},{4,20},{8,24},{12,28},{16,0},{20,4},{24,8},{28,12},{1,17},{... | collective-permute-start | bytes 405512 | tf_op jit(solution)/shard_map/ppermute | solution.py:267
  24.8 2.4 %collective-permute-start.7 = (f32[264,128]{1,0:T(8,128)S(1)}, f32[264,128]{1,0:T(8,128)S(1)}, u32[]{:S(2)}, u32[]{:S(2)}) collective-permute-start(f32[264,128]{1,0:T(8,128)S(1)} %add.12.refs_0_), channel_id=1, source_target_pairs={{0,24},{4,28},{8,16},{12,20},{16,8},{20,12},{24,0},{28,4},{1,25},{... | collective-permute-start | bytes 405512 | tf_op jit(solution)/shard_map/ppermute | solution.py:267
  27.1 2.6 %shard_map.134.flipped = bf16[2048,2048]{1,0:T(8,128)(2,1)S(1)} custom-call(bf16[2048,2048]{1,0:T(8,128)(2,1)S(1)} %shard_map.129.codes), custom_call_target="tpu_custom_call" | custom-call | flops 2147483648 | tf_op jit(solution)/shard_map/pallas_call | solution.py:96
  29.8 2.3 %collective-permute-done.5.refs_1_ = f32[264,128]{1,0:T(8,128)S(1)} collective-permute-done((f32[264,128]{1,0:T(8,128)S(1)}, f32[264,128]{1,0:T(8,128)S(1)}, u32[]{:S(2)}, u32[]{:S(2)}) %collective-permute-start.5) | collective-permute-done | bytes 135200 | tf_op jit(solution)/shard_map/ppermute | solution.py:267
  32.6 2.0 %shard_map.135 = f32[8,2176]{1,0:T(8,128)S(1)} custom-call(f32[264,128]{1,0:T(8,128)S(1)} %shard_map.133.sums, bf16[2048,2048]{1,0:T(8,128)(2,1)S(1)} %shard_map.134.flipped, s32[1,2048]{1,0:T(1,128)S(1)} %bitcast.6, f32[8,2048]{1,0:T(8,128)S(1)} %get-tuple-element.19.shuffled, f32[3]{0:T(128)S(1)} %copy-done.8), custom_call_target="tpu_custom_call" | custom-call | tf_op jit(solution)/shard_map/pallas_call | solution.py:193
  34.6 1.2 %collective-permute-done.8 = f32[8,2176]{1,0:T(8,128)S(1)} collective-permute-done((f32[8,2176]{1,0:T(8,128)S(1)}, f32[8,2176]{1,0:T(8,128)S(1)}, u32[]{:S(2)}, u32[]{:S(2)}) %collective-permute-start.8) | collective-permute-done | bytes 69664 | tf_op jit(solution)/shard_map/ppermute | solution.py:267
  35.8 1.6 %collective-permute-start.9 = (f32[8,2176]{1,0:T(8,128)S(1)}, f32[8,2176]{1,0:T(8,128)S(1)}, u32[]{:S(2)}, u32[]{:S(2)}) collective-permute-start(f32[8,2176]{1,0:T(8,128)S(1)} %add.13), channel_id=1, source_target_pairs={{0,2},{1,3},{2,0},{3,1},{4,6},{5,7},{6,4},{7,5},{8,10},{9,11},{10,... | collective-permute-start | bytes 208904 | tf_op jit(solution)/shard_map/ppermute | solution.py:267
  37.8 2.4 %collective-permute-done.9 = f32[8,2176]{1,0:T(8,128)S(1)} collective-permute-done((f32[8,2176]{1,0:T(8,128)S(1)}, f32[8,2176]{1,0:T(8,128)S(1)}, u32[]{:S(2)}, u32[]{:S(2)}) %collective-permute-start.9) | collective-permute-done | bytes 69664 | tf_op jit(solution)/shard_map/ppermute | solution.py:267
  40.2 1.2 %shard_map.137 = (f32[8,2048]{1,0:T(8,128)S(1)}, f32[8,2048]{1,0:T(8,128)S(1)}, f32[72,128]{1,0:T(8,128)S(1)}) custom-call(f32[8,2176]{1,0:T(8,128)S(1)} %add.14.applied, f32[264,128]{1,0:T(8,128)S(1)} %shard_map.133.sums, f32[8,2048]{1,0:T(8,128)S(1)} %get-tuple-element.19.shuffled, f32[8,2048]{1,0:T(8,128)S(1)} %copy-done.1, f32[8,2048]{1,0:T(8,128)S(1)} %copy-done.2, ...), custom_call_target="tpu_custom_call" | custom-call | tf_op jit(solution)/shard_map/pallas_call | solution.py:223
  41.4 1.6 %collective-permute-start.10 = (f32[72,128]{1,0:T(8,128)S(1)}, f32[72,128]{1,0:T(8,128)S(1)}, u32[]{:S(2)}, u32[]{:S(2)}) collective-permute-start(f32[72,128]{1,0:T(8,128)S(1)} %get-tuple-element.23), channel_id=1, source_target_pairs={{0,4},{4,0},{8,12},{12,8},{16,20},{20,16},{24,28},{28,24},{1,5},{5... | collective-permute-start | bytes 110600 | tf_op jit(solution)/shard_map/ppermute | solution.py:267
  43.0 2.4 %collective-permute-done.10 = f32[72,128]{1,0:T(8,128)S(1)} collective-permute-done((f32[72,128]{1,0:T(8,128)S(1)}, f32[72,128]{1,0:T(8,128)S(1)}, u32[]{:S(2)}, u32[]{:S(2)}) %collective-permute-start.10) | collective-permute-done | bytes 36896 | tf_op jit(solution)/shard_map/ppermute | solution.py:267
  45.4 2.1 %collective-permute-start.11 = (f32[72,128]{1,0:T(8,128)S(1)}, f32[72,128]{1,0:T(8,128)S(1)}, u32[]{:S(2)}, u32[]{:S(2)}) collective-permute-start(f32[72,128]{1,0:T(8,128)S(1)} %add.15.refs_0_), channel_id=1, source_target_pairs={{0,24},{4,28},{8,16},{12,20},{16,8},{20,12},{24,0},{28,4},{1,25},{... | collective-permute-start | bytes 110600 | tf_op jit(solution)/shard_map/ppermute | solution.py:267
  47.5 0.9 %collective-permute-start.12 = (f32[72,128]{1,0:T(8,128)S(1)}, f32[72,128]{1,0:T(8,128)S(1)}, u32[]{:S(2)}, u32[]{:S(2)}) collective-permute-start(f32[72,128]{1,0:T(8,128)S(1)} %add.15.refs_0_), channel_id=1, source_target_pairs={{0,16},{4,20},{8,24},{12,28},{16,0},{20,4},{24,8},{28,12},{1,17},{... | collective-permute-start | bytes 110600 | tf_op jit(solution)/shard_map/ppermute | solution.py:267
  48.3 1.4 %collective-permute-start.13 = (f32[72,128]{1,0:T(8,128)S(1)}, f32[72,128]{1,0:T(8,128)S(1)}, u32[]{:S(2)}, u32[]{:S(2)}) collective-permute-start(f32[72,128]{1,0:T(8,128)S(1)} %add.15.refs_0_), channel_id=1, source_target_pairs={{0,8},{4,12},{8,0},{12,4},{16,24},{20,28},{24,16},{28,20},{1,9},{5... | collective-permute-start | bytes 110600 | tf_op jit(solution)/shard_map/ppermute | solution.py:267
  51.1 1.5 %collective-permute-done.12.refs_2_ = f32[72,128]{1,0:T(8,128)S(1)} collective-permute-done((f32[72,128]{1,0:T(8,128)S(1)}, f32[72,128]{1,0:T(8,128)S(1)}, u32[]{:S(2)}, u32[]{:S(2)}) %collective-permute-start.12) | collective-permute-done | bytes 36896 | tf_op jit(solution)/shard_map/ppermute | solution.py:267
  52.7 0.7 %shard_map.138 = (f32[8,2048]{1,0:T(8,128)}, f32[16,512]{1,0:T(8,128)}) custom-call(f32[264,128]{1,0:T(8,128)S(1)} %shard_map.133.sums, f32[8,2048]{1,0:T(8,128)S(1)} %get-tuple-element.27.new_resid, f32[8,2048]{1,0:T(8,128)S(1)} %copy-done.1, f32[72,128]{1,0:T(8,128)S(1)} %add.15.refs_0_, f32[72,128]{1,0:T(8,128)S(1)} %collective-permute-done.11.refs_1_, ...), custom_call_target="tpu_custom_call" | custom-call | tf_op jit(solution)/shard_map/pallas_call | solution.py:246
  (47 shorter events, 3.1 us)
Async XLA Ops:
  0.6 9.8 %slice-start = ((s8[16777216]{0:T(1024)(128)(4,1)}), s8[4194304]{0:T(1024)(128)(4,1)S(1)}, s32[]{:S(2)}) async-start(s8[16777216]{0:T(1024)(128)(4,1)} %bitcast.3), calls=%async_computation | async-start | bytes 8388608
  0.7 9.8 %slice-start.1 = ((s8[16777216]{0:T(1024)(128)(4,1)}), s8[4194304]{0:T(1024)(128)(4,1)S(1)}, s32[]{:S(2)}) async-start(s8[16777216]{0:T(1024)(128)(4,1)} %bitcast.3), calls=%async_computation.1 | async-start | bytes 8388608
  0.7 9.8 %slice-start.2 = ((s8[16777216]{0:T(1024)(128)(4,1)}), s8[4194304]{0:T(1024)(128)(4,1)S(1)}, s32[]{:S(2)}) async-start(s8[16777216]{0:T(1024)(128)(4,1)} %bitcast.3), calls=%async_computation.2 | async-start | bytes 8388608
  0.7 9.7 %slice-start.3 = ((s8[16777216]{0:T(1024)(128)(4,1)}), s8[4194304]{0:T(1024)(128)(4,1)S(1)}, s32[]{:S(2)}) async-start(s8[16777216]{0:T(1024)(128)(4,1)} %bitcast.3), calls=%async_computation.3 | async-start | bytes 8388608
  0.7 4.9 %collective-permute-start = (f32[16,128]{1,0:T(8,128)}, f32[16,128]{1,0:T(8,128)S(1)}, u32[]{:S(2)}, u32[]{:S(2)}) collective-permute-start(f32[16,128]{1,0:T(8,128)} %bitcast.7), channel_id=1, source_target_pairs={{0,4},{4,0},{8,12},{12,8},{16,20},{20,16},{24,28},{28,24},{1,5},{5... | collective-permute-start | bytes 24584 | tf_op jit(solution)/shard_map/ppermute | solution.py:267
  5.6 8.8 %copy-start.1 = (f32[8,2048]{1,0:T(8,128)S(1)}, f32[8,2048]{1,0:T(8,128)}, u32[]{:S(2)}) copy-start(f32[8,2048]{1,0:T(8,128)} %direction.5) | copy-start | bytes 196612
  5.6 8.8 %copy-start.2 = (f32[8,2048]{1,0:T(8,128)S(1)}, f32[8,2048]{1,0:T(8,128)}, u32[]{:S(2)}) copy-start(f32[8,2048]{1,0:T(8,128)} %resid.3) | copy-start | bytes 196612
  5.6 8.8 %copy-start.3 = (s32[8,2048]{1,0:T(8,128)S(1)}, s32[8,2048]{1,0:T(8,128)}, u32[]{:S(2)}) copy-start(s32[8,2048]{1,0:T(8,128)} %perm.1) | copy-start | bytes 196612
  5.6 5.9 %collective-permute-start.1 = (f32[32,128]{1,0:T(8,128)S(1)}, f32[32,128]{1,0:T(8,128)S(1)}, u32[]{:S(2)}, u32[]{:S(2)}) collective-permute-start(f32[32,128]{1,0:T(8,128)S(1)} %shard_map.131.refs_0_), channel_id=1, source_target_pairs={{0,24},{4,28},{8,16},{12,20},{16,8},{20,12},{24,0},{28,4},{1,25},{... | collective-permute-start | bytes 49160 | tf_op jit(solution)/shard_map/ppermute | solution.py:267
  9.8 4.6 %collective-permute-start.2 = (f32[32,128]{1,0:T(8,128)S(1)}, f32[32,128]{1,0:T(8,128)S(1)}, u32[]{:S(2)}, u32[]{:S(2)}) collective-permute-start(f32[32,128]{1,0:T(8,128)S(1)} %shard_map.131.refs_0_), channel_id=1, source_target_pairs={{0,16},{4,20},{8,24},{12,28},{16,0},{20,4},{24,8},{28,12},{1,17},{... | collective-permute-start | bytes 49160 | tf_op jit(solution)/shard_map/ppermute | solution.py:267
  9.8 4.6 %collective-permute-start.3 = (f32[32,128]{1,0:T(8,128)S(1)}, f32[32,128]{1,0:T(8,128)S(1)}, u32[]{:S(2)}, u32[]{:S(2)}) collective-permute-start(f32[32,128]{1,0:T(8,128)S(1)} %shard_map.131.refs_0_), channel_id=1, source_target_pairs={{0,8},{4,12},{8,0},{12,4},{16,24},{20,28},{24,16},{28,20},{1,9},{5... | collective-permute-start | bytes 49160 | tf_op jit(solution)/shard_map/ppermute | solution.py:267
  17.6 5.0 %collective-permute-start.4 = (f32[264,128]{1,0:T(8,128)S(1)}, f32[264,128]{1,0:T(8,128)S(1)}, u32[]{:S(2)}, u32[]{:S(2)}) collective-permute-start(f32[264,128]{1,0:T(8,128)S(1)} %get-tuple-element.16), channel_id=1, source_target_pairs={{0,4},{4,0},{8,12},{12,8},{16,20},{20,16},{24,28},{28,24},{1,5},{5... | collective-permute-start | bytes 405512 | tf_op jit(solution)/shard_map/ppermute | solution.py:267
  22.7 9.9 %copy-start.8 = (f32[3]{0:T(128)S(1)}, f32[3]{0:T(128)}, u32[]{:S(2)}) copy-start(f32[3]{0:T(128)} %var_comp.3) | copy-start | bytes 40
  22.7 9.4 %collective-permute-start.5 = (f32[264,128]{1,0:T(8,128)S(1)}, f32[264,128]{1,0:T(8,128)S(1)}, u32[]{:S(2)}, u32[]{:S(2)}) collective-permute-start(f32[264,128]{1,0:T(8,128)S(1)} %add.12.refs_0_), channel_id=1, source_target_pairs={{0,16},{4,20},{8,24},{12,28},{16,0},{20,4},{24,8},{28,12},{1,17},{... | collective-permute-start | bytes 405512 | tf_op jit(solution)/shard_map/ppermute | solution.py:267
  24.8 7.8 %collective-permute-start.6 = (f32[264,128]{1,0:T(8,128)S(1)}, f32[264,128]{1,0:T(8,128)S(1)}, u32[]{:S(2)}, u32[]{:S(2)}) collective-permute-start(f32[264,128]{1,0:T(8,128)S(1)} %add.12.refs_0_), channel_id=1, source_target_pairs={{0,8},{4,12},{8,0},{12,4},{16,24},{20,28},{24,16},{28,20},{1,9},{5... | collective-permute-start | bytes 405512 | tf_op jit(solution)/shard_map/ppermute | solution.py:267
  24.8 7.8 %collective-permute-start.7 = (f32[264,128]{1,0:T(8,128)S(1)}, f32[264,128]{1,0:T(8,128)S(1)}, u32[]{:S(2)}, u32[]{:S(2)}) collective-permute-start(f32[264,128]{1,0:T(8,128)S(1)} %add.12.refs_0_), channel_id=1, source_target_pairs={{0,24},{4,28},{8,16},{12,20},{16,8},{20,12},{24,0},{28,4},{1,25},{... | collective-permute-start | bytes 405512 | tf_op jit(solution)/shard_map/ppermute | solution.py:267
  29.7 10.5 %copy-start.4 = (f32[8,2048]{1,0:T(8,128)S(1)}, f32[8,2048]{1,0:T(8,128)}, u32[]{:S(2)}) copy-start(f32[8,2048]{1,0:T(8,128)} %solution.1) | copy-start | bytes 196612
  29.8 10.5 %copy-start.7 = (s32[512]{0:T(512)S(1)}, s32[512]{0:T(512)}, u32[]{:S(2)}) copy-start(s32[512]{0:T(512)} %param.13) | copy-start | bytes 6148
  34.5 1.3 %collective-permute-start.8 = (f32[8,2176]{1,0:T(8,128)S(1)}, f32[8,2176]{1,0:T(8,128)S(1)}, u32[]{:S(2)}, u32[]{:S(2)}) collective-permute-start(f32[8,2176]{1,0:T(8,128)S(1)} %shard_map.135), channel_id=1, source_target_pairs={{0,1},{1,0},{2,3},{3,2},{4,5},{5,4},{6,7},{7,6},{8,9},{9,8},{10,11... | collective-permute-start | bytes 208904 | tf_op jit(solution)/shard_map/ppermute | solution.py:267
  35.8 4.4 %collective-permute-start.9 = (f32[8,2176]{1,0:T(8,128)S(1)}, f32[8,2176]{1,0:T(8,128)S(1)}, u32[]{:S(2)}, u32[]{:S(2)}) collective-permute-start(f32[8,2176]{1,0:T(8,128)S(1)} %add.13), channel_id=1, source_target_pairs={{0,2},{1,3},{2,0},{3,1},{4,6},{5,7},{6,4},{7,5},{8,10},{9,11},{10,... | collective-permute-start | bytes 208904 | tf_op jit(solution)/shard_map/ppermute | solution.py:267
  41.4 4.0 %collective-permute-start.10 = (f32[72,128]{1,0:T(8,128)S(1)}, f32[72,128]{1,0:T(8,128)S(1)}, u32[]{:S(2)}, u32[]{:S(2)}) collective-permute-start(f32[72,128]{1,0:T(8,128)S(1)} %get-tuple-element.23), channel_id=1, source_target_pairs={{0,4},{4,0},{8,12},{12,8},{16,20},{20,16},{24,28},{28,24},{1,5},{5... | collective-permute-start | bytes 110600 | tf_op jit(solution)/shard_map/ppermute | solution.py:267
  45.4 5.8 %collective-permute-start.11 = (f32[72,128]{1,0:T(8,128)S(1)}, f32[72,128]{1,0:T(8,128)S(1)}, u32[]{:S(2)}, u32[]{:S(2)}) collective-permute-start(f32[72,128]{1,0:T(8,128)S(1)} %add.15.refs_0_), channel_id=1, source_target_pairs={{0,24},{4,28},{8,16},{12,20},{16,8},{20,12},{24,0},{28,4},{1,25},{... | collective-permute-start | bytes 110600 | tf_op jit(solution)/shard_map/ppermute | solution.py:267
  47.5 5.2 %collective-permute-start.12 = (f32[72,128]{1,0:T(8,128)S(1)}, f32[72,128]{1,0:T(8,128)S(1)}, u32[]{:S(2)}, u32[]{:S(2)}) collective-permute-start(f32[72,128]{1,0:T(8,128)S(1)} %add.15.refs_0_), channel_id=1, source_target_pairs={{0,16},{4,20},{8,24},{12,28},{16,0},{20,4},{24,8},{28,12},{1,17},{... | collective-permute-start | bytes 110600 | tf_op jit(solution)/shard_map/ppermute | solution.py:267
  48.3 4.4 %collective-permute-start.13 = (f32[72,128]{1,0:T(8,128)S(1)}, f32[72,128]{1,0:T(8,128)S(1)}, u32[]{:S(2)}, u32[]{:S(2)}) collective-permute-start(f32[72,128]{1,0:T(8,128)S(1)} %add.15.refs_0_), channel_id=1, source_target_pairs={{0,8},{4,12},{8,0},{12,4},{16,24},{20,28},{24,16},{28,20},{1,9},{5... | collective-permute-start | bytes 110600 | tf_op jit(solution)/shard_map/ppermute | solution.py:267
  (3 other events, 21.5 us)

commit v8 on v7

--- a/solution.py
+++ b/solution.py
@@ -52,10 +52,10 @@
     return y[:rows] + y[rows : 2 * rows] + y[2 * rows :]
 
 
-def fold(x):
-    return jnp.concatenate(
-        [x[:, start : start + LANES] for start in range(0, x.shape[1], LANES)], axis=0
-    )
+def fold(x, out):
+    rows = x.shape[0]
+    for block in range(x.shape[1] // LANES):
+        out[block * rows : (block + 1) * rows, :] = x[:, block * LANES : (block + 1) * LANES]
 
 
 def unfold(x, rows):
@@ -154,7 +154,7 @@
     product = add_pieces(
         jnp.dot(bf16_pieces(both), codes[...], preferred_element_type=jnp.float32)
     )
-    sums[:-rhs, :] = fold(scale * (product - mean * jnp.sum(both, axis=1, keepdims=True)))
+    fold(scale * (product - mean * jnp.sum(both, axis=1, keepdims=True)), sums)
     left = resid[...]
     norm = jnp.sum(left * left, axis=1, keepdims=True)
     length = jnp.sum(straight * straight, axis=1, keepdims=True)
@@ -171,7 +171,7 @@
     )(perm, direction, resid, codes, pct, *table)
 
 
-def kernel_body(sums, flipped, pct, shuffled, var_comp, out, *, slab_total):
+def kernel_body(sums, flipped, pct, shuffled, var_comp, out, norms, *, slab_total):
     rhs, count = shuffled.shape
     weights = unfold(sums[:-rhs, :], 2 * rhs)
     squares = jnp.sum(weights * weights, axis=1, keepdims=True)
@@ -186,25 +186,27 @@
     ) * share
     energy = (var_comp[1] * squares[:rhs] + var_comp[2] * squares[rhs:]) * share
     out[:, count:] = jnp.broadcast_to(energy, (rhs, LANES))
+    half = LANES // 2
+    norms[:rhs, :] = jnp.broadcast_to(sums[-rhs:, :][:, :1], (rhs, LANES))
+    norms[rhs:, :] = jnp.broadcast_to(sums[-rhs:, :][:, half : half + 1], (rhs, LANES))
 
 
 def kernel_part(sums, flipped, pct, shuffled, var_comp, slab_total):
     rhs, count = shuffled.shape
     return call(
         functools.partial(kernel_body, slab_total=slab_total),
-        in_vmem((rhs, count + LANES)),
+        [in_vmem((rhs, count + LANES)), in_vmem((2 * rhs, LANES))],
         [WHOLE] * 4 + [SCALARS],
     )(sums, flipped, pct, shuffled, var_comp)
 
 
-def step_body(applied, sums, shuffled, direction, resid, solution, codes, pct, empty, var_comp,
+def step_body(applied, norms, shuffled, direction, resid, solution, codes, pct, empty, var_comp,
               new_solution, new_resid, scores, *, root):
     rhs, count = shuffled.shape
-    norms = sums[-rhs:, :]
     straight = direction[...]
     image = var_comp[0] * straight + applied[:, :count]
-    curvature = var_comp[0] * norms[:, LANES // 2 : LANES // 2 + 1] + applied[:, count : count + 1]
-    alpha = norms[:, :1] / curvature
+    curvature = var_comp[0] * norms[rhs:, :1] + applied[:, count : count + 1]
+    alpha = norms[:rhs, :1] / curvature
     left = resid[...] - alpha * image
     new_resid[...] = left
     new_solution[...] = solution[...] + alpha * straight
@@ -214,11 +216,11 @@
         jnp.dot(bf16_pieces(both), codes[...], preferred_element_type=jnp.float32)
     )
     product -= mean * jnp.sum(both, axis=1, keepdims=True)
-    scores[:-rhs, :] = fold((scale / root) * product)
+    fold((scale / root) * product, scores)
     scores[-rhs:, :] = empty[...] + jnp.sum(left * left, axis=1, keepdims=True)
 
 
-def step(applied, sums, shuffled, direction, resid, solution, codes, pct, empty, var_comp, root):
+def step(applied, norms, shuffled, direction, resid, solution, codes, pct, empty, var_comp, root):
     rhs, count = shuffled.shape
     return call(
         functools.partial(step_body, root=root),
@@ -228,19 +230,19 @@
             in_vmem((2 * rhs * codes.shape[1] // LANES + rhs, LANES)),
         ],
         [WHOLE] * 9 + [SCALARS],
-    )(applied, sums, shuffled, direction, resid, solution, codes, pct, empty, var_comp)
-
-
-def finish_body(sums, new_resid, direction, *refs):
+    )(applied, norms, shuffled, direction, resid, solution, codes, pct, empty, var_comp)
+
+
+def finish_body(norms, new_resid, direction, *refs):
     *parts, new_direction, scores = refs
     rhs = direction.shape[0]
     total = add_parts([part[...] for part in by_distance(parts, SCORE_ORDER)])
     scores[...] = unfold(total[:-rhs], 2 * rhs)
-    ratio = total[-rhs:, :1] / sums[-rhs:, :1]
+    ratio = total[-rhs:, :1] / norms[:rhs, :1]
     new_direction[...] = new_resid[...] + ratio * direction[...]
 
 
-def finish(parts, sums, new_resid, direction):
+def finish(parts, norms, new_resid, direction):
     rhs = direction.shape[0]
     tests = (parts[0].shape[0] - rhs) // (2 * rhs) * LANES
     return call(
@@ -250,7 +252,7 @@
             jax.ShapeDtypeStruct((2 * rhs, tests), jnp.float32),
         ],
         [WHOLE] * (3 + len(parts)),
-    )(sums, new_resid, direction, *parts)
+    )(norms, new_resid, direction, *parts)
 
 
 def add_body(*refs):
@@ -335,15 +337,15 @@
     flipped = flip_codes(codes, 0, slab)
     parts = sum_parts(sums, "samp", pairs_then_fours, SLAB_ORDER, 2)
     sums = add_up(parts)
-    applied = kernel_part(sums, flipped, pct, shuffled, var_comp, slab_total)
+    applied, norms = kernel_part(sums, flipped, pct, shuffled, var_comp, slab_total)
     applied = sum_all(applied, "var", pairs)
     test_codes = cast_codes(test_geno)
     new_solution, new_resid, scores = step(
-        applied, sums, shuffled, direction, resid, solution, test_codes,
+        applied, norms, shuffled, direction, resid, solution, test_codes,
         test_pct.reshape(1, tests), empty, var_comp, root,
     )
     parts = sum_parts(scores, "samp", pairs_then_fours, SCORE_ORDER)
-    new_direction, scores = finish(parts, sums, new_resid, direction)
+    new_direction, scores = finish(parts, norms, new_resid, direction)
     return (new_solution, new_resid, new_direction, scores)
 
 

time: 53.5 us -> 53.4 us (level)
  no operation moved by 1% of the time
where the time goes in v8:
time: 53.4 us; the launch traced here: 53.3 us
  starting transfers between devices  21.6 us (40%)
  waiting for transfers between devices  18.7 us (35%)
  Pallas kernels  10.8 us (20%)
  local copies, waits for them, and re-layouts  1.33 us (2%)
  between operations  0.84 us (2%)
    ppermute x14, starting transfers between devices, swap(): return lax.ppermute(x, axis, [(i, i ^ distance) for i in range(size)])  21.6 us
    ppermute x14, waiting for transfers between devices, swap(): return lax.ppermute(x, axis, [(i, i ^ distance) for i in range(size)])  18.7 us
    pallas_call x1, Pallas kernels, slab_sums(): call(functools.partial(slab_body, axis=axis), [in_vmem(perm.shape), in_vm...  3.18 us
    pallas_call x1, Pallas kernels, flip_codes(): call(functools.partial(flip_body, start=start), in_vmem((width, codes.sha...  2.59 us
    pallas_call x1, Pallas kernels, kernel_part(): call(functools.partial(kernel_body, slab_total=slab_total), [in_vmem((rhs...  1.94 us
    unnamed x28, local copies, waits for them, and re-layouts  1.33 us
    pallas_call x2, Pallas kernels, cast_codes(): return call(cast_body, in_vmem(geno.shape, jnp.bfloat16), [WHOLE])(geno)  1.31 us
  transfers between devices with their start and end apart: 14, of which 11 were waited for; matrix products, arithmetic and copies ran while one was open for 2% of the time, Pallas kernels for 7%

profile of v8, /device:TPU:0, one launch (start us, length us, event | category | flops | bytes accessed | tf_op | source)
XLA Modules:
  0.0 53.3 jit_solution(7094065192515459060)
XLA Ops:
  0.7 3.0 %collective-permute-start = (f32[16,128]{1,0:T(8,128)}, f32[16,128]{1,0:T(8,128)S(1)}, u32[]{:S(2)}, u32[]{:S(2)}) collective-permute-start(f32[16,128]{1,0:T(8,128)} %bitcast.7), channel_id=1, source_target_pairs={{0,4},{4,0},{8,12},{12,8},{16,20},{20,16},{24,28},{28,24},{1,5},{5... | collective-permute-start | bytes 24584 | tf_op jit(solution)/shard_map/ppermute | solution.py:269
  3.7 1.8 %collective-permute-done.refs_1_ = f32[16,128]{1,0:T(8,128)S(1)} collective-permute-done((f32[16,128]{1,0:T(8,128)}, f32[16,128]{1,0:T(8,128)S(1)}, u32[]{:S(2)}, u32[]{:S(2)}) %collective-permute-start) | collective-permute-done | bytes 8224 | tf_op jit(solution)/shard_map/ppermute | solution.py:269
  5.6 4.2 %collective-permute-start.1 = (f32[32,128]{1,0:T(8,128)S(1)}, f32[32,128]{1,0:T(8,128)S(1)}, u32[]{:S(2)}, u32[]{:S(2)}) collective-permute-start(f32[32,128]{1,0:T(8,128)S(1)} %shard_map.131.refs_0_), channel_id=1, source_target_pairs={{0,24},{4,28},{8,16},{12,20},{16,8},{20,12},{24,0},{28,4},{1,25},{... | collective-permute-start | bytes 49160 | tf_op jit(solution)/shard_map/ppermute | solution.py:269
  10.4 1.0 %shard_map.129.codes = bf16[2048,2048]{1,0:T(8,128)(2,1)S(1)} custom-call(s32[2048,2048]{1,0:T(8,128)S(1)} %bitcast.4), custom_call_target="tpu_custom_call" | custom-call | tf_op jit(solution)/shard_map/pallas_call | solution.py:82
  11.5 2.9 %collective-permute-done.2.refs_2_ = f32[32,128]{1,0:T(8,128)S(1)} collective-permute-done((f32[32,128]{1,0:T(8,128)S(1)}, f32[32,128]{1,0:T(8,128)S(1)}, u32[]{:S(2)}, u32[]{:S(2)}) %collective-permute-start.2) | collective-permute-done | bytes 16416 | tf_op jit(solution)/shard_map/ppermute | solution.py:269
  14.4 3.2 %shard_map.132 = (f32[8,2048]{1,0:T(8,128)S(1)}, f32[264,128]{1,0:T(8,128)S(1)}) custom-call(s32[8,2048]{1,0:T(8,128)S(1)} %copy-done.3, f32[8,2048]{1,0:T(8,128)S(1)} %copy-done.1, f32[8,2048]{1,0:T(8,128)S(1)} %copy-done.2, bf16[2048,2048]{1,0:T(8,128)(2,1)S(1)} %shard_map.129.codes, s32[1,2048]{1,0:T(1,128)S(1)} %bitcast.5, ...), custom_call_target="tpu_custom_call" | custom-call | tf_op jit(solution)/shard_map/pallas_call | solution.py:167
  17.6 1.5 %collective-permute-start.4 = (f32[264,128]{1,0:T(8,128)S(1)}, f32[264,128]{1,0:T(8,128)S(1)}, u32[]{:S(2)}, u32[]{:S(2)}) collective-permute-start(f32[264,128]{1,0:T(8,128)S(1)} %get-tuple-element.18), channel_id=1, source_target_pairs={{0,4},{4,0},{8,12},{12,8},{16,20},{20,16},{24,28},{28,24},{1,5},{5... | collective-permute-start | bytes 405512 | tf_op jit(solution)/shard_map/ppermute | solution.py:269
  19.2 3.5 %collective-permute-done.4 = f32[264,128]{1,0:T(8,128)S(1)} collective-permute-done((f32[264,128]{1,0:T(8,128)S(1)}, f32[264,128]{1,0:T(8,128)S(1)}, u32[]{:S(2)}, u32[]{:S(2)}) %collective-permute-start.4) | collective-permute-done | bytes 135200 | tf_op jit(solution)/shard_map/ppermute | solution.py:269
  22.7 2.1 %collective-permute-start.5 = (f32[264,128]{1,0:T(8,128)S(1)}, f32[264,128]{1,0:T(8,128)S(1)}, u32[]{:S(2)}, u32[]{:S(2)}) collective-permute-start(f32[264,128]{1,0:T(8,128)S(1)} %add.12.refs_0_), channel_id=1, source_target_pairs={{0,16},{4,20},{8,24},{12,28},{16,0},{20,4},{24,8},{28,12},{1,17},{... | collective-permute-start | bytes 405512 | tf_op jit(solution)/shard_map/ppermute | solution.py:269
  24.8 2.4 %collective-permute-start.7 = (f32[264,128]{1,0:T(8,128)S(1)}, f32[264,128]{1,0:T(8,128)S(1)}, u32[]{:S(2)}, u32[]{:S(2)}) collective-permute-start(f32[264,128]{1,0:T(8,128)S(1)} %add.12.refs_0_), channel_id=1, source_target_pairs={{0,24},{4,28},{8,16},{12,20},{16,8},{20,12},{24,0},{28,4},{1,25},{... | collective-permute-start | bytes 405512 | tf_op jit(solution)/shard_map/ppermute | solution.py:269
  27.1 2.6 %shard_map.134.flipped = bf16[2048,2048]{1,0:T(8,128)(2,1)S(1)} custom-call(bf16[2048,2048]{1,0:T(8,128)(2,1)S(1)} %shard_map.129.codes), custom_call_target="tpu_custom_call" | custom-call | flops 2147483648 | tf_op jit(solution)/shard_map/pallas_call | solution.py:96
  29.8 2.3 %collective-permute-done.5.refs_1_ = f32[264,128]{1,0:T(8,128)S(1)} collective-permute-done((f32[264,128]{1,0:T(8,128)S(1)}, f32[264,128]{1,0:T(8,128)S(1)}, u32[]{:S(2)}, u32[]{:S(2)}) %collective-permute-start.5) | collective-permute-done | bytes 135200 | tf_op jit(solution)/shard_map/ppermute | solution.py:269
  32.6 1.9 %shard_map.135 = (f32[8,2176]{1,0:T(8,128)S(1)}, f32[16,128]{1,0:T(8,128)S(1)}) custom-call(f32[264,128]{1,0:T(8,128)S(1)} %shard_map.133.sums, bf16[2048,2048]{1,0:T(8,128)(2,1)S(1)} %shard_map.134.flipped, s32[1,2048]{1,0:T(1,128)S(1)} %bitcast.6, f32[8,2048]{1,0:T(8,128)S(1)} %get-tuple-element.21.shuffled, f32[3]{0:T(128)S(1)} %copy-done.8), custom_call_target="tpu_custom_call" | custom-call | tf_op jit(solution)/shard_map/pallas_call | solution.py:196
  34.5 1.2 %collective-permute-done.8 = f32[8,2176]{1,0:T(8,128)S(1)} collective-permute-done((f32[8,2176]{1,0:T(8,128)S(1)}, f32[8,2176]{1,0:T(8,128)S(1)}, u32[]{:S(2)}, u32[]{:S(2)}) %collective-permute-start.8) | collective-permute-done | bytes 69664 | tf_op jit(solution)/shard_map/ppermute | solution.py:269
  35.8 1.7 %collective-permute-start.9 = (f32[8,2176]{1,0:T(8,128)S(1)}, f32[8,2176]{1,0:T(8,128)S(1)}, u32[]{:S(2)}, u32[]{:S(2)}) collective-permute-start(f32[8,2176]{1,0:T(8,128)S(1)} %add.13), channel_id=1, source_target_pairs={{0,2},{1,3},{2,0},{3,1},{4,6},{5,7},{6,4},{7,5},{8,10},{9,11},{10,... | collective-permute-start | bytes 208904 | tf_op jit(solution)/shard_map/ppermute | solution.py:269
  37.8 2.4 %collective-permute-done.9 = f32[8,2176]{1,0:T(8,128)S(1)} collective-permute-done((f32[8,2176]{1,0:T(8,128)S(1)}, f32[8,2176]{1,0:T(8,128)S(1)}, u32[]{:S(2)}, u32[]{:S(2)}) %collective-permute-start.9) | collective-permute-done | bytes 69664 | tf_op jit(solution)/shard_map/ppermute | solution.py:269
  40.2 1.0 %shard_map.137 = (f32[8,2048]{1,0:T(8,128)S(1)}, f32[8,2048]{1,0:T(8,128)S(1)}, f32[72,128]{1,0:T(8,128)S(1)}) custom-call(f32[8,2176]{1,0:T(8,128)S(1)} %add.14.applied, f32[16,128]{1,0:T(8,128)S(1)} %get-tuple-element.23.norms, f32[8,2048]{1,0:T(8,128)S(1)} %get-tuple-element.21.shuffled, f32[8,2048]{1,0:T(8,128)S(1)} %copy-done.1, ...), custom_call_target="tpu_custom_call" | custom-call | tf_op jit(solution)/shard_map/pallas_call | solution.py:225
  41.2 1.7 %collective-permute-start.10 = (f32[72,128]{1,0:T(8,128)S(1)}, f32[72,128]{1,0:T(8,128)S(1)}, u32[]{:S(2)}, u32[]{:S(2)}) collective-permute-start(f32[72,128]{1,0:T(8,128)S(1)} %get-tuple-element.27), channel_id=1, source_target_pairs={{0,4},{4,0},{8,12},{12,8},{16,20},{20,16},{24,28},{28,24},{1,5},{5... | collective-permute-start | bytes 110600 | tf_op jit(solution)/shard_map/ppermute | solution.py:269
  42.9 2.3 %collective-permute-done.10 = f32[72,128]{1,0:T(8,128)S(1)} collective-permute-done((f32[72,128]{1,0:T(8,128)S(1)}, f32[72,128]{1,0:T(8,128)S(1)}, u32[]{:S(2)}, u32[]{:S(2)}) %collective-permute-start.10) | collective-permute-done | bytes 36896 | tf_op jit(solution)/shard_map/ppermute | solution.py:269
  45.2 2.1 %collective-permute-start.11 = (f32[72,128]{1,0:T(8,128)S(1)}, f32[72,128]{1,0:T(8,128)S(1)}, u32[]{:S(2)}, u32[]{:S(2)}) collective-permute-start(f32[72,128]{1,0:T(8,128)S(1)} %add.15.refs_0_), channel_id=1, source_target_pairs={{0,24},{4,28},{8,16},{12,20},{16,8},{20,12},{24,0},{28,4},{1,25},{... | collective-permute-start | bytes 110600 | tf_op jit(solution)/shard_map/ppermute | solution.py:269
  47.4 0.8 %collective-permute-start.12 = (f32[72,128]{1,0:T(8,128)S(1)}, f32[72,128]{1,0:T(8,128)S(1)}, u32[]{:S(2)}, u32[]{:S(2)}) collective-permute-start(f32[72,128]{1,0:T(8,128)S(1)} %add.15.refs_0_), channel_id=1, source_target_pairs={{0,16},{4,20},{8,24},{12,28},{16,0},{20,4},{24,8},{28,12},{1,17},{... | collective-permute-start | bytes 110600 | tf_op jit(solution)/shard_map/ppermute | solution.py:269
  48.2 1.4 %collective-permute-start.13 = (f32[72,128]{1,0:T(8,128)S(1)}, f32[72,128]{1,0:T(8,128)S(1)}, u32[]{:S(2)}, u32[]{:S(2)}) collective-permute-start(f32[72,128]{1,0:T(8,128)S(1)} %add.15.refs_0_), channel_id=1, source_target_pairs={{0,8},{4,12},{8,0},{12,4},{16,24},{20,28},{24,16},{28,20},{1,9},{5... | collective-permute-start | bytes 110600 | tf_op jit(solution)/shard_map/ppermute | solution.py:269
  51.0 1.6 %collective-permute-done.12.refs_2_ = f32[72,128]{1,0:T(8,128)S(1)} collective-permute-done((f32[72,128]{1,0:T(8,128)S(1)}, f32[72,128]{1,0:T(8,128)S(1)}, u32[]{:S(2)}, u32[]{:S(2)}) %collective-permute-start.12) | collective-permute-done | bytes 36896 | tf_op jit(solution)/shard_map/ppermute | solution.py:269
  52.6 0.7 %shard_map.138 = (f32[8,2048]{1,0:T(8,128)}, f32[16,512]{1,0:T(8,128)}) custom-call(f32[16,128]{1,0:T(8,128)S(1)} %get-tuple-element.23.norms, f32[8,2048]{1,0:T(8,128)S(1)} %get-tuple-element.31.new_resid, f32[8,2048]{1,0:T(8,128)S(1)} %copy-done.1, f32[72,128]{1,0:T(8,128)S(1)} %add.15.refs_0_, f32[72,128]{1,0:T(8,128)S(1)} %collective-permute-done.11.refs_1_, ...), custom_call_target="tpu_custom_call" | custom-call | tf_op jit(solution)/shard_map/pallas_call | solution.py:248
  (47 shorter events, 3.1 us)
Async XLA Ops:
  0.6 9.8 %slice-start = ((s8[16777216]{0:T(1024)(128)(4,1)}), s8[4194304]{0:T(1024)(128)(4,1)S(1)}, s32[]{:S(2)}) async-start(s8[16777216]{0:T(1024)(128)(4,1)} %bitcast.3), calls=%async_computation | async-start | bytes 8388608
  0.7 9.8 %slice-start.1 = ((s8[16777216]{0:T(1024)(128)(4,1)}), s8[4194304]{0:T(1024)(128)(4,1)S(1)}, s32[]{:S(2)}) async-start(s8[16777216]{0:T(1024)(128)(4,1)} %bitcast.3), calls=%async_computation.1 | async-start | bytes 8388608
  0.7 9.8 %slice-start.2 = ((s8[16777216]{0:T(1024)(128)(4,1)}), s8[4194304]{0:T(1024)(128)(4,1)S(1)}, s32[]{:S(2)}) async-start(s8[16777216]{0:T(1024)(128)(4,1)} %bitcast.3), calls=%async_computation.2 | async-start | bytes 8388608
  0.7 9.7 %slice-start.3 = ((s8[16777216]{0:T(1024)(128)(4,1)}), s8[4194304]{0:T(1024)(128)(4,1)S(1)}, s32[]{:S(2)}) async-start(s8[16777216]{0:T(1024)(128)(4,1)} %bitcast.3), calls=%async_computation.3 | async-start | bytes 8388608
  0.7 4.9 %collective-permute-start = (f32[16,128]{1,0:T(8,128)}, f32[16,128]{1,0:T(8,128)S(1)}, u32[]{:S(2)}, u32[]{:S(2)}) collective-permute-start(f32[16,128]{1,0:T(8,128)} %bitcast.7), channel_id=1, source_target_pairs={{0,4},{4,0},{8,12},{12,8},{16,20},{20,16},{24,28},{28,24},{1,5},{5... | collective-permute-start | bytes 24584 | tf_op jit(solution)/shard_map/ppermute | solution.py:269
  5.6 8.8 %copy-start.1 = (f32[8,2048]{1,0:T(8,128)S(1)}, f32[8,2048]{1,0:T(8,128)}, u32[]{:S(2)}) copy-start(f32[8,2048]{1,0:T(8,128)} %direction.5) | copy-start | bytes 196612
  5.6 8.8 %copy-start.2 = (f32[8,2048]{1,0:T(8,128)S(1)}, f32[8,2048]{1,0:T(8,128)}, u32[]{:S(2)}) copy-start(f32[8,2048]{1,0:T(8,128)} %resid.3) | copy-start | bytes 196612
  5.6 8.8 %copy-start.3 = (s32[8,2048]{1,0:T(8,128)S(1)}, s32[8,2048]{1,0:T(8,128)}, u32[]{:S(2)}) copy-start(s32[8,2048]{1,0:T(8,128)} %perm.1) | copy-start | bytes 196612
  5.6 5.9 %collective-permute-start.1 = (f32[32,128]{1,0:T(8,128)S(1)}, f32[32,128]{1,0:T(8,128)S(1)}, u32[]{:S(2)}, u32[]{:S(2)}) collective-permute-start(f32[32,128]{1,0:T(8,128)S(1)} %shard_map.131.refs_0_), channel_id=1, source_target_pairs={{0,24},{4,28},{8,16},{12,20},{16,8},{20,12},{24,0},{28,4},{1,25},{... | collective-permute-start | bytes 49160 | tf_op jit(solution)/shard_map/ppermute | solution.py:269
  9.8 4.6 %collective-permute-start.2 = (f32[32,128]{1,0:T(8,128)S(1)}, f32[32,128]{1,0:T(8,128)S(1)}, u32[]{:S(2)}, u32[]{:S(2)}) collective-permute-start(f32[32,128]{1,0:T(8,128)S(1)} %shard_map.131.refs_0_), channel_id=1, source_target_pairs={{0,16},{4,20},{8,24},{12,28},{16,0},{20,4},{24,8},{28,12},{1,17},{... | collective-permute-start | bytes 49160 | tf_op jit(solution)/shard_map/ppermute | solution.py:269
  9.8 4.6 %collective-permute-start.3 = (f32[32,128]{1,0:T(8,128)S(1)}, f32[32,128]{1,0:T(8,128)S(1)}, u32[]{:S(2)}, u32[]{:S(2)}) collective-permute-start(f32[32,128]{1,0:T(8,128)S(1)} %shard_map.131.refs_0_), channel_id=1, source_target_pairs={{0,8},{4,12},{8,0},{12,4},{16,24},{20,28},{24,16},{28,20},{1,9},{5... | collective-permute-start | bytes 49160 | tf_op jit(solution)/shard_map/ppermute | solution.py:269
  17.6 5.0 %collective-permute-start.4 = (f32[264,128]{1,0:T(8,128)S(1)}, f32[264,128]{1,0:T(8,128)S(1)}, u32[]{:S(2)}, u32[]{:S(2)}) collective-permute-start(f32[264,128]{1,0:T(8,128)S(1)} %get-tuple-element.18), channel_id=1, source_target_pairs={{0,4},{4,0},{8,12},{12,8},{16,20},{20,16},{24,28},{28,24},{1,5},{5... | collective-permute-start | bytes 405512 | tf_op jit(solution)/shard_map/ppermute | solution.py:269
  22.7 9.9 %copy-start.8 = (f32[3]{0:T(128)S(1)}, f32[3]{0:T(128)}, u32[]{:S(2)}) copy-start(f32[3]{0:T(128)} %var_comp.3) | copy-start | bytes 40
  22.7 9.4 %collective-permute-start.5 = (f32[264,128]{1,0:T(8,128)S(1)}, f32[264,128]{1,0:T(8,128)S(1)}, u32[]{:S(2)}, u32[]{:S(2)}) collective-permute-start(f32[264,128]{1,0:T(8,128)S(1)} %add.12.refs_0_), channel_id=1, source_target_pairs={{0,16},{4,20},{8,24},{12,28},{16,0},{20,4},{24,8},{28,12},{1,17},{... | collective-permute-start | bytes 405512 | tf_op jit(solution)/shard_map/ppermute | solution.py:269
  24.8 7.8 %collective-permute-start.6 = (f32[264,128]{1,0:T(8,128)S(1)}, f32[264,128]{1,0:T(8,128)S(1)}, u32[]{:S(2)}, u32[]{:S(2)}) collective-permute-start(f32[264,128]{1,0:T(8,128)S(1)} %add.12.refs_0_), channel_id=1, source_target_pairs={{0,8},{4,12},{8,0},{12,4},{16,24},{20,28},{24,16},{28,20},{1,9},{5... | collective-permute-start | bytes 405512 | tf_op jit(solution)/shard_map/ppermute | solution.py:269
  24.8 7.8 %collective-permute-start.7 = (f32[264,128]{1,0:T(8,128)S(1)}, f32[264,128]{1,0:T(8,128)S(1)}, u32[]{:S(2)}, u32[]{:S(2)}) collective-permute-start(f32[264,128]{1,0:T(8,128)S(1)} %add.12.refs_0_), channel_id=1, source_target_pairs={{0,24},{4,28},{8,16},{12,20},{16,8},{20,12},{24,0},{28,4},{1,25},{... | collective-permute-start | bytes 405512 | tf_op jit(solution)/shard_map/ppermute | solution.py:269
  29.7 10.5 %copy-start.4 = (f32[8,2048]{1,0:T(8,128)S(1)}, f32[8,2048]{1,0:T(8,128)}, u32[]{:S(2)}) copy-start(f32[8,2048]{1,0:T(8,128)} %solution.1) | copy-start | bytes 196612
  29.8 10.5 %copy-start.7 = (s32[512]{0:T(512)S(1)}, s32[512]{0:T(512)}, u32[]{:S(2)}) copy-start(s32[512]{0:T(512)} %param.13) | copy-start | bytes 6148
  34.5 1.3 %collective-permute-start.8 = (f32[8,2176]{1,0:T(8,128)S(1)}, f32[8,2176]{1,0:T(8,128)S(1)}, u32[]{:S(2)}, u32[]{:S(2)}) collective-permute-start(f32[8,2176]{1,0:T(8,128)S(1)} %get-tuple-element.22), channel_id=1, source_target_pairs={{0,1},{1,0},{2,3},{3,2},{4,5},{5,4},{6,7},{7,6},{8,9},{9,8},{10,11... | collective-permute-start | bytes 208904 | tf_op jit(solution)/shard_map/ppermute | solution.py:269
  35.8 4.4 %collective-permute-start.9 = (f32[8,2176]{1,0:T(8,128)S(1)}, f32[8,2176]{1,0:T(8,128)S(1)}, u32[]{:S(2)}, u32[]{:S(2)}) collective-permute-start(f32[8,2176]{1,0:T(8,128)S(1)} %add.13), channel_id=1, source_target_pairs={{0,2},{1,3},{2,0},{3,1},{4,6},{5,7},{6,4},{7,5},{8,10},{9,11},{10,... | collective-permute-start | bytes 208904 | tf_op jit(solution)/shard_map/ppermute | solution.py:269
  41.2 4.0 %collective-permute-start.10 = (f32[72,128]{1,0:T(8,128)S(1)}, f32[72,128]{1,0:T(8,128)S(1)}, u32[]{:S(2)}, u32[]{:S(2)}) collective-permute-start(f32[72,128]{1,0:T(8,128)S(1)} %get-tuple-element.27), channel_id=1, source_target_pairs={{0,4},{4,0},{8,12},{12,8},{16,20},{20,16},{24,28},{28,24},{1,5},{5... | collective-permute-start | bytes 110600 | tf_op jit(solution)/shard_map/ppermute | solution.py:269
  45.2 5.8 %collective-permute-start.11 = (f32[72,128]{1,0:T(8,128)S(1)}, f32[72,128]{1,0:T(8,128)S(1)}, u32[]{:S(2)}, u32[]{:S(2)}) collective-permute-start(f32[72,128]{1,0:T(8,128)S(1)} %add.15.refs_0_), channel_id=1, source_target_pairs={{0,24},{4,28},{8,16},{12,20},{16,8},{20,12},{24,0},{28,4},{1,25},{... | collective-permute-start | bytes 110600 | tf_op jit(solution)/shard_map/ppermute | solution.py:269
  47.4 5.2 %collective-permute-start.12 = (f32[72,128]{1,0:T(8,128)S(1)}, f32[72,128]{1,0:T(8,128)S(1)}, u32[]{:S(2)}, u32[]{:S(2)}) collective-permute-start(f32[72,128]{1,0:T(8,128)S(1)} %add.15.refs_0_), channel_id=1, source_target_pairs={{0,16},{4,20},{8,24},{12,28},{16,0},{20,4},{24,8},{28,12},{1,17},{... | collective-permute-start | bytes 110600 | tf_op jit(solution)/shard_map/ppermute | solution.py:269
  48.2 4.4 %collective-permute-start.13 = (f32[72,128]{1,0:T(8,128)S(1)}, f32[72,128]{1,0:T(8,128)S(1)}, u32[]{:S(2)}, u32[]{:S(2)}) collective-permute-start(f32[72,128]{1,0:T(8,128)S(1)} %add.15.refs_0_), channel_id=1, source_target_pairs={{0,8},{4,12},{8,0},{12,4},{16,24},{20,28},{24,16},{28,20},{1,9},{5... | collective-permute-start | bytes 110600 | tf_op jit(solution)/shard_map/ppermute | solution.py:269
  (3 other events, 21.5 us)
